TPU v7x, 32 devices: a whole 2x2x4 slice. The times are simulated.
32 devices in a mesh: dp: 8 (over z, x), fsdp: 4 (over y, core).
Axes of the slice: x: 2, y: 2, z: 4, core: 2. Of those that a mesh axis runs over, the one named last changes fastest.
Arguments:
- tokens: bfloat16 [4096, 768], P(('dp', 'fsdp')), may hold values from -6 to 6
- encoded: bfloat16 [131072, 768], P(('dp', 'fsdp')), may hold values from -6 to 6
- segment_ids: int32 [32, 128], P(('dp', 'fsdp')), may hold values from 0 to 3, never falling along the last dimension, each value on 1 to 64 neighbouring positions
- passage_group: int32 [32, 4], P(('dp', 'fsdp')), may hold values from 0 to 3, each once within a row
- cotangent: bfloat16 [4096, 768], P(('dp', 'fsdp')), may hold values from -6 to 6
- self_gain: bfloat16 [768], P(('dp', 'fsdp')), may hold values from 0.5 to 1.5
- cross_gain: bfloat16 [768], P(('dp', 'fsdp')), may hold values from 0.5 to 1.5
- ffn_gain: bfloat16 [768], P(('dp', 'fsdp')), may hold values from 0.5 to 1.5
- self_query: bfloat16 [768, 768], P(('dp', 'fsdp')), may hold values from -0.21875 to 0.21875
- self_key: bfloat16 [768, 768], P(('dp', 'fsdp')), may hold values from -0.21875 to 0.21875
- self_value: bfloat16 [768, 768], P(('dp', 'fsdp')), may hold values from -0.21875 to 0.21875
- self_out: bfloat16 [768, 768], P(('dp', 'fsdp')), may hold values from -0.625 to 0.625
- cross_query: bfloat16 [768, 768], P(('dp', 'fsdp')), may hold values from -0.21875 to 0.21875
- cross_key: bfloat16 [768, 768], P(('dp', 'fsdp')), may hold values from -0.21875 to 0.21875
- cross_value: bfloat16 [768, 768], P(('dp', 'fsdp')), may hold values from -0.21875 to 0.21875
- cross_out: bfloat16 [768, 768], P(('dp', 'fsdp')), may hold values from -6 to 6
- ffn_in: bfloat16 [768, 3072], P(('dp', 'fsdp')), may hold values from -0.21875 to 0.21875
- ffn_out: bfloat16 [3072, 768], P(('dp', 'fsdp')), may hold values from -0.21875 to 0.21875
Outputs:
- block_out: bfloat16 [4096, 768], P(('dp', 'fsdp'))
- tokens_grad: float32 [4096, 768], P(('dp', 'fsdp'))
- encoded_grad: float32 [131072, 768], P(('dp', 'fsdp'))
- self_gain_grad: float32 [768], P(('dp', 'fsdp'))
- cross_gain_grad: float32 [768], P(('dp', 'fsdp'))
- ffn_gain_grad: float32 [768], P(('dp', 'fsdp'))
- self_query_grad: float32 [768, 768], P(('dp', 'fsdp'))
- self_key_grad: float32 [768, 768], P(('dp', 'fsdp'))
- self_value_grad: float32 [768, 768], P(('dp', 'fsdp'))
- self_out_grad: float32 [768, 768], P(('dp', 'fsdp'))
- cross_query_grad: float32 [768, 768], P(('dp', 'fsdp'))
- cross_key_grad: float32 [768, 768], P(('dp', 'fsdp'))
- cross_value_grad: float32 [768, 768], P(('dp', 'fsdp'))
- cross_out_grad: float32 [768, 768], P(('dp', 'fsdp'))
- ffn_in_grad: float32 [768, 3072], P(('dp', 'fsdp'))
- ffn_out_grad: float32 [3072, 768], P(('dp', 'fsdp'))
Inputs may be any that keep to these rules, and one draw needn't show every extreme that they name: `segment_ids`: within a packed row the query numbers never fall; every one of the 4 queries has 1 to 64 tokens. `passage_group`: each packed row's entries are a permutation of 0 to 3: every query reads a passage block of its own.
All inputs are finite; a program needn't handle non-finite values.
Results may differ from a plain program's by a relative error of at most 0.02.
Values may be sent and summed in bfloat16 or wider, within the bound.
No kernel may reach another device: no remote copies, remote signals or barrier semaphores. Data moves between devices by JAX's collectives and lax.ppermute only.
A program may use at most 192 MiB of HBM per device.

v0:
```python
import jax
import jax.numpy as jnp
from jax import lax
from jax.sharding import PartitionSpec as P

HEAD = 64
SEGS = 4
PASSAGES = 4
PASS_LEN = 256


score_scale = 0.125
epsilon = 1e-06
masked_score = -1e30


def rms_norm(values, gain_row):
    return (
        values * lax.rsqrt(jnp.mean(values * values, axis=-1, keepdims=True) + epsilon) * gain_row
    )


def product(left_side, right_side):
    return jnp.dot(left_side, right_side, preferred_element_type=jnp.float32)


def product_left(left_side, right_side):
    return jnp.einsum("ti,td->id", left_side, right_side, preferred_element_type=jnp.float32)


def product_right(left_side, right_side):
    return jnp.einsum("td,id->ti", left_side, right_side, preferred_element_type=jnp.float32)


def split_heads(matrix):
    return matrix.reshape(matrix.shape[0], -1, HEAD)


def block_scores(query_block, key_heads, allowed):
    scores = (
        jnp.einsum("qhd,khd->hqk", query_block, key_heads, preferred_element_type=jnp.float32)
        * score_scale
    )
    return jnp.where(allowed[None], scores, masked_score)


def attend_forward(queries, key_rows, value_rows, allow_rule):
    row_count = queries.shape[0]
    block_rows = min(512, row_count)
    query_heads = split_heads(queries)
    key_heads = split_heads(key_rows)
    value_heads = split_heads(value_rows)
    scores = block_scores(query_heads, key_heads, allow_rule(0, block_rows))
    largest = jnp.max(scores, axis=-1, keepdims=True)
    weights = jnp.exp(scores - largest)
    totals = jnp.sum(weights, axis=-1, keepdims=True)
    probabilities = (weights / totals).astype(jnp.bfloat16)
    context = jnp.einsum(
        "hqk,khd->qhd", probabilities, value_heads, preferred_element_type=jnp.float32
    )
    contexts = context.reshape(block_rows, -1).astype(jnp.bfloat16)
    log_totals = [largest + jnp.log(totals)]
    return (contexts, log_totals)


def attend_backward(queries, key_rows, value_rows, log_totals, grad_context, allow_rule):
    row_count = queries.shape[0]
    block_rows = min(512, row_count)
    query_heads = split_heads(queries)
    key_heads = split_heads(key_rows)
    value_heads = split_heads(value_rows)
    key_grad = jnp.zeros(key_heads.shape, jnp.float32)
    value_grad = jnp.zeros(value_heads.shape, jnp.float32)
    query_grads = []
    for block_number, begin_row in enumerate(range(0, row_count, block_rows)):
        scores = block_scores(query_heads, key_heads, allow_rule(begin_row, block_rows))
        probabilities = jnp.exp(scores - log_totals[block_number])
        grad_block = split_heads(grad_context)
        value_grad = jnp.einsum(
            "hqk,qhd->khd",
            probabilities.astype(jnp.bfloat16),
            grad_block,
            preferred_element_type=jnp.float32,
        )
        prob_grad = jnp.einsum(
            "qhd,khd->hqk", grad_block, value_heads, preferred_element_type=jnp.float32
        )
        inner_sum = jnp.sum(probabilities * prob_grad, axis=-1, keepdims=True)
        score_grad = (probabilities * (prob_grad - inner_sum)).astype(jnp.bfloat16)
        query_grad = jnp.einsum(
            "hqk,khd->qhd", score_grad, key_heads, preferred_element_type=jnp.float32
        )
        query_grads.append(query_grad.reshape(block_rows, -1) * score_scale)
        key_grad = (
            jnp.einsum("hqk,qhd->khd", score_grad, query_heads, preferred_element_type=jnp.float32)
            * score_scale
        )
    return (
        query_grads[0].astype(jnp.bfloat16),
        key_grad.reshape(key_rows.shape[0], -1).astype(jnp.bfloat16),
        value_grad.reshape(value_rows.shape[0], -1).astype(jnp.bfloat16),
    )


def norm_backward(values, gain_row, grad_normed):
    unused_value, pull_back = jax.vjp(rms_norm, values, gain_row)
    grad_values, grad_gain = pull_back(grad_normed)
    return (grad_values, grad_gain)


def per_device(
    tokens,
    encoded,
    segment_ids,
    passage_group,
    cotangent,
    self_gain,
    cross_gain,
    ffn_gain,
    self_query,
    self_key,
    self_value,
    self_out,
    cross_query,
    cross_key,
    cross_value,
    cross_out,
    ffn_in,
    ffn_out,
):
    shards = (
        self_gain,
        cross_gain,
        ffn_gain,
        self_query,
        self_key,
        self_value,
        self_out,
        cross_query,
        cross_key,
        cross_value,
        cross_out,
        ffn_in,
        ffn_out,
    )
    gathered = (
        lax.all_gather(self_gain, ("dp", "fsdp"), axis=0, tiled=True),
        lax.all_gather(cross_gain, ("dp", "fsdp"), axis=0, tiled=True),
        lax.all_gather(ffn_gain, ("dp", "fsdp"), axis=0, tiled=True),
        lax.all_gather(self_query, ("dp", "fsdp"), axis=0, tiled=True),
        lax.all_gather(self_key, ("dp", "fsdp"), axis=0, tiled=True),
        lax.all_gather(self_value, ("dp", "fsdp"), axis=0, tiled=True),
        lax.all_gather(self_out, ("dp", "fsdp"), axis=0, tiled=True),
        lax.all_gather(cross_query, ("dp", "fsdp"), axis=0, tiled=True),
        lax.all_gather(cross_key, ("dp", "fsdp"), axis=0, tiled=True),
        lax.all_gather(cross_value, ("dp", "fsdp"), axis=0, tiled=True),
        lax.all_gather(cross_out, ("dp", "fsdp"), axis=0, tiled=True),
        lax.all_gather(ffn_in, ("dp", "fsdp"), axis=0, tiled=True),
        lax.all_gather(ffn_out, ("dp", "fsdp"), axis=0, tiled=True),
    )
    segments = segment_ids[0]
    groups_row = passage_group[0]
    row_count = tokens.shape[0]
    encoder_count = encoded.shape[0]
    positions = lax.iota(jnp.int32, row_count)
    token_group = jnp.sum(
        jnp.where(segments[:, None] == lax.iota(jnp.int32, SEGS)[None, :], groups_row[None, :], 0),
        axis=1,
    )
    key_group = lax.iota(jnp.int32, encoder_count) // (PASSAGES * PASS_LEN)

    def self_rule(begin_row, block_rows):
        return (segments[:, None] == segments[None, :]) & (positions[None, :] <= positions[:, None])

    def cross_rule(begin_row, block_rows):
        return token_group[begin_row : begin_row + block_rows, None] == key_group[None, :]

    (
        gain_self,
        gain_cross,
        gain_ffn,
        weight_query,
        weight_key,
        weight_value,
        weight_out,
        weight_cq,
        weight_ck,
        weight_cv,
        weight_co,
        weight_in,
        weight_down,
    ) = gathered
    hidden_in = tokens.astype(jnp.float32)
    normed_one = rms_norm(hidden_in, gain_self.astype(jnp.float32)).astype(jnp.bfloat16)
    queries_one = product(normed_one, weight_query).astype(jnp.bfloat16)
    keys_one = product(normed_one, weight_key).astype(jnp.bfloat16)
    values_one = product(normed_one, weight_value).astype(jnp.bfloat16)
    context_one, log_one = attend_forward(queries_one, keys_one, values_one, self_rule)
    after_self = hidden_in + product(context_one, weight_out)
    normed_two = rms_norm(after_self, gain_cross.astype(jnp.float32)).astype(jnp.bfloat16)
    queries_two = product(normed_two, weight_cq).astype(jnp.bfloat16)
    keys_two = product(encoded, weight_ck).astype(jnp.bfloat16)
    values_two = product(encoded, weight_cv).astype(jnp.bfloat16)
    context_two, log_two = attend_forward(queries_two, keys_two, values_two, cross_rule)
    after_cross = after_self + product(context_two, weight_co)
    normed_three = rms_norm(after_cross, gain_ffn.astype(jnp.float32)).astype(jnp.bfloat16)
    pre_act = product(normed_three, weight_in)
    activated = jax.nn.gelu(pre_act).astype(jnp.bfloat16)
    block_out = (after_cross + product(activated, weight_down)).astype(jnp.bfloat16)
    again = (
        lax.all_gather(shards[0], ("dp", "fsdp"), axis=0, tiled=True),
        lax.all_gather(shards[1], ("dp", "fsdp"), axis=0, tiled=True),
        lax.all_gather(shards[2], ("dp", "fsdp"), axis=0, tiled=True),
        lax.all_gather(shards[3], ("dp", "fsdp"), axis=0, tiled=True),
        lax.all_gather(shards[4], ("dp", "fsdp"), axis=0, tiled=True),
        lax.all_gather(shards[5], ("dp", "fsdp"), axis=0, tiled=True),
        lax.all_gather(shards[6], ("dp", "fsdp"), axis=0, tiled=True),
        lax.all_gather(shards[7], ("dp", "fsdp"), axis=0, tiled=True),
        lax.all_gather(shards[8], ("dp", "fsdp"), axis=0, tiled=True),
        lax.all_gather(shards[9], ("dp", "fsdp"), axis=0, tiled=True),
        lax.all_gather(shards[10], ("dp", "fsdp"), axis=0, tiled=True),
        lax.all_gather(shards[11], ("dp", "fsdp"), axis=0, tiled=True),
        lax.all_gather(shards[12], ("dp", "fsdp"), axis=0, tiled=True),
    )
    (
        gain_self,
        gain_cross,
        gain_ffn,
        weight_query,
        weight_key,
        weight_value,
        weight_out,
        weight_cq,
        weight_ck,
        weight_cv,
        weight_co,
        weight_in,
        weight_down,
    ) = again
    grad_down = product_left(activated, cotangent)
    summed_down = lax.psum_scatter(grad_down, ("dp", "fsdp"), scatter_dimension=0, tiled=True)
    grad_act = product_right(cotangent, weight_down).astype(jnp.bfloat16)
    unused_act, gelu_back = jax.vjp(jax.nn.gelu, pre_act)
    grad_pre = gelu_back(grad_act.astype(jnp.float32))[0].astype(jnp.bfloat16)
    grad_in = product_left(normed_three, grad_pre)
    grad_normed_three = product_right(grad_pre, weight_in)
    grad_residual, grad_gain_three = norm_backward(
        after_cross, gain_ffn.astype(jnp.float32), grad_normed_three
    )
    grad_after_cross = cotangent.astype(jnp.float32) + grad_residual
    summed_up = (
        lax.psum_scatter(grad_gain_three, ("dp", "fsdp"), scatter_dimension=0, tiled=True),
        lax.psum_scatter(grad_in, ("dp", "fsdp"), scatter_dimension=0, tiled=True),
    )
    branch_two = grad_after_cross.astype(jnp.bfloat16)
    grad_cross_out = product_left(context_two, branch_two)
    grad_context_two = product_right(branch_two, weight_co).astype(jnp.bfloat16)
    grad_queries_two, grad_keys_two, grad_values_two = attend_backward(
        queries_two, keys_two, values_two, log_two, grad_context_two, cross_rule
    )
    grad_cross_query = product_left(normed_two, grad_queries_two)
    grad_cross_key = product_left(encoded, grad_keys_two)
    grad_cross_value = product_left(encoded, grad_values_two)
    grad_normed_two = product_right(grad_queries_two, weight_cq)
    encoded_grad = product_right(grad_keys_two, weight_ck) + product_right(
        grad_values_two, weight_cv
    )
    grad_residual, grad_gain_two = norm_backward(
        after_self, gain_cross.astype(jnp.float32), grad_normed_two
    )
    grad_after_self = grad_after_cross + grad_residual
    summed_cross = (
        lax.psum_scatter(grad_gain_two, ("dp", "fsdp"), scatter_dimension=0, tiled=True),
        lax.psum_scatter(grad_cross_query, ("dp", "fsdp"), scatter_dimension=0, tiled=True),
        lax.psum_scatter(grad_cross_key, ("dp", "fsdp"), scatter_dimension=0, tiled=True),
        lax.psum_scatter(grad_cross_value, ("dp", "fsdp"), scatter_dimension=0, tiled=True),
        lax.psum_scatter(grad_cross_out, ("dp", "fsdp"), scatter_dimension=0, tiled=True),
    )
    branch_one = grad_after_self.astype(jnp.bfloat16)
    grad_self_out = product_left(context_one, branch_one)
    grad_context_one = product_right(branch_one, weight_out).astype(jnp.bfloat16)
    grad_queries_one, grad_keys_one, grad_values_one = attend_backward(
        queries_one, keys_one, values_one, log_one, grad_context_one, self_rule
    )
    grad_self_query = product_left(normed_one, grad_queries_one)
    grad_self_key = product_left(normed_one, grad_keys_one)
    grad_self_value = product_left(normed_one, grad_values_one)
    grad_normed_one = (
        product_right(grad_queries_one, weight_query)
        + product_right(grad_keys_one, weight_key)
        + product_right(grad_values_one, weight_value)
    )
    grad_residual, grad_gain_one = norm_backward(
        hidden_in, gain_self.astype(jnp.float32), grad_normed_one
    )
    tokens_grad = grad_after_self + grad_residual
    summed_self = (
        lax.psum_scatter(grad_gain_one, ("dp", "fsdp"), scatter_dimension=0, tiled=True),
        lax.psum_scatter(grad_self_query, ("dp", "fsdp"), scatter_dimension=0, tiled=True),
        lax.psum_scatter(grad_self_key, ("dp", "fsdp"), scatter_dimension=0, tiled=True),
        lax.psum_scatter(grad_self_value, ("dp", "fsdp"), scatter_dimension=0, tiled=True),
        lax.psum_scatter(grad_self_out, ("dp", "fsdp"), scatter_dimension=0, tiled=True),
    )
    summed = (
        summed_self[0],
        summed_cross[0],
        summed_up[0],
        summed_self[1],
        summed_self[2],
        summed_self[3],
        summed_self[4],
        summed_cross[1],
        summed_cross[2],
        summed_cross[3],
        summed_cross[4],
        summed_up[1],
        summed_down,
    )
    return (
        block_out,
        tokens_grad,
        encoded_grad,
        summed[0],
        summed[1],
        summed[2],
        summed[3],
        summed[4],
        summed[5],
        summed[6],
        summed[7],
        summed[8],
        summed[9],
        summed[10],
        summed[11],
        summed[12],
    )


def solution(mesh):
    return jax.shard_map(
        per_device,
        mesh=mesh,
        in_specs=(
            P(("dp", "fsdp"), None),
            P(("dp", "fsdp"), None),
            P(("dp", "fsdp"), None),
            P(("dp", "fsdp"), None),
            P(("dp", "fsdp"), None),
            P(("dp", "fsdp")),
            P(("dp", "fsdp")),
            P(("dp", "fsdp")),
            P(("dp", "fsdp"), None),
            P(("dp", "fsdp"), None),
            P(("dp", "fsdp"), None),
            P(("dp", "fsdp"), None),
            P(("dp", "fsdp"), None),
            P(("dp", "fsdp"), None),
            P(("dp", "fsdp"), None),
            P(("dp", "fsdp"), None),
            P(("dp", "fsdp"), None),
            P(("dp", "fsdp"), None),
        ),
        out_specs=(
            P(("dp", "fsdp"), None),
            P(("dp", "fsdp"), None),
            P(("dp", "fsdp"), None),
            P(("dp", "fsdp")),
            P(("dp", "fsdp")),
            P(("dp", "fsdp")),
            P(("dp", "fsdp"), None),
            P(("dp", "fsdp"), None),
            P(("dp", "fsdp"), None),
            P(("dp", "fsdp"), None),
            P(("dp", "fsdp"), None),
            P(("dp", "fsdp"), None),
            P(("dp", "fsdp"), None),
            P(("dp", "fsdp"), None),
            P(("dp", "fsdp"), None),
            P(("dp", "fsdp"), None),
        ),
        check_vma=False,
    )
```

profile of v0, /device:TPU:0, one launch (start us, length us, event | category | flops | bytes accessed | tf_op | source)
XLA Modules:
  0.0 1774.4 jit_solution(13704277484429112686)
XLA Ops:
  16.6 42.1 %all-reduce.7 = (bf16[768]{0:T(1024)(128)(2,1)S(1)}, bf16[768]{0:T(1024)(128)(2,1)S(1)}, bf16[768]{0:T(1024)(128)(2,1)S(1)}) all-reduce(bf16[768]{0:T(1024)(128)(2,1)S(1)} %dynamic-update-slice, bf16[768]{0:T(1024)(128)(2,1)S(1)} %dynamic-update-slice.1, ...), channel_id=1, replica_groups=mesh['dp'=8,'fsdp'=4] {'dp','fsdp'}, use_global_device_ids=true, to_apply=%add | all-reduce | flops 2304 | bytes 9216
  69.8 54.0 %all-gather.13.cloned.1.call-done = bf16[768,768]{1,0:T(8,128)(2,1)} async-done(((bf16[24,768]{1,0:T(8,128)(2,1)}), bf16[768,768]{1,0:T(8,128)(2,1)}) %all-gather.13.cloned.1.call-update) | async-done | bytes 1179664 | tf_op jit(solution)/shard_map/all_gather | solution.py:150
  125.6 54.2 %all-gather.15.cloned.1.call-done = bf16[768,768]{1,0:T(8,128)(2,1)} async-done(((bf16[24,768]{1,0:T(8,128)(2,1)}), bf16[768,768]{1,0:T(8,128)(2,1)}) %all-gather.15.cloned.1.call-update) | async-done | bytes 1179664 | tf_op jit(solution)/shard_map/all_gather | solution.py:151
  182.4 53.2 %all-gather.17.cloned.1.call-done = bf16[768,768]{1,0:T(8,128)(2,1)} async-done(((bf16[24,768]{1,0:T(8,128)(2,1)}), bf16[768,768]{1,0:T(8,128)(2,1)}) %all-gather.17.cloned.1.call-update) | async-done | bytes 1179664 | tf_op jit(solution)/shard_map/all_gather | solution.py:153
  237.3 54.1 %all-gather.23.cloned.1.call-done = bf16[768,768]{1,0:T(8,128)(2,1)} async-done(((bf16[24,768]{1,0:T(8,128)(2,1)}), bf16[768,768]{1,0:T(8,128)(2,1)}) %all-gather.23.cloned.1.call-update) | async-done | bytes 1179664 | tf_op jit(solution)/shard_map/all_gather | solution.py:155
  291.4 9.2 convolution_convert_fusion
  300.6 46.7 %all-gather.21.cloned.1.call-done = bf16[768,768]{1,0:T(8,128)(2,1)} async-done(((bf16[24,768]{1,0:T(8,128)(2,1)}), bf16[768,768]{1,0:T(8,128)(2,1)}) %all-gather.21.cloned.1.call-update) | async-done | bytes 1179664 | tf_op jit(solution)/shard_map/all_gather | solution.py:154
  349.0 12.5 fusion.63
  361.6 10.5 fusion
  372.0 31.2 %all-gather.19.cloned.1.call-done = bf16[768,768]{1,0:T(8,128)(2,1)} async-done(((bf16[24,768]{1,0:T(8,128)(2,1)}), bf16[768,768]{1,0:T(8,128)(2,1)}) %all-gather.19.cloned.1.call-update) | async-done | bytes 1179664 | tf_op jit(solution)/shard_map/all_gather | solution.py:156
  413.5 11.1 fusion.22
  424.5 34.6 %all-gather.25.cloned.1.call-done = bf16[768,768]{1,0:T(8,128)(2,1)} async-done(((bf16[24,768]{1,0:T(8,128)(2,1)}), bf16[768,768]{1,0:T(8,128)(2,1)}) %all-gather.25.cloned.1.call-update) | async-done | bytes 1179664 | tf_op jit(solution)/shard_map/all_gather | solution.py:157
  460.9 63.7 %all-gather.27.cloned.1.call-done = bf16[768,3072]{1,0:T(8,128)(2,1)} async-done(((bf16[24,3072]{1,0:T(8,128)(2,1)}), bf16[768,3072]{1,0:T(8,128)(2,1)}) %all-gather.27.cloned.1.call-update) | async-done | bytes 4718608 | tf_op jit(solution)/shard_map/all_gather | solution.py:158
  529.0 60.8 %all-gather.29.cloned.1.call-done = bf16[3072,768]{1,0:T(8,128)(2,1)} async-done(((bf16[96,768]{1,0:T(8,128)(2,1)}), bf16[3072,768]{1,0:T(8,128)(2,1)}) %all-gather.29.cloned.1.call-update) | async-done | bytes 4718608 | tf_op jit(solution)/shard_map/all_gather | solution.py:159
  597.4 19.1 %multiply_reduce_fusion = (f32[12,128]{1,0:T(8,128)S(1)}, f32[12,128,4096]{2,1,0:T(8,128)}) fusion(f32[12,128,4096]{2,1,0:T(8,128)} %get-tuple-element.97, f32[12,128]{1,0:T(8,128)S(1)} %log_add_fusion.1, bf16[128,12,64]{0,2,1:T(8,128)(2,1)S(1)} %bitcast.118, bf16[4096,12,64]{0,2,1:T(8,128)(2,1)} %bitcast.111), kind=kOutput, calls=%fused_computation.1 | convolution fusion | flops 824179200 | bytes 56832000 | tf_op jit(solution)/shard_map/qhd,khd->hqk/dot_general | solution.py:85
  616.5 21.2 %multiply_convert_fusion = bf16[12,128,4096]{2,1,0:T(8,128)(2,1)} fusion(f32[12,128,4096]{2,1,0:T(8,128)} %get-tuple-element.102, f32[12,128,4096]{2,1,0:T(8,128)} %get-tuple-element.97, f32[12,128]{1,0:T(8,128)S(1)} %get-tuple-element.101, f32[12,128]{1,0:T(8,128)S(1)} %log_add_fusion.1), kind=kLoop, calls=%fused_computation | loop fusion | flops 25165824 | bytes 62926848 | tf_op jit(solution)/shard_map/convert_element_type | solution.py:89
  637.8 10.8 fusion.19
  676.1 9.4 convolution_bitcast_fusion.1
  688.6 13.0 fusion.6
  701.6 10.3 convolution_bitcast_fusion
  736.1 40.0 %all-reduce.6 = (f32[768]{0:T(1024)S(1)}, f32[768]{0:T(1024)S(1)}, f32[768]{0:T(1024)S(1)}) all-reduce(f32[768]{0:T(1024)S(1)} %get-tuple-element.84, f32[768]{0:T(1024)S(1)} %get-tuple-element.82, f32[768]{0:T(1024)S(1)} %get-tuple-element.80), channel_id=2, replica_groups=mesh['dp'=8,'fsdp'=4] {'dp','fsdp'}, use_global_device_ids=true, to_apply=%region_14.15.clone | all-reduce | flops 2304 | bytes 18432
  784.6 8.2 fusion.65
  792.9 11.3 convolution_add_fusion
  804.1 54.6 %reduce-scatter.17.cloned.1.call-done = f32[24,768]{1,0:T(8,128)} async-done(((f32[768,768]{1,0:T(8,128)}), f32[24,768]{1,0:T(8,128)}) %reduce-scatter.17.cloned.1.call-update) | async-done | bytes 73744 | tf_op jit(solution)/shard_map/reduce_scatter | solution.py:300
  858.7 103.9 %reduce-scatter.19.cloned.1.call-done = f32[24,768]{1,0:T(8,128)} async-done(((f32[768,768]{1,0:T(8,128)}), f32[24,768]{1,0:T(8,128)}) %reduce-scatter.19.cloned.1.call-update) | async-done | bytes 73744 | tf_op jit(solution)/shard_map/reduce_scatter | solution.py:301
  962.6 104.7 %reduce-scatter.21.cloned.1.call-done = f32[24,768]{1,0:T(8,128)} async-done(((f32[768,768]{1,0:T(8,128)}), f32[24,768]{1,0:T(8,128)}) %reduce-scatter.21.cloned.1.call-update) | async-done | bytes 73744 | tf_op jit(solution)/shard_map/reduce_scatter | solution.py:302
  1067.3 103.8 %reduce-scatter.23.cloned.1.call-done = f32[24,768]{1,0:T(8,128)} async-done(((f32[768,768]{1,0:T(8,128)}), f32[24,768]{1,0:T(8,128)}) %reduce-scatter.23.cloned.1.call-update) | async-done | bytes 73744 | tf_op jit(solution)/shard_map/reduce_scatter | solution.py:274
  1171.1 104.6 %reduce-scatter.31.cloned.1.call-done = f32[24,768]{1,0:T(8,128)} async-done(((f32[768,768]{1,0:T(8,128)}), f32[24,768]{1,0:T(8,128)}) %reduce-scatter.31.cloned.1.call-update) | async-done | bytes 73744
  1275.7 103.8 %reduce-scatter.33.cloned.1.call-done = f32[24,768]{1,0:T(8,128)} async-done(((f32[768,768]{1,0:T(8,128)}), f32[24,768]{1,0:T(8,128)}) %reduce-scatter.33.cloned.1.call-update) | async-done | bytes 73744
  1379.4 104.7 %reduce-scatter.25.cloned.1.call-done = f32[24,768]{1,0:T(8,128)} async-done(((f32[768,768]{1,0:T(8,128)}), f32[24,768]{1,0:T(8,128)}) %reduce-scatter.25.cloned.1.call-update) | async-done | bytes 73744 | tf_op jit(solution)/shard_map/reduce_scatter | solution.py:277
  1484.1 141.1 %reduce-scatter.27.cloned.1.call-done = f32[24,3072]{1,0:T(8,128)} async-done(((f32[768,3072]{1,0:T(8,128)}), f32[24,3072]{1,0:T(8,128)}) %reduce-scatter.27.cloned.1.call-update) | async-done | bytes 294928 | tf_op jit(solution)/shard_map/reduce_scatter | solution.py:253
  1625.2 142.0 %reduce-scatter.29.cloned.1.call-done = f32[96,768]{1,0:T(8,128)} async-done(((f32[3072,768]{1,0:T(8,128)}), f32[96,768]{1,0:T(8,128)}) %reduce-scatter.29.cloned.1.call-update) | async-done | bytes 294928 | tf_op jit(solution)/shard_map/reduce_scatter | solution.py:241
  (190 shorter events, 114.8 us)
Async XLA Ops:
  7.2 116.6 %copy-start = (bf16[128,768]{1,0:T(8,128)(2,1)S(1)}, bf16[128,768]{1,0:T(8,128)(2,1)}, u32[]{:S(2)}) copy-start(bf16[128,768]{1,0:T(8,128)(2,1)} %param.18) | copy-start | bytes 589828
  7.2 60.7 %all-gather.11.cloned.1.call-start = ((), (), s32[]{:S(2)}) async-start(), calls=%async_computation.10 | async-start | bytes 1216512 | tf_op jit(solution)/shard_map/all_gather | solution.py:152
  7.9 115.9 %all-gather.13.cloned.1.call-start = ((), (), s32[]{:S(2)}) async-start(), calls=%async_computation.11 | async-start | bytes 1216512 | tf_op jit(solution)/shard_map/all_gather | solution.py:150
  8.7 171.1 %all-gather.15.cloned.1.call-start = ((), (), s32[]{:S(2)}) async-start(), calls=%async_computation.12 | async-start | bytes 1216512 | tf_op jit(solution)/shard_map/all_gather | solution.py:151
  9.4 226.2 %all-gather.17.cloned.1.call-start = ((), (), s32[]{:S(2)}) async-start(), calls=%async_computation.13 | async-start | bytes 1216512 | tf_op jit(solution)/shard_map/all_gather | solution.py:153
  10.0 281.4 %all-gather.23.cloned.1.call-start = ((), (), s32[]{:S(2)}) async-start(), calls=%async_computation.16 | async-start | bytes 1216512 | tf_op jit(solution)/shard_map/all_gather | solution.py:155
  10.6 336.7 %all-gather.21.cloned.1.call-start = ((), (), s32[]{:S(2)}) async-start(), calls=%async_computation.15 | async-start | bytes 1216512 | tf_op jit(solution)/shard_map/all_gather | solution.py:154
  11.1 392.1 %all-gather.19.cloned.1.call-start = ((), (), s32[]{:S(2)}) async-start(), calls=%async_computation.14 | async-start | bytes 1216512 | tf_op jit(solution)/shard_map/all_gather | solution.py:156
  11.9 447.3 %all-gather.25.cloned.1.call-start = ((), (), s32[]{:S(2)}) async-start(), calls=%async_computation.17 | async-start | bytes 1216512 | tf_op jit(solution)/shard_map/all_gather | solution.py:157
  12.6 512.0 %all-gather.27.cloned.1.call-start = ((), (), s32[]{:S(2)}) async-start(), calls=%async_computation.18 | async-start | bytes 4866048 | tf_op jit(solution)/shard_map/all_gather | solution.py:158
  13.4 576.4 %all-gather.29.cloned.1.call-start = ((), (), s32[]{:S(2)}) async-start(), calls=%async_computation.19 | async-start | bytes 4866048 | tf_op jit(solution)/shard_map/all_gather | solution.py:159
  14.0 790.1 %reduce-scatter.15.cloned.1.call-start = ((), (), s32[]{:S(2)}) async-start(), calls=%async_computation.20 | async-start | bytes 2433024 | tf_op jit(solution)/shard_map/reduce_scatter | solution.py:299
  69.8 112.3 %copy-start.29 = (bf16[128,768]{0,1:T(8,128)(2,1)}, bf16[128,768]{0,1:T(8,128)(2,1)S(1)}, u32[]{:S(2)}) copy-start(bf16[128,768]{0,1:T(8,128)(2,1)S(1)} %copy.76) | copy-start | bytes 589828
  125.6 56.7 %copy-start.18 = (bf16[128,768]{0,1:T(8,128)(2,1)}, bf16[128,768]{0,1:T(8,128)(2,1)S(1)}, u32[]{:S(2)}) copy-start(bf16[128,768]{0,1:T(8,128)(2,1)S(1)} %copy.77) | copy-start | bytes 589828
  182.3 118.2 %copy-start.27 = (bf16[12,64,128]{2,1,0:T(8,128)(2,1)}, bf16[12,64,128]{2,1,0:T(8,128)(2,1)S(1)}, u32[]{:S(2)}) copy-start(bf16[12,64,128]{2,1,0:T(8,128)(2,1)S(1)} %convolution_convert_fusion.7) | copy-start | bytes 589828
  424.5 104.5 %copy-start.25 = (bf16[12,64,128]{2,1,0:T(8,128)(2,1)}, bf16[12,64,128]{2,1,0:T(8,128)(2,1)S(1)}, u32[]{:S(2)}) copy-start(bf16[12,64,128]{2,1,0:T(8,128)(2,1)S(1)} %fusion.22) | copy-start | bytes 589828
  524.6 65.2 %copy-start.23 = (bf16[128,768]{1,0:T(8,128)(2,1)S(1)}, bf16[128,768]{1,0:T(8,128)(2,1)}, u32[]{:S(2)}) copy-start(bf16[128,768]{1,0:T(8,128)(2,1)} %param.22) | copy-start | bytes 589828
  656.0 202.7 %reduce-scatter.17.cloned.1.call-start = ((), (), s32[]{:S(2)}) async-start(), calls=%async_computation.21 | async-start | bytes 2433024 | tf_op jit(solution)/shard_map/reduce_scatter | solution.py:300
  660.0 302.6 %reduce-scatter.19.cloned.1.call-start = ((), (), s32[]{:S(2)}) async-start(), calls=%async_computation.22 | async-start | bytes 2433024 | tf_op jit(solution)/shard_map/reduce_scatter | solution.py:301
  662.6 404.7 %reduce-scatter.21.cloned.1.call-start = ((), (), s32[]{:S(2)}) async-start(), calls=%async_computation.23 | async-start | bytes 2433024 | tf_op jit(solution)/shard_map/reduce_scatter | solution.py:302
  664.5 506.6 %reduce-scatter.23.cloned.1.call-start = ((), (), s32[]{:S(2)}) async-start(), calls=%async_computation.24 | async-start | bytes 2433024 | tf_op jit(solution)/shard_map/reduce_scatter | solution.py:274
  666.6 609.1 %reduce-scatter.31.cloned.1.call-start = ((), (), s32[]{:S(2)}) async-start(), calls=%async_computation.28 | async-start | bytes 2433024
  688.6 690.9 %reduce-scatter.33.cloned.1.call-start = ((), (), s32[]{:S(2)}) async-start(), calls=%async_computation.29 | async-start | bytes 2433024
  715.1 769.0 %reduce-scatter.25.cloned.1.call-start = ((), (), s32[]{:S(2)}) async-start(), calls=%async_computation.25 | async-start | bytes 2433024 | tf_op jit(solution)/shard_map/reduce_scatter | solution.py:277
  717.9 907.3 %reduce-scatter.27.cloned.1.call-start = ((), (), s32[]{:S(2)}) async-start(), calls=%async_computation.26 | async-start | bytes 9732096 | tf_op jit(solution)/shard_map/reduce_scatter | solution.py:253
  723.1 1044.0 %reduce-scatter.29.cloned.1.call-start = ((), (), s32[]{:S(2)}) async-start(), calls=%async_computation.27 | async-start | bytes 9732096 | tf_op jit(solution)/shard_map/reduce_scatter | solution.py:241
  731.5 46.3 %copy-start.31 = (f32[128]{0:T(128)S(1)}, f32[128]{0:T(128)}, u32[]{:S(2)}) copy-start(f32[128]{0:T(128)} %copy-done.30) | copy-start | bytes 1540
  733.3 51.3 %slice-start = ((s8[6291456]{0:T(1024)(128)(4,1)}), s8[2097152]{0:T(1024)(128)(4,1)S(1)}, s32[]{:S(2)}) async-start(s8[6291456]{0:T(1024)(128)(4,1)} %bitcast.107), calls=%async_computation.30 | async-start | bytes 4194304
  777.8 6.8 copy-start.32
  779.8 13.0 slice-start.2
  784.6 8.2 slice-start.3
  784.6 8.2 copy-start.33
  (26 other events, 51.8 us)
Sparse Core Ops, SparseCore 0:
  10.9 56.8 all-gather.10
  70.8 52.9 all-gather.12
  126.7 53.0 all-gather.14
  182.5 53.0 all-gather.16
  238.3 53.0 all-gather.22
  294.2 53.0 all-gather.20
  350.1 53.0 all-gather.18
  406.1 53.0 all-gather.24
  462.1 62.5 all-gather.26
  527.4 62.3 all-gather.28
  656.1 97.8 reduce-scatter.14
  760.6 97.9 reduce-scatter.16
  864.5 98.0 reduce-scatter.18
  969.2 98.0 reduce-scatter.20
  1073.0 98.0 reduce-scatter.22
  1177.6 98.0 reduce-scatter.30
  1281.4 97.9 reduce-scatter.32
  1386.0 98.0 reduce-scatter.24
  1490.6 134.5 reduce-scatter.26
  1632.5 134.5 reduce-scatter.28
where the time goes:
time: 1780 us; the launch traced here: 1770 us
  waiting for transfers between devices  1430 us (80%)
  matrix products  189 us (11%)
  blocking collectives  82.1 us (5%)
  other arithmetic  37.3 us (2%)
  local copies, waits for them, and re-layouts  21.4 us (1%)
    unnamed x22, waiting for transfers between devices  215 us
    reduce_scatter x1, waiting for transfers between devices, per_device(): lax.psum_scatter(grad_down, ('dp', 'fsdp'), scatter_dimension=0, tiled=True)  142 us
    reduce_scatter x1, waiting for transfers between devices, per_device(): lax.psum_scatter(grad_in, ('dp', 'fsdp'), scatter_dimension=0, tiled=True)  141 us
    reduce_scatter x1, waiting for transfers between devices, per_device(): lax.psum_scatter(grad_self_out, ('dp', 'fsdp'), scatter_dimension=0, tile...  105 us
    reduce_scatter x1, waiting for transfers between devices, per_device(): lax.psum_scatter(grad_cross_out, ('dp', 'fsdp'), scatter_dimension=0, til...  105 us
    reduce_scatter x1, waiting for transfers between devices, per_device(): lax.psum_scatter(grad_self_value, ('dp', 'fsdp'), scatter_dimension=0, ti...  104 us
    reduce_scatter x1, waiting for transfers between devices, per_device(): lax.psum_scatter(grad_cross_query, ('dp', 'fsdp'), scatter_dimension=0, t...  104 us
    unnamed x2, blocking collectives  82.1 us
  transfers between devices with their start and end apart: 20, of which 19 were waited for; matrix products, arithmetic and copies ran while one was open for 10% of the time, Pallas kernels for 0%

commit v1 on v0

--- a/solution.py
+++ b/solution.py
@@ -1,3 +1,5 @@
+import functools
+
 import jax
 import jax.numpy as jnp
 from jax import lax
@@ -108,7 +110,52 @@
     return (grad_values, grad_gain)
 
 
+AXES = ("dp", "fsdp")
+
+
+def swap_with(piece, mask, devices):
+    pairs = [(index, index ^ mask) for index in range(devices)]
+    return lax.ppermute(piece, AXES, pairs)
+
+
+def bit_of(me, bit):
+    return (me >> bit) & 1
+
+
+def pair_up(mine, theirs, my_bit, axis):
+    low = jnp.where(my_bit == 0, mine, theirs)
+    high = jnp.where(my_bit == 0, theirs, mine)
+    return jnp.stack([low, high], axis=axis)
+
+
+def gather_bits(block, order, bits, me, devices):
+    held = block
+    done = []
+    for bit in order:
+        theirs = swap_with(held, 1 << bit, devices)
+        place = sum(1 for other in done if other > bit)
+        held = pair_up(held, theirs, bit_of(me, bit), place)
+        done.append(bit)
+    return held.reshape(-1, block.shape[-1])
+
+
+def scatter_bits(partial, order, bits, me, devices):
+    rows = partial.shape[0] >> len(bits)
+    held = partial.reshape((2,) * len(bits) + (rows, partial.shape[-1]))
+    left = sorted(bits, reverse=True)
+    for bit in order:
+        place = left.index(bit)
+        mine = lax.dynamic_index_in_dim(held, bit_of(me, bit), place, keepdims=False)
+        other = lax.dynamic_index_in_dim(held, 1 - bit_of(me, bit), place, keepdims=False)
+        theirs = swap_with(other.astype(jnp.bfloat16), 1 << bit, devices)
+        held = mine.astype(jnp.float32) + theirs.astype(jnp.float32)
+        left.remove(bit)
+    return held
+
+
 def per_device(
+    fsdp,
+    devices,
     tokens,
     encoded,
     segment_ids,
@@ -128,36 +175,94 @@
     ffn_in,
     ffn_out,
 ):
-    shards = (
-        self_gain,
-        cross_gain,
-        ffn_gain,
-        self_query,
-        self_key,
-        self_value,
-        self_out,
-        cross_query,
-        cross_key,
-        cross_value,
-        cross_out,
-        ffn_in,
-        ffn_out,
-    )
-    gathered = (
-        lax.all_gather(self_gain, ("dp", "fsdp"), axis=0, tiled=True),
-        lax.all_gather(cross_gain, ("dp", "fsdp"), axis=0, tiled=True),
-        lax.all_gather(ffn_gain, ("dp", "fsdp"), axis=0, tiled=True),
-        lax.all_gather(self_query, ("dp", "fsdp"), axis=0, tiled=True),
-        lax.all_gather(self_key, ("dp", "fsdp"), axis=0, tiled=True),
-        lax.all_gather(self_value, ("dp", "fsdp"), axis=0, tiled=True),
-        lax.all_gather(self_out, ("dp", "fsdp"), axis=0, tiled=True),
-        lax.all_gather(cross_query, ("dp", "fsdp"), axis=0, tiled=True),
-        lax.all_gather(cross_key, ("dp", "fsdp"), axis=0, tiled=True),
-        lax.all_gather(cross_value, ("dp", "fsdp"), axis=0, tiled=True),
-        lax.all_gather(cross_out, ("dp", "fsdp"), axis=0, tiled=True),
-        lax.all_gather(ffn_in, ("dp", "fsdp"), axis=0, tiled=True),
-        lax.all_gather(ffn_out, ("dp", "fsdp"), axis=0, tiled=True),
-    )
+    me = lax.axis_index("dp") * fsdp + lax.axis_index("fsdp")
+    core = bit_of(me, 0)
+    chip_bits = list(range(1, devices.bit_length() - 1))
+    line_bits = [bit for bit in reversed(chip_bits) if bit > 2]
+    forward_orders = (line_bits + [2, 1], line_bits + [1, 2])
+    backward_orders = ([2, 1] + line_bits[::-1], [1, 2] + line_bits[::-1])
+
+    def my_columns(matrix, owner):
+        half = matrix.shape[-1] // 2
+        return lax.dynamic_slice_in_dim(matrix, owner * half, half, axis=matrix.ndim - 1)
+
+    def gather_group(first, second, extra):
+        pieces = [first, second]
+        counts = len(first)
+        send = jnp.concatenate([my_columns(s, 1 - core) for s in first + second] + extra, axis=1)
+        keep = jnp.concatenate([my_columns(s, core) for s in first + second] + extra, axis=1)
+        theirs = swap_with(send, 1, devices)
+        block = pair_up(keep, theirs, core, 0).reshape(-1, keep.shape[1])
+        cut = counts * (first[0].shape[1] // 2)
+        parts = [block[:, cut:], block[:, :cut]]
+        wholes = []
+        for part, order in zip(parts, forward_orders):
+            mine = gather_bits(part, order, chip_bits, me, devices)
+            sibling = swap_with(mine[:, : cut], 1, devices)
+            pair = (jnp.where(core == 0, mine[:, :cut], sibling), jnp.where(core == 0, sibling, mine[:, :cut]))
+            half = cut // counts
+            wholes.append(
+                [
+                    jnp.concatenate([side[:, n * half : (n + 1) * half] for side in pair], axis=1)
+                    for n in range(counts)
+                ]
+                + [mine[:, cut:]]
+            )
+        return wholes[1][:-1], wholes[0][:-1], wholes[0][-1]
+
+    gains = jnp.stack([self_gain, cross_gain, ffn_gain], axis=1)
+    gains = jnp.pad(gains, ((0, 0), (0, 125)))
+    (weight_query, weight_key), (weight_value, weight_out), gain_block = gather_group(
+        [self_query, self_key], [self_value, self_out], [gains]
+    )
+    (weight_cq, weight_ck), (weight_cv, weight_co), unused_block = gather_group(
+        [cross_query, cross_key], [cross_value, cross_out], []
+    )
+    gain_self, gain_cross, gain_ffn = gain_block[:, 0], gain_block[:, 1], gain_block[:, 2]
+    model = ffn_out.shape[1]
+    rows_in = ffn_in.shape[0]
+    ffn_shard = jnp.concatenate(
+        [ffn_in[:, n * model : (n + 1) * model] for n in range(ffn_in.shape[1] // model)] + [ffn_out],
+        axis=0,
+    )
+    ffn_all = lax.all_gather(ffn_shard, AXES, axis=0)
+    blocks_in = ffn_in.shape[1] // model
+    weight_in = jnp.concatenate(
+        [ffn_all[:, n * rows_in : (n + 1) * rows_in].reshape(-1, model) for n in range(blocks_in)], axis=1
+    )
+    weight_down = ffn_all[:, blocks_in * rows_in :].reshape(-1, model)
+
+    def core_terms(left, right):
+        mine = product_left(left, my_columns(right, core)).astype(jnp.bfloat16)
+        other = product_left(left, my_columns(right, 1 - core)).astype(jnp.bfloat16)
+        return mine, other
+
+    def core_sum(mine, other):
+        theirs = swap_with(other, 1, devices)
+        return mine.astype(jnp.float32) + theirs.astype(jnp.float32)
+
+    def reduce_groups(group_first, group_second):
+        answers = []
+        for group, order in zip((group_first, group_second), backward_orders):
+            mine = jnp.concatenate([pair[0] for pair in group], axis=1)
+            other = jnp.concatenate([pair[1] for pair in group], axis=1)
+            total = core_sum(mine, other)
+            total = scatter_bits(total, order, chip_bits, me, devices)
+            half_rows = total.shape[0] // 2
+            keep = lax.dynamic_slice_in_dim(total, core * half_rows, half_rows, axis=0)
+            send = lax.dynamic_slice_in_dim(total, (1 - core) * half_rows, half_rows, axis=0)
+            theirs = swap_with(send, 1, devices)
+            low = jnp.where(core == 0, keep, theirs)
+            high = jnp.where(core == 0, theirs, keep)
+            at = 0
+            found = []
+            for pair in group:
+                width = pair[0].shape[1]
+                found.append(jnp.concatenate([low[:, at : at + width], high[:, at : at + width]], axis=1))
+                at += width
+            answers.append(found)
+        return answers
+
     segments = segment_ids[0]
     groups_row = passage_group[0]
     row_count = tokens.shape[0]
@@ -175,21 +280,6 @@
     def cross_rule(begin_row, block_rows):
         return token_group[begin_row : begin_row + block_rows, None] == key_group[None, :]
 
-    (
-        gain_self,
-        gain_cross,
-        gain_ffn,
-        weight_query,
-        weight_key,
-        weight_value,
-        weight_out,
-        weight_cq,
-        weight_ck,
-        weight_cv,
-        weight_co,
-        weight_in,
-        weight_down,
-    ) = gathered
     hidden_in = tokens.astype(jnp.float32)
     normed_one = rms_norm(hidden_in, gain_self.astype(jnp.float32)).astype(jnp.bfloat16)
     queries_one = product(normed_one, weight_query).astype(jnp.bfloat16)
@@ -207,60 +297,49 @@
     pre_act = product(normed_three, weight_in)
     activated = jax.nn.gelu(pre_act).astype(jnp.bfloat16)
     block_out = (after_cross + product(activated, weight_down)).astype(jnp.bfloat16)
-    again = (
-        lax.all_gather(shards[0], ("dp", "fsdp"), axis=0, tiled=True),
-        lax.all_gather(shards[1], ("dp", "fsdp"), axis=0, tiled=True),
-        lax.all_gather(shards[2], ("dp", "fsdp"), axis=0, tiled=True),
-        lax.all_gather(shards[3], ("dp", "fsdp"), axis=0, tiled=True),
-        lax.all_gather(shards[4], ("dp", "fsdp"), axis=0, tiled=True),
-        lax.all_gather(shards[5], ("dp", "fsdp"), axis=0, tiled=True),
-        lax.all_gather(shards[6], ("dp", "fsdp"), axis=0, tiled=True),
-        lax.all_gather(shards[7], ("dp", "fsdp"), axis=0, tiled=True),
-        lax.all_gather(shards[8], ("dp", "fsdp"), axis=0, tiled=True),
-        lax.all_gather(shards[9], ("dp", "fsdp"), axis=0, tiled=True),
-        lax.all_gather(shards[10], ("dp", "fsdp"), axis=0, tiled=True),
-        lax.all_gather(shards[11], ("dp", "fsdp"), axis=0, tiled=True),
-        lax.all_gather(shards[12], ("dp", "fsdp"), axis=0, tiled=True),
-    )
-    (
-        gain_self,
-        gain_cross,
-        gain_ffn,
-        weight_query,
-        weight_key,
-        weight_value,
-        weight_out,
-        weight_cq,
-        weight_ck,
-        weight_cv,
-        weight_co,
-        weight_in,
-        weight_down,
-    ) = again
-    grad_down = product_left(activated, cotangent)
-    summed_down = lax.psum_scatter(grad_down, ("dp", "fsdp"), scatter_dimension=0, tiled=True)
+    terms_down = core_terms(activated, cotangent)
     grad_act = product_right(cotangent, weight_down).astype(jnp.bfloat16)
     unused_act, gelu_back = jax.vjp(jax.nn.gelu, pre_act)
     grad_pre = gelu_back(grad_act.astype(jnp.float32))[0].astype(jnp.bfloat16)
-    grad_in = product_left(normed_three, grad_pre)
+    terms_in = core_terms(normed_three, grad_pre)
     grad_normed_three = product_right(grad_pre, weight_in)
     grad_residual, grad_gain_three = norm_backward(
         after_cross, gain_ffn.astype(jnp.float32), grad_normed_three
     )
     grad_after_cross = cotangent.astype(jnp.float32) + grad_residual
-    summed_up = (
-        lax.psum_scatter(grad_gain_three, ("dp", "fsdp"), scatter_dimension=0, tiled=True),
-        lax.psum_scatter(grad_in, ("dp", "fsdp"), scatter_dimension=0, tiled=True),
+    half_in = terms_in[0].shape[1] // 2
+    down_chips = [
+        term.reshape(devices // 2, 2, -1, term.shape[1]).swapaxes(0, 1).reshape(2, -1, term.shape[1])
+        for term in terms_down
+    ]
+    ((sum_in_first,), (sum_in_second,)) = reduce_groups(
+        [(terms_in[0][:, :half_in], terms_in[1][:, :half_in])],
+        [(terms_in[0][:, half_in:], terms_in[1][:, half_in:])],
+    )
+    quarter = half_in
+    summed_in = jnp.concatenate(
+        [sum_in_first[:, :quarter], sum_in_second[:, :quarter], sum_in_first[:, quarter:], sum_in_second[:, quarter:]],
+        axis=1,
+    )
+    down_parts = []
+    for side, order in zip((0, 1), backward_orders):
+        total = core_sum(down_chips[0][side], down_chips[1][side])
+        down_parts.append(scatter_bits(total, order, chip_bits, me, devices))
+    down_keep = jnp.where(core == 0, down_parts[0], down_parts[1])
+    down_send = jnp.where(core == 0, down_parts[1], down_parts[0])
+    down_theirs = swap_with(down_send, 1, devices)
+    summed_down = jnp.concatenate(
+        [jnp.where(core == 0, down_keep, down_theirs), jnp.where(core == 0, down_theirs, down_keep)], axis=1
     )
     branch_two = grad_after_cross.astype(jnp.bfloat16)
-    grad_cross_out = product_left(context_two, branch_two)
+    terms_co = core_terms(context_two, branch_two)
     grad_context_two = product_right(branch_two, weight_co).astype(jnp.bfloat16)
     grad_queries_two, grad_keys_two, grad_values_two = attend_backward(
         queries_two, keys_two, values_two, log_two, grad_context_two, cross_rule
     )
-    grad_cross_query = product_left(normed_two, grad_queries_two)
-    grad_cross_key = product_left(encoded, grad_keys_two)
-    grad_cross_value = product_left(encoded, grad_values_two)
+    terms_cq = core_terms(normed_two, grad_queries_two)
+    terms_ck = core_terms(encoded, grad_keys_two)
+    terms_cv = core_terms(encoded, grad_values_two)
     grad_normed_two = product_right(grad_queries_two, weight_cq)
     encoded_grad = product_right(grad_keys_two, weight_ck) + product_right(
         grad_values_two, weight_cv
@@ -269,22 +348,16 @@
         after_self, gain_cross.astype(jnp.float32), grad_normed_two
     )
     grad_after_self = grad_after_cross + grad_residual
-    summed_cross = (
-        lax.psum_scatter(grad_gain_two, ("dp", "fsdp"), scatter_dimension=0, tiled=True),
-        lax.psum_scatter(grad_cross_query, ("dp", "fsdp"), scatter_dimension=0, tiled=True),
-        lax.psum_scatter(grad_cross_key, ("dp", "fsdp"), scatter_dimension=0, tiled=True),
-        lax.psum_scatter(grad_cross_value, ("dp", "fsdp"), scatter_dimension=0, tiled=True),
-        lax.psum_scatter(grad_cross_out, ("dp", "fsdp"), scatter_dimension=0, tiled=True),
-    )
+    (summed_cq, summed_co), (summed_ck, summed_cv) = reduce_groups([terms_cq, terms_co], [terms_ck, terms_cv])
     branch_one = grad_after_self.astype(jnp.bfloat16)
-    grad_self_out = product_left(context_one, branch_one)
+    terms_out = core_terms(context_one, branch_one)
     grad_context_one = product_right(branch_one, weight_out).astype(jnp.bfloat16)
     grad_queries_one, grad_keys_one, grad_values_one = attend_backward(
         queries_one, keys_one, values_one, log_one, grad_context_one, self_rule
     )
-    grad_self_query = product_left(normed_one, grad_queries_one)
-    grad_self_key = product_left(normed_one, grad_keys_one)
-    grad_self_value = product_left(normed_one, grad_values_one)
+    terms_query = core_terms(normed_one, grad_queries_one)
+    terms_key = core_terms(normed_one, grad_keys_one)
+    terms_value = core_terms(normed_one, grad_values_one)
     grad_normed_one = (
         product_right(grad_queries_one, weight_query)
         + product_right(grad_keys_one, weight_key)
@@ -294,51 +367,35 @@
         hidden_in, gain_self.astype(jnp.float32), grad_normed_one
     )
     tokens_grad = grad_after_self + grad_residual
-    summed_self = (
-        lax.psum_scatter(grad_gain_one, ("dp", "fsdp"), scatter_dimension=0, tiled=True),
-        lax.psum_scatter(grad_self_query, ("dp", "fsdp"), scatter_dimension=0, tiled=True),
-        lax.psum_scatter(grad_self_key, ("dp", "fsdp"), scatter_dimension=0, tiled=True),
-        lax.psum_scatter(grad_self_value, ("dp", "fsdp"), scatter_dimension=0, tiled=True),
-        lax.psum_scatter(grad_self_out, ("dp", "fsdp"), scatter_dimension=0, tiled=True),
-    )
-    summed = (
-        summed_self[0],
-        summed_cross[0],
-        summed_up[0],
-        summed_self[1],
-        summed_self[2],
-        summed_self[3],
-        summed_self[4],
-        summed_cross[1],
-        summed_cross[2],
-        summed_cross[3],
-        summed_cross[4],
-        summed_up[1],
-        summed_down,
-    )
+    grad_gains = jnp.pad(jnp.stack([grad_gain_one, grad_gain_two, grad_gain_three], axis=1), ((0, 0), (0, 125)))
+    grad_gains = grad_gains.astype(jnp.bfloat16)
+    (summed_query, summed_key, summed_gains), (summed_value, summed_out) = reduce_groups(
+        [terms_query, terms_key, (grad_gains, grad_gains)], [terms_value, terms_out]
+    )
+    own_gains = jnp.where(core == 0, summed_gains[:, :128], summed_gains[:, 128:])
     return (
         block_out,
         tokens_grad,
         encoded_grad,
-        summed[0],
-        summed[1],
-        summed[2],
-        summed[3],
-        summed[4],
-        summed[5],
-        summed[6],
-        summed[7],
-        summed[8],
-        summed[9],
-        summed[10],
-        summed[11],
-        summed[12],
+        own_gains[:, 0],
+        own_gains[:, 1],
+        own_gains[:, 2],
+        summed_query,
+        summed_key,
+        summed_value,
+        summed_out,
+        summed_cq,
+        summed_ck,
+        summed_cv,
+        summed_co,
+        summed_in,
+        summed_down,
     )
 
 
 def solution(mesh):
     return jax.shard_map(
-        per_device,
+        functools.partial(per_device, mesh.shape["fsdp"], mesh.size),
         mesh=mesh,
         in_specs=(
             P(("dp", "fsdp"), None),

time: 1780 us -> 523 us (0.29)
  waiting for transfers between devices: 1430 us -> 134 us
  blocking collectives: 82.1 us -> 0 us
  starting transfers between devices: 1.26 us -> 81.5 us
  local copies, waits for them, and re-layouts: 21.4 us -> 61.8 us
  matrix products: 189 us -> 154 us
  other arithmetic: 37.3 us -> 68.2 us
    reduce_scatter x8 -> x0, waiting for transfers between devices: 755 us -> none  [the longest x1 142 us: per_device(): lax.psum_scatter(grad_down, ('dp', 'fsdp'), scatter_dimension=0, tiled=True)]
    all_gather x10 -> x1, waiting for transfers between devices: 459 us -> 0.02 us  [per_device(): ffn_all = lax.all_gather(ffn_shard, AXES, axis=0)]
    unnamed x22 -> x1, waiting for transfers between devices: 215 us -> 0.02 us
    ppermute x0 -> x69, waiting for transfers between devices: none -> 134 us  [swap_with(): return lax.ppermute(piece, AXES, pairs)]
    unnamed x2 -> x0, blocking collectives: 82.1 us -> none
    ppermute x0 -> x69, starting transfers between devices: none -> 81.5 us  [swap_with(): return lax.ppermute(piece, AXES, pairs)]
    dot_general x10 -> x20, matrix products: 41.7 us -> 26.8 us  [product_left(): jnp.einsum('ti,td->id', left_side, right_side, preferred_element_type=jnp...]
  transfers between devices with their start and end apart: 20 -> 70, of which waited for: 19 -> 31; matrix products, arithmetic and copies ran while one was open for 10% -> 26% of each run, Pallas kernels for 0% -> 0%
where the time goes in v1:
time: 523 us; the launch traced here: 517 us
  matrix products  154 us (29%)
  waiting for transfers between devices  134 us (26%)
  starting transfers between devices  81.5 us (16%)
  other arithmetic  68.2 us (13%)
  local copies, waits for them, and re-layouts  61.8 us (12%)
  between operations  16.9 us (3%)
    ppermute x69, waiting for transfers between devices, swap_with(): return lax.ppermute(piece, AXES, pairs)  134 us
    ppermute x69, starting transfers between devices, swap_with(): return lax.ppermute(piece, AXES, pairs)  81.5 us
    dot_general x10, matrix products, product_right(): jnp.einsum('td,id->ti', left_side, right_side, preferred_element_type=jnp...  30.3 us
    dot_general x20, matrix products, product_left(): jnp.einsum('ti,td->id', left_side, right_side, preferred_element_type=jnp...  26.8 us
    convert_element_type x2, other arithmetic, attend_backward(): score_grad = (probabilities * (prob_grad - inner_sum)).astype(jnp.bfloat16)  21.6 us
    dot_general x10, matrix products, product(): return jnp.dot(left_side, right_side, preferred_element_type=jnp.float32)  20.2 us
    dot_general x2, matrix products, attend_backward(): jnp.einsum('qhd,khd->hqk', grad_block, value_heads, preferred_element_typ...  19.6 us
    unnamed x199, local copies, waits for them, and re-layouts  18.2 us
  transfers between devices with their start and end apart: 70, of which 31 were waited for; matrix products, arithmetic and copies ran while one was open for 26% of the time, Pallas kernels for 0%

profile of v1, /device:TPU:0, one launch (start us, length us, event | category | flops | bytes accessed | tf_op | source)
XLA Modules:
  0.0 516.6 jit_solution(10133328884258486880)
XLA Ops:
  18.9 4.1 collective-permute-start.17
  29.3 8.1 %collective-permute-start.18 = (bf16[2,48,768]{2,1,0:T(8,128)(2,1)S(1)}, bf16[2,48,768]{2,1,0:T(8,128)(2,1)S(1)}, u32[]{:S(2)}, u32[]{:S(2)}) collective-permute-start(bf16[2,48,768]{2,1,0:T(8,128)(2,1)S(1)} %pad_maximum_fusion.51), channel_id=1, source_target_pairs={{0,8},{1,9},{2,10},{3,11},{4,12},{5,13},{6,14},{7,15},{8,0},{9,1},... | collective-permute-start | bytes 442376 | tf_op jit(solution)/shard_map/ppermute | solution.py:118
  57.5 6.5 %collective-permute-done.8 = bf16[2,2,48,768]{3,2,0,1:T(8,128)(2,1)S(1)} collective-permute-done((bf16[2,2,48,768]{3,2,0,1:T(8,128)(2,1)S(1)}, bf16[2,2,48,768]{3,2,0,1:T(8,128)(2,1)S(1)}, u32[]{:S(2)}, u32[]{:S(2)}) %collective-permute-start.8) | collective-permute-done | bytes 294944 | tf_op jit(solution)/shard_map/ppermute | solution.py:118
  65.9 12.2 %collective-permute-done.14 = bf16[2,2,48,768]{3,2,0,1:T(8,128)(2,1)S(1)} collective-permute-done((bf16[2,2,48,768]{3,2,0,1:T(8,128)(2,1)S(1)}, bf16[2,2,48,768]{3,2,0,1:T(8,128)(2,1)S(1)}, u32[]{:S(2)}, u32[]{:S(2)}) %collective-permute-start.14) | collective-permute-done | bytes 294944 | tf_op jit(solution)/shard_map/ppermute | solution.py:118
  80.5 13.9 %collective-permute-done.20 = bf16[2,2,2,48,768]{4,3,0,1,2:T(8,128)(2,1)S(1)} collective-permute-done((bf16[2,2,2,48,768]{4,3,0,1,2:T(8,128)(2,1)S(1)}, bf16[2,2,2,48,768]{4,3,0,1,2:T(8,128)(2,1)S(1)}, u32[]{:S(2)}, u32[]{:S(2)}) %collective-permute-start.20) | collective-permute-done | bytes 589856 | tf_op jit(solution)/shard_map/ppermute | solution.py:118
  94.8 23.3 %collective-permute-done.9 = bf16[2,2,2,48,768]{4,3,0,1,2:T(8,128)(2,1)S(1)} collective-permute-done((bf16[2,2,2,48,768]{4,3,0,1,2:T(8,128)(2,1)S(1)}, bf16[2,2,2,48,768]{4,3,0,1,2:T(8,128)(2,1)S(1)}, u32[]{:S(2)}, u32[]{:S(2)}) %collective-permute-start.9) | collective-permute-done | bytes 589856 | tf_op jit(solution)/shard_map/ppermute | solution.py:118
  126.0 7.3 %convolution_convert_fusion = bf16[768,4096]{1,0:T(8,128)(2,1)} fusion(bf16[4096,768]{1,0:T(8,128)(2,1)S(1)} %bitcast.455, bf16[768,384]{1,0:T(8,128)(2,1)S(1)} %get-tuple-element.58, bf16[768,384]{1,0:T(8,128)(2,1)S(1)} %get-tuple-element.56), kind=kOutput, calls=%fused_computation.13 | convolution fusion | flops 4837343232 | bytes 13762560 | tf_op jit(solution)/shard_map/dot_general | solution.py:26
  142.2 7.0 %convolution_convert_fusion.1 = bf16[768,4096]{1,0:T(8,128)(2,1)} fusion(bf16[4096,768]{1,0:T(8,128)(2,1)S(1)} %bitcast.457, bf16[768,384]{1,0:T(8,128)(2,1)S(1)} %get-tuple-element.55, bf16[768,384]{1,0:T(8,128)(2,1)S(1)} %get-tuple-element.53), kind=kOutput, calls=%fused_computation.14 | convolution fusion | flops 4837343232 | bytes 13762560 | tf_op jit(solution)/shard_map/dot_general | solution.py:26
  155.8 12.6 %fusion.207 = (f32[12,128]{1,0:T(8,128)S(1)}, f32[12,128,4096]{2,1,0:T(8,128)}) fusion(bf16[128,12,64]{0,2,1:T(8,128)(2,1)S(1)} %bitcast.402, bf16[4096,12,64]{0,2,1:T(8,128)(2,1)} %bitcast.365, pred[128,4096]{1,0:T(8,128)(4,1)S(1)} %broadcast_compare_fusion), kind=kOutput, calls=%fused_computation.490 | convolution fusion | flops 824179200 | bytes 32184320 | tf_op jit(solution)/shard_map/qhd,khd->hqk/dot_general | solution.py:43
  168.4 10.6 %fusion = f32[12,128]{1,0:T(8,128)S(1)} fusion(f32[12,128,4096]{2,1,0:T(8,128)} %get-tuple-element.156, f32[12,128]{1,0:T(8,128)S(1)} %get-tuple-element.155), kind=kLoop, calls=%fused_computation.6 | loop fusion | flops 12581376 | bytes 25178112 | tf_op jit(solution)/shard_map/reduce_sum | solution.py:58
  179.1 12.5 %fusion.55 = bf16[12,64,128]{2,1,0:T(8,128)(2,1)S(1)} fusion(bf16[4096,12,64]{0,2,1:T(8,128)(2,1)} %bitcast.391, f32[12,128,4096]{2,1,0:T(8,128)} %get-tuple-element.156, f32[12,128]{1,0:T(8,128)S(1)} %fusion, f32[12,128]{1,0:T(8,128)S(1)} %get-tuple-element.155), kind=kOutput, calls=%fused_computation.133 | convolution fusion | flops 824279040 | bytes 31666176 | tf_op jit(solution)/shard_map/hqk,khd->qhd/dot_general | solution.py:60
  206.8 19.3 %multiply_reduce_fusion = (f32[12,128]{1,0:T(8,128)S(1)}, f32[12,128,4096]{2,1,0:T(8,128)}) fusion(f32[12,128,4096]{2,1,0:T(8,128)} %get-tuple-element.156, f32[12,128]{1,0:T(8,128)S(1)} %log_add_fusion.1, bf16[128,12,64]{0,2,1:T(8,128)(2,1)S(1)} %bitcast.406, bf16[4096,12,64]{0,2,1:T(8,128)(2,1)} %bitcast.392), kind=kOutput, calls=%fused_computation.1 | convolution fusion | flops 824179200 | bytes 56832000 | tf_op jit(solution)/shard_map/qhd,khd->hqk/dot_general | solution.py:87
  226.1 21.5 %multiply_convert_fusion = bf16[12,128,4096]{2,1,0:T(8,128)(2,1)} fusion(f32[12,128,4096]{2,1,0:T(8,128)} %get-tuple-element.161, f32[12,128,4096]{2,1,0:T(8,128)} %get-tuple-element.156, f32[12,128]{1,0:T(8,128)S(1)} %get-tuple-element.160, f32[12,128]{1,0:T(8,128)S(1)} %log_add_fusion.1), kind=kLoop, calls=%fused_computation | loop fusion | flops 25165824 | bytes 62926848 | tf_op jit(solution)/shard_map/convert_element_type | solution.py:91
  247.6 10.8 %fusion.52 = bf16[12,64,128]{2,1,0:T(8,128)(2,1)S(1)} fusion(bf16[4096,12,64]{0,2,1:T(8,128)(2,1)} %bitcast.366, bf16[12,128,4096]{2,1,0:T(8,128)(2,1)} %multiply_convert_fusion), kind=kOutput, calls=%fused_computation.122 | convolution fusion | flops 805502976 | bytes 19070976 | tf_op jit(solution)/shard_map/hqk,khd->qhd/dot_general | solution.py:92
  265.0 12.7 %fusion.6 = bf16[12,64,4096]{2,1,0:T(8,128)(2,1)} fusion(bf16[128,12,64]{0,2,1:T(8,128)(2,1)S(1)} %bitcast.407, f32[12,128,4096]{2,1,0:T(8,128)} %get-tuple-element.156, f32[12,128]{1,0:T(8,128)S(1)} %log_add_fusion.1), kind=kOutput, calls=%fused_computation.12 | convolution fusion | flops 821035008 | bytes 31660032 | tf_op jit(solution)/shard_map/hqk,qhd->khd/dot_general | solution.py:81
  277.7 6.5 %multiply_convert_fusion.1 = bf16[12,64,4096]{2,1,0:T(8,128)(2,1)S(1)} fusion(bf16[128,12,64]{0,2,1:T(8,128)(2,1)S(1)} %bitcast.403, bf16[12,128,4096]{2,1,0:T(8,128)(2,1)} %multiply_convert_fusion), kind=kOutput, calls=%fused_computation.9 | convolution fusion | flops 811597824 | bytes 19070976 | tf_op jit(solution)/shard_map/hqk,qhd->khd/dot_general | solution.py:97
  290.7 8.4 %fusion.59 = f32[4096,768]{1,0:T(8,128)} fusion(bf16[4096,768]{0,1:T(8,128)(2,1)S(1)} %bitcast.393, bf16[768,384]{1,0:T(8,128)(2,1)S(1)} %copy-done.59, bf16[768,384]{1,0:T(8,128)(2,1)S(1)} %copy-done.63), kind=kOutput, calls=%fused_computation.147 | convolution fusion | flops 4834197504 | bytes 20054016 | tf_op jit(solution)/shard_map/td,id->ti/dot_general | solution.py:34
  299.1 5.6 %fusion.39 = bf16[768,384]{0,1:T(8,128)(2,1)S(1)} fusion(bf16[4096,768]{1,0:T(8,128)(2,1)} %param.19, bf16[4096,768]{0,1:T(8,128)(2,1)S(1)} %bitcast.394, s32[]{:T(128)S(6)} %select_n.491), kind=kOutput, calls=%fused_computation.73 | convolution fusion | flops 2416214016 | bytes 10027012 | tf_op jit(solution)/shard_map/ti,td->id/dot_general | solution.py:30
  304.7 3.5 fusion.45
  308.2 3.5 fusion.42
  311.6 3.4 fusion.48
  320.0 11.4 %convolution_add_fusion = f32[4096,768]{1,0:T(8,128)} fusion(f32[4096,768]{1,0:T(8,128)} %fusion.59, bf16[4096,768]{0,1:T(8,128)(2,1)S(1)} %bitcast.369, bf16[768,384]{1,0:T(8,128)(2,1)S(1)} %copy-done.48, bf16[768,384]{1,0:T(8,128)(2,1)S(1)} %copy-done.50), kind=kOutput, calls=%fused_computation.15 | convolution fusion | flops 4837343232 | bytes 32636928 | tf_op jit(solution)/shard_map/td,id->ti/dot_general | solution.py:34
  398.5 8.9 %collective-permute-done.53 = bf16[2,2,2,48,768]{4,3,0,1,2:T(8,128)(2,1)} collective-permute-done((bf16[2,2,2,48,768]{4,3,0,1,2:T(8,128)(2,1)}, bf16[2,2,2,48,768]{4,3,0,1,2:T(8,128)(2,1)}, u32[]{:S(2)}, u32[]{:S(2)}) %collective-permute-start.53) | collective-permute-done | bytes 589856 | tf_op jit(solution)/shard_map/ppermute | solution.py:118
  414.1 5.9 %collective-permute-done.64 = bf16[2,2,2,96,384]{4,3,0,1,2:T(8,128)(2,1)S(1)} collective-permute-done((bf16[2,2,2,96,384]{4,3,0,1,2:T(8,128)(2,1)S(1)}, bf16[2,2,2,96,384]{4,3,0,1,2:T(8,128)(2,1)S(1)}, u32[]{:S(2)}, u32[]{:S(2)}) %collective-permute-start.64) | collective-permute-done | bytes 589856 | tf_op jit(solution)/shard_map/ppermute | solution.py:118
  424.9 5.5 %collective-permute-done.30 = bf16[2,2,48,768]{3,2,1,0:T(8,128)(2,1)S(1)} collective-permute-done((bf16[2,2,48,768]{3,2,1,0:T(8,128)(2,1)S(1)}, bf16[2,2,48,768]{3,2,1,0:T(8,128)(2,1)S(1)}, u32[]{:S(2)}, u32[]{:S(2)}) %collective-permute-start.30) | collective-permute-done | bytes 294944 | tf_op jit(solution)/shard_map/ppermute | solution.py:118
  433.2 3.5 collective-permute-done.42
  437.6 5.5 %collective-permute-done.54 = bf16[2,2,48,768]{3,2,0,1:T(8,128)(2,1)S(1)} collective-permute-done((bf16[2,2,48,768]{3,2,0,1:T(8,128)(2,1)S(1)}, bf16[2,2,48,768]{3,2,0,1:T(8,128)(2,1)S(1)}, u32[]{:S(2)}, u32[]{:S(2)}) %collective-permute-start.54) | collective-permute-done | bytes 294944 | tf_op jit(solution)/shard_map/ppermute | solution.py:118
  459.3 4.9 collective-permute-start.32
  464.3 3.9 collective-permute-start.38
  476.6 4.8 collective-permute-done.44
  493.5 5.5 %collective-permute-done.25 = bf16[2,48,896]{2,1,0:T(8,128)(2,1)S(1)} collective-permute-done((bf16[2,48,896]{2,1,0:T(8,128)(2,1)S(1)}, bf16[2,48,896]{2,1,0:T(8,128)(2,1)S(1)}, u32[]{:S(2)}, u32[]{:S(2)}) %collective-permute-start.25) | collective-permute-done | bytes 172064 | tf_op jit(solution)/shard_map/ppermute | solution.py:118
  499.5 6.4 %collective-permute-done.26 = bf16[48,896]{1,0:T(8,128)(2,1)S(1)} collective-permute-done((bf16[48,896]{1,0:T(8,128)(2,1)S(1)}, bf16[48,896]{1,0:T(8,128)(2,1)S(1)}, u32[]{:S(2)}, u32[]{:S(2)}) %collective-permute-start.26) | collective-permute-done | bytes 86048 | tf_op jit(solution)/shard_map/ppermute | solution.py:118
  (574 shorter events, 220.5 us)
Async XLA Ops:
  7.2 185.0 %all-gather.3.cloned.1.call-start = ((), (), s32[]{:S(2)}) async-start(), calls=%async_computation | async-start | bytes 9732096 | tf_op jit(solution)/shard_map/all_gather | solution.py:228
  23.1 17.7 %collective-permute-start.1 = (bf16[48,896]{1,0:T(8,128)(2,1)S(1)}, bf16[48,896]{1,0:T(8,128)(2,1)S(1)}, u32[]{:S(2)}, u32[]{:S(2)}) collective-permute-start(bf16[48,896]{1,0:T(8,128)(2,1)S(1)} %slice.258), channel_id=1, source_target_pairs={{0,16},{1,17},{2,18},{3,19},{4,20},{5,21},{6,22},{7,23},{8,24},{9,... | collective-permute-start | bytes 258056 | tf_op jit(solution)/shard_map/ppermute | solution.py:118
  29.3 16.1 %collective-permute-start.18 = (bf16[2,48,768]{2,1,0:T(8,128)(2,1)S(1)}, bf16[2,48,768]{2,1,0:T(8,128)(2,1)S(1)}, u32[]{:S(2)}, u32[]{:S(2)}) collective-permute-start(bf16[2,48,768]{2,1,0:T(8,128)(2,1)S(1)} %pad_maximum_fusion.51), channel_id=1, source_target_pairs={{0,8},{1,9},{2,10},{3,11},{4,12},{5,13},{6,14},{7,15},{8,0},{9,1},... | collective-permute-start | bytes 442376 | tf_op jit(solution)/shard_map/ppermute | solution.py:118
  52.3 27.4 %collective-permute-start.3 = (bf16[2,2,48,896]{3,2,1,0:T(8,128)(2,1)S(1)}, bf16[2,2,48,896]{3,2,1,0:T(8,128)(2,1)S(1)}, u32[]{:S(2)}, u32[]{:S(2)}) collective-permute-start(bf16[2,2,48,896]{3,2,1,0:T(8,128)(2,1)S(1)} %pad_maximum_fusion.40), channel_id=1, source_target_pairs={{0,4},{1,5},{2,6},{3,7},{4,0},{5,1},{6,2},{7,3},{8,12},{9,13},{10,... | collective-permute-start | bytes 1032200 | tf_op jit(solution)/shard_map/ppermute | solution.py:118
  55.1 23.0 %collective-permute-start.14 = (bf16[2,2,48,768]{3,2,0,1:T(8,128)(2,1)S(1)}, bf16[2,2,48,768]{3,2,0,1:T(8,128)(2,1)S(1)}, u32[]{:S(2)}, u32[]{:S(2)}) collective-permute-start(bf16[2,2,48,768]{3,2,0,1:T(8,128)(2,1)S(1)} %pad_maximum_fusion.42), channel_id=1, source_target_pairs={{0,4},{1,5},{2,6},{3,7},{4,0},{5,1},{6,2},{7,3},{8,12},{9,13},{10,... | collective-permute-start | bytes 884744 | tf_op jit(solution)/shard_map/ppermute | solution.py:118
  57.0 37.5 %collective-permute-start.20 = (bf16[2,2,2,48,768]{4,3,0,1,2:T(8,128)(2,1)S(1)}, bf16[2,2,2,48,768]{4,3,0,1,2:T(8,128)(2,1)S(1)}, u32[]{:S(2)}, u32[]{:S(2)}) collective-permute-start(bf16[2,2,2,48,768]{4,3,0,1,2:T(8,128)(2,1)S(1)} %pad_maximum_fusion.39), channel_id=1, source_target_pairs={{0,4},{1,5},{2,6},{3,7},{4,0},{5,1},{6,2},{7,3},{8,12},{9,13},{10,... | collective-permute-start | bytes 1769480 | tf_op jit(solution)/shard_map/ppermute | solution.py:118
  64.2 53.9 %collective-permute-start.9 = (bf16[2,2,2,48,768]{4,3,0,1,2:T(8,128)(2,1)S(1)}, bf16[2,2,2,48,768]{4,3,0,1,2:T(8,128)(2,1)S(1)}, u32[]{:S(2)}, u32[]{:S(2)}) collective-permute-start(bf16[2,2,2,48,768]{4,3,0,1,2:T(8,128)(2,1)S(1)} %pad_maximum_fusion.37), channel_id=1, source_target_pairs={{0,4},{1,5},{2,6},{3,7},{4,0},{5,1},{6,2},{7,3},{8,12},{9,13},{10,... | collective-permute-start | bytes 1769480 | tf_op jit(solution)/shard_map/ppermute | solution.py:118
  78.2 40.3 %collective-permute-start.15 = (bf16[2,2,2,48,768]{4,3,0,1,2:T(8,128)(2,1)S(1)}, bf16[2,2,2,48,768]{4,3,0,1,2:T(8,128)(2,1)S(1)}, u32[]{:S(2)}, u32[]{:S(2)}) collective-permute-start(bf16[2,2,2,48,768]{4,3,0,1,2:T(8,128)(2,1)S(1)} %pad_maximum_fusion.38), channel_id=1, source_target_pairs={{0,2},{1,3},{2,0},{3,1},{4,6},{5,7},{6,4},{7,5},{8,10},{9,11},{10,... | collective-permute-start | bytes 1769480 | tf_op jit(solution)/shard_map/ppermute | solution.py:118
  79.9 42.0 %collective-permute-start.4 = (bf16[2,2,2,48,896]{4,3,2,1,0:T(8,128)(2,1)S(1)}, bf16[2,2,2,48,896]{4,3,2,1,0:T(8,128)(2,1)S(1)}, u32[]{:S(2)}, u32[]{:S(2)}) collective-permute-start(bf16[2,2,2,48,896]{4,3,2,1,0:T(8,128)(2,1)S(1)} %pad_maximum_fusion.36), channel_id=1, source_target_pairs={{0,2},{1,3},{2,0},{3,1},{4,6},{5,7},{6,4},{7,5},{8,10},{9,11},{10,... | collective-permute-start | bytes 2064392 | tf_op jit(solution)/shard_map/ppermute | solution.py:118
  94.8 29.0 %collective-permute-start.21 = (bf16[768,768]{1,0:T(8,128)(2,1)S(1)}, bf16[768,768]{1,0:T(8,128)(2,1)S(1)}, u32[]{:S(2)}, u32[]{:S(2)}) collective-permute-start(bf16[768,768]{1,0:T(8,128)(2,1)S(1)} %bitcast.396), channel_id=1, source_target_pairs={{0,1},{1,0},{2,3},{3,2},{4,5},{5,4},{6,7},{7,6},{8,9},{9,8},{10,11... | collective-permute-start | bytes 3538952 | tf_op jit(solution)/shard_map/ppermute | solution.py:118
  119.8 18.4 %collective-permute-start.16 = (bf16[768,768]{1,0:T(8,128)(2,1)}, bf16[768,768]{1,0:T(8,128)(2,1)}, u32[]{:S(2)}, u32[]{:S(2)}) collective-permute-start(bf16[768,768]{1,0:T(8,128)(2,1)} %bitcast.44), channel_id=1, source_target_pairs={{0,1},{1,0},{2,3},{3,2},{4,5},{5,4},{6,7},{7,6},{8,9},{9,8},{10,11... | collective-permute-start | bytes 3538952 | tf_op jit(solution)/shard_map/ppermute | solution.py:118
  123.3 25.9 %collective-permute-start.5 = (bf16[768,768]{1,0:T(8,128)(2,1)}, bf16[768,768]{1,0:T(8,128)(2,1)}, u32[]{:S(2)}, u32[]{:S(2)}) collective-permute-start(bf16[768,768]{1,0:T(8,128)(2,1)} %slice.260), channel_id=1, source_target_pairs={{0,1},{1,0},{2,3},{3,2},{4,5},{5,4},{6,7},{7,6},{8,9},{9,8},{10,11... | collective-permute-start | bytes 3538952 | tf_op jit(solution)/shard_map/ppermute | solution.py:118
  332.6 47.1 %collective-permute-start.22 = (bf16[768,896]{0,1:T(8,128)(2,1)}, bf16[768,896]{0,1:T(8,128)(2,1)}, u32[]{:S(2)}, u32[]{:S(2)}) collective-permute-start(bf16[768,896]{0,1:T(8,128)(2,1)} %pad_maximum_fusion.1), channel_id=1, source_target_pairs={{0,1},{1,0},{2,3},{3,2},{4,5},{5,4},{6,7},{7,6},{8,9},{9,8},{10,11... | collective-permute-start | bytes 4128776 | tf_op jit(solution)/shard_map/ppermute | solution.py:118
  336.9 28.8 %collective-permute-start.46 = (bf16[768,768]{1,0:T(8,128)(2,1)}, bf16[768,768]{1,0:T(8,128)(2,1)}, u32[]{:S(2)}, u32[]{:S(2)}) collective-permute-start(bf16[768,768]{1,0:T(8,128)(2,1)} %get-tuple-element.42), channel_id=1, source_target_pairs={{0,1},{1,0},{2,3},{3,2},{4,5},{5,4},{6,7},{7,6},{8,9},{9,8},{10,11... | collective-permute-start | bytes 3538952 | tf_op jit(solution)/shard_map/ppermute | solution.py:118
  347.4 19.9 %collective-permute-start.52 = (bf16[768,768]{1,0:T(8,128)(2,1)}, bf16[768,768]{1,0:T(8,128)(2,1)}, u32[]{:S(2)}, u32[]{:S(2)}) collective-permute-start(bf16[768,768]{1,0:T(8,128)(2,1)} %get-tuple-element.43), channel_id=1, source_target_pairs={{0,1},{1,0},{2,3},{3,2},{4,5},{5,4},{6,7},{7,6},{8,9},{9,8},{10,11... | collective-permute-start | bytes 3538952 | tf_op jit(solution)/shard_map/ppermute | solution.py:118
  347.7 25.8 %collective-permute-start.58 = (bf16[1536,384]{1,0:T(8,128)(2,1)}, bf16[1536,384]{1,0:T(8,128)(2,1)}, u32[]{:S(2)}, u32[]{:S(2)}) collective-permute-start(bf16[1536,384]{1,0:T(8,128)(2,1)} %bitcast.156), channel_id=1, source_target_pairs={{0,1},{1,0},{2,3},{3,2},{4,5},{5,4},{6,7},{7,6},{8,9},{9,8},{10,11... | collective-permute-start | bytes 3538952 | tf_op jit(solution)/shard_map/ppermute | solution.py:118
  349.9 25.8 %collective-permute-start.63 = (bf16[1536,384]{1,0:T(8,128)(2,1)}, bf16[1536,384]{1,0:T(8,128)(2,1)}, u32[]{:S(2)}, u32[]{:S(2)}) collective-permute-start(bf16[1536,384]{1,0:T(8,128)(2,1)} %bitcast.169), channel_id=1, source_target_pairs={{0,1},{1,0},{2,3},{3,2},{4,5},{5,4},{6,7},{7,6},{8,9},{9,8},{10,11... | collective-permute-start | bytes 3538952 | tf_op jit(solution)/shard_map/ppermute | solution.py:118
  365.7 20.6 %collective-permute-start.29 = (bf16[2,2,2,48,768]{4,3,2,1,0:T(8,128)(2,1)}, bf16[2,2,2,48,768]{4,3,2,1,0:T(8,128)(2,1)}, u32[]{:S(2)}, u32[]{:S(2)}) collective-permute-start(bf16[2,2,2,48,768]{4,3,2,1,0:T(8,128)(2,1)} %fusion.64), channel_id=1, source_target_pairs={{0,2},{1,3},{2,0},{3,1},{4,6},{5,7},{6,4},{7,5},{8,10},{9,11},{10,... | collective-permute-start | bytes 1769480 | tf_op jit(solution)/shard_map/ppermute | solution.py:118
  367.3 22.0 %collective-permute-start.35 = (bf16[2,2,2,48,768]{4,3,0,1,2:T(8,128)(2,1)}, bf16[2,2,2,48,768]{4,3,0,1,2:T(8,128)(2,1)}, u32[]{:S(2)}, u32[]{:S(2)}) collective-permute-start(bf16[2,2,2,48,768]{4,3,0,1,2:T(8,128)(2,1)} %fusion.66), channel_id=1, source_target_pairs={{0,4},{1,5},{2,6},{3,7},{4,0},{5,1},{6,2},{7,3},{8,12},{9,13},{10,... | collective-permute-start | bytes 1769480 | tf_op jit(solution)/shard_map/ppermute | solution.py:118
  373.5 21.4 %collective-permute-start.41 = (bf16[2,2,2,48,768]{4,3,0,1,2:T(8,128)(2,1)}, bf16[2,2,2,48,768]{4,3,0,1,2:T(8,128)(2,1)}, u32[]{:S(2)}, u32[]{:S(2)}) collective-permute-start(bf16[2,2,2,48,768]{4,3,0,1,2:T(8,128)(2,1)} %fusion.67), channel_id=1, source_target_pairs={{0,2},{1,3},{2,0},{3,1},{4,6},{5,7},{6,4},{7,5},{8,10},{9,11},{10,... | collective-permute-start | bytes 1769480 | tf_op jit(solution)/shard_map/ppermute | solution.py:118
  375.7 31.7 %collective-permute-start.53 = (bf16[2,2,2,48,768]{4,3,0,1,2:T(8,128)(2,1)}, bf16[2,2,2,48,768]{4,3,0,1,2:T(8,128)(2,1)}, u32[]{:S(2)}, u32[]{:S(2)}) collective-permute-start(bf16[2,2,2,48,768]{4,3,0,1,2:T(8,128)(2,1)} %fusion.69), channel_id=1, source_target_pairs={{0,2},{1,3},{2,0},{3,1},{4,6},{5,7},{6,4},{7,5},{8,10},{9,11},{10,... | collective-permute-start | bytes 1769480 | tf_op jit(solution)/shard_map/ppermute | solution.py:118
  380.2 30.9 %collective-permute-start.47 = (bf16[2,2,2,48,768]{4,3,0,1,2:T(8,128)(2,1)}, bf16[2,2,2,48,768]{4,3,0,1,2:T(8,128)(2,1)}, u32[]{:S(2)}, u32[]{:S(2)}) collective-permute-start(bf16[2,2,2,48,768]{4,3,0,1,2:T(8,128)(2,1)} %fusion.68), channel_id=1, source_target_pairs={{0,4},{1,5},{2,6},{3,7},{4,0},{5,1},{6,2},{7,3},{8,12},{9,13},{10,... | collective-permute-start | bytes 1769480 | tf_op jit(solution)/shard_map/ppermute | solution.py:118
  386.3 27.4 %collective-permute-start.59 = (bf16[2,2,2,96,384]{4,3,2,1,0:T(8,128)(2,1)}, bf16[2,2,2,96,384]{4,3,2,1,0:T(8,128)(2,1)S(1)}, u32[]{:S(2)}, u32[]{:S(2)}) collective-permute-start(bf16[2,2,2,96,384]{4,3,2,1,0:T(8,128)(2,1)} %fusion.65), channel_id=1, source_target_pairs={{0,4},{1,5},{2,6},{3,7},{4,0},{5,1},{6,2},{7,3},{8,12},{9,13},{10,... | collective-permute-start | bytes 1769480 | tf_op jit(solution)/shard_map/ppermute | solution.py:118
  389.3 30.7 %collective-permute-start.64 = (bf16[2,2,2,96,384]{4,3,0,1,2:T(8,128)(2,1)S(1)}, bf16[2,2,2,96,384]{4,3,0,1,2:T(8,128)(2,1)S(1)}, u32[]{:S(2)}, u32[]{:S(2)}) collective-permute-start(bf16[2,2,2,96,384]{4,3,0,1,2:T(8,128)(2,1)S(1)} %fusion.70), channel_id=1, source_target_pairs={{0,2},{1,3},{2,0},{3,1},{4,6},{5,7},{6,4},{7,5},{8,10},{9,11},{10,... | collective-permute-start | bytes 1769480 | tf_op jit(solution)/shard_map/ppermute | solution.py:118
  394.8 29.3 %collective-permute-start.23 = (bf16[2,2,2,48,896]{4,3,2,1,0:T(8,128)(2,1)S(1)}, bf16[2,2,2,48,896]{4,3,2,1,0:T(8,128)(2,1)S(1)}, u32[]{:S(2)}, u32[]{:S(2)}) collective-permute-start(bf16[2,2,2,48,896]{4,3,2,1,0:T(8,128)(2,1)S(1)} %fusion.62), channel_id=1, source_target_pairs={{0,4},{1,5},{2,6},{3,7},{4,0},{5,1},{6,2},{7,3},{8,12},{9,13},{10,... | collective-permute-start | bytes 2064392 | tf_op jit(solution)/shard_map/ppermute | solution.py:118
  407.4 23.0 %collective-permute-start.30 = (bf16[2,2,48,768]{3,2,1,0:T(8,128)(2,1)S(1)}, bf16[2,2,48,768]{3,2,1,0:T(8,128)(2,1)S(1)}, u32[]{:S(2)}, u32[]{:S(2)}) collective-permute-start(bf16[2,2,48,768]{3,2,1,0:T(8,128)(2,1)S(1)} %fusion.88), channel_id=1, source_target_pairs={{0,4},{1,5},{2,6},{3,7},{4,0},{5,1},{6,2},{7,3},{8,12},{9,13},{10,... | collective-permute-start | bytes 884744 | tf_op jit(solution)/shard_map/ppermute | solution.py:118
  411.1 20.1 %collective-permute-start.36 = (bf16[2,2,48,768]{3,2,0,1:T(8,128)(2,1)S(1)}, bf16[2,2,48,768]{3,2,0,1:T(8,128)(2,1)S(1)}, u32[]{:S(2)}, u32[]{:S(2)}) collective-permute-start(bf16[2,2,48,768]{3,2,0,1:T(8,128)(2,1)S(1)} %fusion.89), channel_id=1, source_target_pairs={{0,2},{1,3},{2,0},{3,1},{4,6},{5,7},{6,4},{7,5},{8,10},{9,11},{10,... | collective-permute-start | bytes 884744 | tf_op jit(solution)/shard_map/ppermute | solution.py:118
  413.7 23.0 %collective-permute-start.42 = (bf16[2,2,48,768]{3,2,0,1:T(8,128)(2,1)S(1)}, bf16[2,2,48,768]{3,2,0,1:T(8,128)(2,1)S(1)}, u32[]{:S(2)}, u32[]{:S(2)}) collective-permute-start(bf16[2,2,48,768]{3,2,0,1:T(8,128)(2,1)S(1)} %fusion.90), channel_id=1, source_target_pairs={{0,4},{1,5},{2,6},{3,7},{4,0},{5,1},{6,2},{7,3},{8,12},{9,13},{10,... | collective-permute-start | bytes 884744 | tf_op jit(solution)/shard_map/ppermute | solution.py:118
  420.0 23.1 %collective-permute-start.54 = (bf16[2,2,48,768]{3,2,0,1:T(8,128)(2,1)S(1)}, bf16[2,2,48,768]{3,2,0,1:T(8,128)(2,1)S(1)}, u32[]{:S(2)}, u32[]{:S(2)}) collective-permute-start(bf16[2,2,48,768]{3,2,0,1:T(8,128)(2,1)S(1)} %fusion.92), channel_id=1, source_target_pairs={{0,4},{1,5},{2,6},{3,7},{4,0},{5,1},{6,2},{7,3},{8,12},{9,13},{10,... | collective-permute-start | bytes 884744 | tf_op jit(solution)/shard_map/ppermute | solution.py:118
  424.1 19.0 %collective-permute-start.48 = (bf16[2,2,48,768]{3,2,0,1:T(8,128)(2,1)S(1)}, bf16[2,2,48,768]{3,2,0,1:T(8,128)(2,1)S(1)}, u32[]{:S(2)}, u32[]{:S(2)}) collective-permute-start(bf16[2,2,48,768]{3,2,0,1:T(8,128)(2,1)S(1)} %fusion.91), channel_id=1, source_target_pairs={{0,2},{1,3},{2,0},{3,1},{4,6},{5,7},{6,4},{7,5},{8,10},{9,11},{10,... | collective-permute-start | bytes 884744 | tf_op jit(solution)/shard_map/ppermute | solution.py:118
  431.3 17.5 %collective-permute-start.65 = (bf16[2,2,96,384]{3,2,0,1:T(8,128)(2,1)S(1)}, bf16[2,2,96,384]{3,2,0,1:T(8,128)(2,1)S(1)}, u32[]{:S(2)}, u32[]{:S(2)}) collective-permute-start(bf16[2,2,96,384]{3,2,0,1:T(8,128)(2,1)S(1)} %fusion.94), channel_id=1, source_target_pairs={{0,4},{1,5},{2,6},{3,7},{4,0},{5,1},{6,2},{7,3},{8,12},{9,13},{10,... | collective-permute-start | bytes 884744 | tf_op jit(solution)/shard_map/ppermute | solution.py:118
  436.7 55.3 %collective-permute-start.24 = (bf16[2,2,48,896]{3,2,1,0:T(8,128)(2,1)S(1)}, bf16[2,2,48,896]{3,2,1,0:T(8,128)(2,1)S(1)}, u32[]{:S(2)}, u32[]{:S(2)}) collective-permute-start(bf16[2,2,48,896]{3,2,1,0:T(8,128)(2,1)S(1)} %fusion.87), channel_id=1, source_target_pairs={{0,2},{1,3},{2,0},{3,1},{4,6},{5,7},{6,4},{7,5},{8,10},{9,11},{10,... | collective-permute-start | bytes 1032200 | tf_op jit(solution)/shard_map/ppermute | solution.py:118
  (133 other events, 965.1 us)
Sparse Core Ops, SparseCore 0:
  18.2 116.6 all-gather.2

commit v2 on v1

v2 whole, which is shorter than its diff:
```python
import functools

import jax
import jax.numpy as jnp
from jax import lax
from jax.experimental import pallas as pl
from jax.experimental.pallas import tpu as pltpu
from jax.sharding import PartitionSpec as P

HEAD = 64
CHUNK = 16
PAIR = 2 * HEAD
epsilon = 1e-06
masked_score = -1e30
VMEM_BYTES = 60 << 20


def contract(left, right, left_dim, right_dim):
    return lax.dot_general(
        left, right, (((left_dim,), (right_dim,)), ((), ())), preferred_element_type=jnp.float32
    )


def low(values):
    return values.astype(jnp.bfloat16)


def normalize(values, gain_row):
    return values * lax.rsqrt(jnp.mean(values * values, axis=-1, keepdims=True) + epsilon) * gain_row


def norm_backward(values, gain_row, grad):
    scale = lax.rsqrt(jnp.mean(values * values, axis=-1, keepdims=True) + epsilon)
    grad_gain = jnp.sum(grad * values * scale, axis=0, keepdims=True)
    weighted = gain_row * grad
    inner = jnp.mean(weighted * values, axis=-1, keepdims=True)
    return scale * weighted - values * (scale * scale * scale) * inner, grad_gain


def pair_rows(block):
    lane = lax.broadcasted_iota(jnp.int32, block.shape, 1)
    zero = jnp.zeros_like(block)
    return jnp.concatenate(
        [jnp.where(lane < HEAD, block, zero), jnp.where(lane >= HEAD, block, zero)], axis=0
    )


def pair_lanes(both):
    rows = both.shape[0] // 2
    lane = lax.broadcasted_iota(jnp.int32, (rows, both.shape[1]), 1)
    return jnp.where(lane < HEAD, both[:rows], both[rows:])


def weight_copies(core, sources, kept, sems):
    half = kept.shape[-1]
    copies = []
    for number in range(kept.shape[0]):
        for side, source in enumerate(sources[number // 2]):
            place = core if side == 0 else 1 - core
            copies.append(
                pltpu.make_async_copy(
                    source.at[:, (number % 2) * half : (number % 2 + 1) * half],
                    kept.at[number, place],
                    sems.at[2 * number + side],
                )
            )
    return copies


def times(left, kept, number):
    return jnp.concatenate([contract(left, kept[number, side], 1, 0) for side in range(2)], axis=1)


def times_back(left, kept, number):
    half = kept.shape[-1]
    return contract(left[:, :half], kept[number, 0], 1, 1) + contract(left[:, half:], kept[number, 1], 1, 1)


def grad_into(left, right, held, number):
    half = held.shape[-1]
    for side in range(2):
        held[number, side] = low(contract(left, right[:, side * half : (side + 1) * half], 0, 0))


def grad_copies(core, targets, held, number, sems):
    half = held.shape[-1]
    copies = []
    for side, target in enumerate(targets[number // 2]):
        place = core if side == 0 else 1 - core
        copies.append(
            pltpu.make_async_copy(
                held.at[number, place],
                target.at[:, (number % 2) * half : (number % 2 + 1) * half],
                sems.at[2 * number + side],
            )
        )
    return copies


def self_mask(ids_row):
    tokens = ids_row.shape[1]
    wide = jnp.broadcast_to(ids_row.astype(jnp.float32), (tokens, tokens))
    query = lax.broadcasted_iota(jnp.int32, (tokens, tokens), 0)
    key = lax.broadcasted_iota(jnp.int32, (tokens, tokens), 1)
    allowed = jnp.where((wide == wide.T) & (key <= query), 1.0, 0.0)
    return jnp.concatenate([allowed, allowed], axis=0) > 0.5


def self_probs(queries, keys, allowed):
    scores = jnp.where(allowed, contract(pair_rows(queries), keys, 1, 1) * 0.125, masked_score)
    weights = jnp.exp(scores - jnp.max(scores, axis=-1, keepdims=True))
    return weights / jnp.sum(weights, axis=-1, keepdims=True)


def self_forward_kernel(
    core_ref, ids, tokens, gains, first_mine, first_sibling, second_mine, second_sibling,
    projected, context, after, kept, sems,
):
    core = core_ref[0]
    copies = weight_copies(
        core, ((first_mine, first_sibling), (second_mine, second_sibling)), kept, sems
    )
    for copy in copies:
        copy.start()
    model = tokens.shape[1]
    hidden = tokens[...].astype(jnp.float32)
    normed = low(normalize(hidden, gains[0:1, :]))
    for number in range(3):
        copies[2 * number].wait()
        copies[2 * number + 1].wait()
        projected[number] = low(times(normed, kept, number))
    allowed = self_mask(ids[...])
    for j in range(model // PAIR):
        columns = slice(j * PAIR, (j + 1) * PAIR)
        probs = self_probs(projected[0, :, columns], projected[1, :, columns], allowed)
        context[:, columns] = low(pair_lanes(contract(low(probs), projected[2, :, columns], 1, 0)))
    copies[6].wait()
    copies[7].wait()
    after[...] = hidden + times(context[...], kept, 3)


def self_backward_kernel(
    core_ref, ids, tokens, gains, grad_after, gain_grads, projected, context,
    first_mine, first_sibling, second_mine, second_sibling,
    tokens_grad, first_grad, first_other, second_grad, second_other,
    kept, held, gain_held, sems, out_sems,
):
    core = core_ref[0]
    copies = weight_copies(
        core, ((first_mine, first_sibling), (second_mine, second_sibling)), kept, sems
    )
    for copy in copies:
        copy.start()
    model = tokens.shape[1]
    count = tokens.shape[0]
    hidden = tokens[...].astype(jnp.float32)
    normed = low(normalize(hidden, gains[0:1, :]))
    branch = low(grad_after[...])
    targets = ((first_grad, first_other), (second_grad, second_other))
    started = []

    def send(number):
        for copy in grad_copies(core, targets, held, number, out_sems):
            copy.start()
            started.append(copy)

    grad_into(context[...], branch, held, 3)
    send(3)
    for copy in copies:
        copy.wait()
    grad_context = low(times_back(branch, kept, 3))
    allowed = self_mask(ids[...])
    found = ([], [], [])
    for j in range(model // PAIR):
        columns = slice(j * PAIR, (j + 1) * PAIR)
        queries, keys = projected[0, :, columns], projected[1, :, columns]
        probs = self_probs(queries, keys, allowed)
        pulled = pair_rows(grad_context[:, columns])
        prob_grad = contract(pulled, projected[2, :, columns], 1, 1)
        inner = jnp.sum(probs * prob_grad, axis=-1, keepdims=True)
        score_grad = low(probs * (prob_grad - inner))
        found[0].append(low(pair_lanes(contract(score_grad, keys, 1, 0)) * 0.125))
        found[1].append(low(contract(score_grad, pair_rows(queries), 0, 0) * 0.125))
        found[2].append(low(contract(low(probs), pulled, 0, 0)))
    grad_normed = None
    for number in range(3):
        whole = jnp.concatenate(found[number], axis=1)
        grad_into(normed, whole, held, number)
        send(number)
        part = times_back(whole, kept, number)
        grad_normed = part if grad_normed is None else grad_normed + part
    grad_hidden, grad_gain = norm_backward(hidden, gains[0:1, :], grad_normed)
    tokens_grad[...] = grad_after[...] + grad_hidden
    row = lax.broadcasted_iota(jnp.int32, (count, model), 0)
    others = gain_grads[...]
    wide = jnp.where(
        row == 0, grad_gain, jnp.where(row == 1, others[0:1], jnp.where(row == 2, others[1:2], 0.0))
    )
    gain_held[...] = low(wide.T)
    for slot, target in enumerate((first_grad, first_other)):
        copy = pltpu.make_async_copy(gain_held, target.at[:, model : model + PAIR], out_sems.at[8 + slot])
        copy.start()
        started.append(copy)
    for copy in started:
        copy.wait()


def row_copies(encoded, rows_ref, sems, segs):
    size = encoded.shape[0] // segs
    return [
        pltpu.make_async_copy(
            encoded.at[pl.ds(s * size, size)], rows_ref.at[pl.ds(s * size, size)], sems.at[s]
        )
        for s in range(segs)
    ]


def segment_length(ids, s):
    return lax.fori_loop(
        0, ids.shape[1], lambda at, found: found + (ids[0, at] == s).astype(jnp.int32), 0
    )


def in_segment(token, begin, end, heads):
    row = lax.broadcasted_iota(jnp.int32, (heads, CHUNK, 1), 1) + token
    return (row >= begin) & (row < end)


def pair_weight(kept, number, j):
    per_half = kept.shape[-1] // PAIR
    return kept[number, j // per_half, :, (j % per_half) * PAIR : (j % per_half + 1) * PAIR]


def cross_forward_kernel(
    core_ref, ids, groups, after_self, gains, encoded,
    first_mine, first_sibling, second_mine, second_sibling,
    queries, context, after_cross, probs_out, mixed_out, spread_out,
    rows_ref, kept, sems, weight_sems,
):
    core = core_ref[0]
    heads, tokens, model = spread_out.shape
    segs = groups.shape[1]
    block_rows = encoded.shape[0] // segs
    copies = weight_copies(
        core, ((first_mine, first_sibling), (second_mine, second_sibling)), kept, weight_sems
    )
    for copy in copies[:4]:
        copy.start()
    row_moves = row_copies(encoded, rows_ref, sems, segs)
    for copy in row_moves:
        copy.start()
    for copy in copies[4:]:
        copy.start()
    normed = low(normalize(after_self[...], gains[1:2, :]))
    for copy in copies[:4]:
        copy.wait()
    queries[...] = low(times(normed, kept, 0))
    for j in range(heads // 2):
        block = queries[:, j * PAIR : (j + 1) * PAIR] * jnp.bfloat16(0.125)
        spread = low(contract(pair_rows(block), pair_weight(kept, 1, j), 1, 1))
        spread_out[2 * j] = spread[:tokens]
        spread_out[2 * j + 1] = spread[tokens:]
    for copy in row_moves:
        copy.wait()

    def segment(s, begin):
        end = begin + segment_length(ids, s)
        base = pl.multiple_of(groups[0, s] * block_rows, block_rows)

        def chunk(c, carry):
            token = pl.multiple_of(c * CHUNK, CHUNK)
            rows = rows_ref[pl.ds(base, block_rows), :]
            left = spread_out[:, pl.ds(token, CHUNK), :].reshape(heads * CHUNK, model)
            scores = contract(left, rows, 1, 1)
            weights = jnp.exp(scores - jnp.max(scores, axis=-1, keepdims=True))
            totals = jnp.sum(weights, axis=-1, keepdims=True)
            probs = low(weights * (1.0 / totals))
            mixed = low(contract(probs, rows, 1, 0))
            inside = in_segment(token, begin, end, heads)
            at = (slice(None), pl.ds(token, CHUNK), slice(None))
            probs = probs.reshape(heads, CHUNK, block_rows)
            mixed = mixed.reshape(heads, CHUNK, model)
            probs_out[at] = jnp.where(inside, probs, probs_out[at])
            mixed_out[at] = jnp.where(inside, mixed, mixed_out[at])
            return carry

        lax.fori_loop(begin >> 4, (end + CHUNK - 1) >> 4, chunk, 0)
        return end

    lax.fori_loop(0, segs, segment, 0)
    for copy in copies[4:]:
        copy.wait()
    for j in range(heads // 2):
        both = jnp.concatenate([mixed_out[2 * j], mixed_out[2 * j + 1]], axis=0)
        found = contract(both, pair_weight(kept, 2, j), 1, 0)
        context[:, j * PAIR : (j + 1) * PAIR] = low(pair_lanes(found))
    after_cross[...] = after_self[...] + times(context[...], kept, 3)


def cross_backward_kernel(
    core_ref, ids, groups, grad_after, after_self, gains, ffn_gain_grad, queries, context, encoded,
    probs_ref, mixed, spread, first_mine, first_sibling, second_mine, second_sibling,
    grad_self, gain_grads, grad_rows, first_grad, first_other, second_grad, second_other,
    rows_ref, pulled_ref, moved_ref, sum_ref, kept, held, sems, row_sems, weight_sems, out_sems,
):
    core = core_ref[0]
    heads, tokens, model = spread.shape
    segs = groups.shape[1]
    block_rows = encoded.shape[0] // segs
    half = kept.shape[-1]
    copies = weight_copies(
        core, ((first_mine, first_sibling), (second_mine, second_sibling)), kept, weight_sems
    )
    for copy in copies[4:] + copies[:4]:
        copy.start()
    row_moves = row_copies(encoded, rows_ref, sems, segs)
    for copy in row_moves:
        copy.start()
    targets = ((first_grad, first_other), (second_grad, second_other))
    started = []

    def send(number):
        for copy in grad_copies(core, targets, held, number, out_sems):
            copy.start()
            started.append(copy)

    branch = low(grad_after[...])
    grad_into(context[...], branch, held, 3)
    send(3)
    for copy in copies:
        copy.wait()
    grad_context = low(times_back(branch, kept, 3))
    for j in range(heads // 2):
        block = grad_context[:, j * PAIR : (j + 1) * PAIR]
        pulled = low(contract(pair_rows(block), pair_weight(kept, 2, j), 1, 1))
        pulled_ref[2 * j] = pulled[:tokens]
        pulled_ref[2 * j + 1] = pulled[tokens:]
    for copy in row_moves:
        copy.wait()

    def write_out(s):
        slot = s & 1
        base = pl.multiple_of(groups[0, s] * block_rows, block_rows)
        return pltpu.make_async_copy(
            sum_ref.at[slot], grad_rows.at[pl.ds(base, block_rows)], row_sems.at[slot]
        )

    def segment(s, begin):
        end = begin + segment_length(ids, s)
        base = pl.multiple_of(groups[0, s] * block_rows, block_rows)
        slot = s & 1

        @pl.when(s >= 2)
        def _():
            write_out(s - 2).wait()

        sum_ref[slot] = jnp.zeros((block_rows, model), jnp.float32)

        def chunk(c, carry):
            token = pl.multiple_of(c * CHUNK, CHUNK)
            at = (slice(None), pl.ds(token, CHUNK), slice(None))
            rows = rows_ref[pl.ds(base, block_rows), :]
            inside = in_segment(token, begin, end, heads)
            pulled = jnp.where(inside, pulled_ref[at], jnp.zeros((), jnp.bfloat16))
            pulled = pulled.reshape(heads * CHUNK, model)
            probs = probs_ref[at].reshape(heads * CHUNK, block_rows)
            prob_grad = contract(pulled, rows, 1, 1)
            wide = probs.astype(jnp.float32)
            inner = jnp.sum(wide * prob_grad, axis=-1, keepdims=True)
            score_grad = low(wide * (prob_grad - inner))
            moved = low(contract(score_grad, rows, 1, 0)).reshape(heads, CHUNK, model)
            moved_ref[at] = jnp.where(inside, moved, moved_ref[at])
            left = jnp.concatenate([score_grad, probs], axis=0)
            right = jnp.concatenate([spread[at].reshape(heads * CHUNK, model), pulled], axis=0)
            sum_ref[slot] += contract(left, right, 0, 0)
            return carry

        lax.fori_loop(begin >> 4, (end + CHUNK - 1) >> 4, chunk, 0)
        write_out(s).start()
        return end

    lax.fori_loop(0, segs, segment, 0)
    found = []
    per_half = half // PAIR
    for j in range(heads // 2):
        columns = slice((j % per_half) * PAIR, (j % per_half + 1) * PAIR)
        both = jnp.concatenate([moved_ref[2 * j], moved_ref[2 * j + 1]], axis=0)
        found.append(low(pair_lanes(contract(both, pair_weight(kept, 1, j), 1, 0)) * 0.125))
        block = queries[:, j * PAIR : (j + 1) * PAIR] * jnp.bfloat16(0.125)
        held[1, j // per_half, :, columns] = low(contract(both, pair_rows(block), 0, 0))
    send(1)
    for j in range(heads // 2):
        columns = slice((j % per_half) * PAIR, (j % per_half + 1) * PAIR)
        block = grad_context[:, j * PAIR : (j + 1) * PAIR]
        both = jnp.concatenate([mixed[2 * j], mixed[2 * j + 1]], axis=0)
        held[2, j // per_half, :, columns] = low(contract(both, pair_rows(block), 0, 0))
    send(2)
    grad_queries = jnp.concatenate(found, axis=1)
    values = after_self[...]
    grad_into(low(normalize(values, gains[1:2, :])), grad_queries, held, 0)
    send(0)
    grad_values, grad_gain = norm_backward(values, gains[1:2, :], times_back(grad_queries, kept, 0))
    grad_self[...] = grad_after[...] + grad_values
    gain_grads[0:1, :] = grad_gain
    gain_grads[1:2, :] = ffn_gain_grad[0:1, :]
    for copy in started:
        copy.wait()
    for s in range(segs - 2, segs):
        write_out(s).wait()


def gelu_both(values):
    scale = 0.7978845608028654
    square = values * values
    bend = jnp.tanh(scale * (values + 0.044715 * (square * values)))
    half = 0.5 * (1.0 + bend)
    slope = half + 0.5 * values * (1.0 - bend * bend) * (scale * (1.0 + 3.0 * 0.044715 * square))
    return values * half, slope


def ffn_kernel(
    direct,
    core_ref, after_cross, gains, cotangent, weight_in, gathered,
    block_out, grad_after, gain_grad, in_mine, in_other, down_mine, down_other,
    kept_in, kept_down, held_in, held_down, sems, out_sems,
):
    core = core_ref[0]
    blocks, model, width = weight_in.shape
    per_block, rows_down = kept_down.shape[1:3]
    copies = []
    for j in range(blocks):
        copies.append(pltpu.make_async_copy(weight_in.at[j], kept_in.at[j], sems.at[2 * j]))
        copies.append(
            pltpu.make_async_copy(
                gathered.at[pl.ds(j * per_block, per_block), pl.ds(gathered.shape[1] - rows_down, rows_down)]
                if direct
                else gathered.at[j],
                kept_down.at[j],
                sems.at[2 * j + 1],
            )
        )
    for copy in copies:
        copy.start()
    values = after_cross[...]
    normed = low(normalize(values, gains[2:3, :]))
    pull = cotangent[...]
    total = values
    grad_normed = jnp.zeros(values.shape, jnp.float32)
    chips = per_block // 2
    started = []
    for j in range(blocks):
        copies[2 * j].wait()
        copies[2 * j + 1].wait()
        weight_up = kept_in[j]
        weight_down = kept_down[j].reshape(width, model)
        activated, slope = gelu_both(contract(normed, weight_up, 1, 0))
        activated = low(activated)
        total = total + contract(activated, weight_down, 1, 0)
        grad_act = low(contract(pull, weight_down, 1, 1)).astype(jnp.float32)
        grad_pre = low(slope * grad_act)
        grad_normed = grad_normed + contract(grad_pre, weight_up, 1, 1)
        held_in[j] = low(contract(normed, grad_pre, 0, 0))
        grad_down = low(contract(activated, pull, 0, 0))
        if direct:
            for k in range(per_block):
                at = (j * chips + k // 2) * rows_down
                held_down[k % 2, at : at + rows_down] = grad_down[k * rows_down : (k + 1) * rows_down]
        else:
            held_down[j // 2, (j % 2) * width : (j % 2 + 1) * width] = grad_down
    half = blocks // 2
    for side, target in enumerate((in_mine, in_other)):
        place = core if side == 0 else 1 - core
        for j in range(half):
            copy = pltpu.make_async_copy(
                held_in.at[place * half + j],
                target.at[:, j * width : (j + 1) * width],
                out_sems.at[side * half + j],
            )
            copy.start()
            started.append(copy)
    for side, target in enumerate((down_mine, down_other)):
        place = (core if side == 0 else 1 - core) if direct else side
        copy = pltpu.make_async_copy(held_down.at[place], target, out_sems.at[2 * half + side])
        copy.start()
        started.append(copy)
    block_out[...] = low(total)
    grad_values, grad_gain = norm_backward(values, gains[2:3, :], grad_normed)
    grad_after[...] = pull.astype(jnp.float32) + grad_values
    gain_grad[0:1, :] = grad_gain
    for copy in started:
        copy.wait()

AXES = ("dp", "fsdp")


def swap_with(piece, mask, devices):
    pairs = [(index, index ^ mask) for index in range(devices)]
    return lax.ppermute(piece, AXES, pairs)


def bit_of(me, bit):
    return (me >> bit) & 1


def pair_up(mine, theirs, my_bit, axis):
    first = jnp.where(my_bit == 0, mine, theirs)
    second = jnp.where(my_bit == 0, theirs, mine)
    return jnp.stack([first, second], axis=axis)


def gather_bits(block, order, me, devices):
    held = block
    done = []
    for bit in order:
        theirs = swap_with(held, 1 << bit, devices)
        place = sum(1 for other in done if other > bit)
        held = pair_up(held, theirs, bit_of(me, bit), place)
        done.append(bit)
    return held.reshape(-1, block.shape[-1])


def core_sum(mine, other, devices):
    theirs = swap_with(other, 1, devices)
    return low(mine.astype(jnp.float32) + theirs.astype(jnp.float32))


def scatter_bits(partial, order, me, devices):
    rows = partial.shape[0] >> len(order)
    held = partial.reshape((2,) * len(order) + (rows, partial.shape[-1]))
    left = sorted(order, reverse=True)
    for bit in order:
        place = left.index(bit)
        mine = lax.dynamic_index_in_dim(held, bit_of(me, bit), place, keepdims=False)
        other = lax.dynamic_index_in_dim(held, 1 - bit_of(me, bit), place, keepdims=False)
        theirs = swap_with(low(other), 1 << bit, devices)
        held = mine.astype(jnp.float32) + theirs.astype(jnp.float32)
        left.remove(bit)
    return held


def core_rows(total, core, devices):
    rows = total.shape[0] // 2
    keep = lax.dynamic_slice_in_dim(total, core * rows, rows, axis=0)
    send = lax.dynamic_slice_in_dim(total, (1 - core) * rows, rows, axis=0)
    theirs = swap_with(send, 1, devices)
    return jnp.where(core == 0, keep, theirs), jnp.where(core == 0, theirs, keep)


VMEM = pl.BlockSpec(memory_space=pltpu.VMEM)
SMEM = pl.BlockSpec(memory_space=pltpu.SMEM)
HBM = pl.BlockSpec(memory_space=pl.ANY)


def shaped(shape, dtype):
    return jax.ShapeDtypeStruct(shape, dtype)


def call(kernel, name, flops, in_specs, out_specs, out_shape, scratch):
    return pl.pallas_call(
        kernel,
        out_shape=out_shape,
        in_specs=in_specs,
        out_specs=out_specs,
        scratch_shapes=scratch,
        compiler_params=pltpu.CompilerParams(vmem_limit_bytes=VMEM_BYTES),
        cost_estimate=pl.CostEstimate(flops=flops, bytes_accessed=10_000_000, transcendentals=0),
        name=name,
    )


def per_device(
    fsdp,
    devices,
    tokens,
    encoded,
    segment_ids,
    passage_group,
    cotangent,
    self_gain,
    cross_gain,
    ffn_gain,
    self_query,
    self_key,
    self_value,
    self_out,
    cross_query,
    cross_key,
    cross_value,
    cross_out,
    ffn_in,
    ffn_out,
):
    me = lax.axis_index("dp") * fsdp + lax.axis_index("fsdp")
    core = bit_of(me, 0)
    core_word = core.reshape(1).astype(jnp.int32)
    chip_bits = list(range(1, devices.bit_length() - 1))
    line_bits = [bit for bit in reversed(chip_bits) if bit > 2]
    forward_orders = (line_bits + [2, 1], line_bits + [1, 2])
    backward_orders = ([2, 1] + line_bits[::-1], [1, 2] + line_bits[::-1])
    count, model = tokens.shape
    encoder_count = encoded.shape[0]
    hidden_units = ffn_in.shape[1]
    heads = model // HEAD
    half = model // 2
    segs = passage_group.shape[1]
    low_type, wide_type = jnp.bfloat16, jnp.float32

    def my_columns(matrix, owner):
        width = matrix.shape[-1] // 2
        return lax.dynamic_slice_in_dim(matrix, owner * width, width, axis=matrix.ndim - 1)

    def gather_group(shards, extra):
        first, second = shards[:2], shards[2:]

        def chip_block(pair, also):
            send = jnp.concatenate([my_columns(shard, 1 - core) for shard in pair] + also, axis=1)
            keep = jnp.concatenate([my_columns(shard, core) for shard in pair] + also, axis=1)
            theirs = swap_with(send, 1, devices)
            return pair_up(keep, theirs, core, 0).reshape(-1, keep.shape[1])

        wholes = []
        for pair, also, order in zip((first, second), (extra, []), forward_orders):
            mine = gather_bits(chip_block(pair, also), order, me, devices)
            wholes.append((mine, swap_with(mine[:, :model], 1, devices)))
        return wholes

    gains = jnp.stack([self_gain, cross_gain, ffn_gain], axis=1)
    gains = jnp.pad(gains, ((0, 0), (0, PAIR - 3)))
    self_weights = gather_group([self_query, self_key, self_value, self_out], [gains])
    cross_weights = gather_group([cross_query, cross_key, cross_value, cross_out], [])
    gain_rows = jnp.pad(self_weights[0][0][:, model : model + 8].T.astype(wide_type), ((0, 0), (0, 0)))
    self_flat = self_weights[0] + self_weights[1]
    cross_flat = cross_weights[0] + cross_weights[1]

    blocks = hidden_units // model
    rows_in = ffn_in.shape[0]
    rows_down = ffn_out.shape[0]
    ffn_shard = jnp.concatenate(
        [ffn_in[:, n * model : (n + 1) * model] for n in range(blocks)] + [ffn_out], axis=0
    )
    gathered = lax.all_gather(ffn_shard, AXES, axis=0)
    weight_in = jnp.stack(
        [gathered[:, n * rows_in : (n + 1) * rows_in].reshape(model, model) for n in range(blocks)]
    )
    direct = rows_down % 16 == 0
    down_shape = (devices // blocks, rows_down) if direct else (1, model)
    down_source = gathered if direct else gathered[:, blocks * rows_in :].reshape(blocks, 1, model, model)

    dma = pltpu.SemaphoreType.DMA
    weights_kept = pltpu.VMEM((4, 2, model, half), low_type)
    projected, context_one, after_self = call(
        self_forward_kernel,
        "self_forward",
        2 * count * model * model * 5,
        [SMEM, VMEM, VMEM, VMEM] + [HBM] * 4,
        [VMEM] * 3,
        (
            shaped((3, count, model), low_type),
            shaped((count, model), low_type),
            shaped((count, model), wide_type),
        ),
        [weights_kept, dma((8,))],
    )(core_word, segment_ids, tokens, gain_rows, *self_flat)

    per_token = (heads, count, model)
    probs_shape = (heads, count, encoder_count // segs)
    queries_two, context_two, after_cross, probs, mixed, spread = call(
        cross_forward_kernel,
        "cross_forward",
        12_000_000_000,
        [SMEM, SMEM, SMEM, VMEM, VMEM] + [HBM] * 5,
        [VMEM] * 6,
        (
            shaped((count, model), low_type),
            shaped((count, model), low_type),
            shaped((count, model), wide_type),
            shaped(probs_shape, low_type),
            shaped(per_token, low_type),
            shaped(per_token, low_type),
        ),
        [pltpu.VMEM(encoded.shape, low_type), weights_kept, dma((segs,)), dma((8,))],
    )(core_word, segment_ids, passage_group, after_self, gain_rows, encoded, *cross_flat)

    (block_out, grad_after_cross, ffn_gain_grad, in_mine, in_other, down_mine, down_other) = call(
        functools.partial(ffn_kernel, direct),
        "ffn",
        2 * count * model * hidden_units * 6,
        [SMEM, VMEM, VMEM, VMEM, HBM, HBM],
        [VMEM] * 3 + [HBM] * 4,
        (
            shaped((count, model), low_type),
            shaped((count, model), wide_type),
            shaped((8, model), wide_type),
            shaped((model, hidden_units // 2), low_type),
            shaped((model, hidden_units // 2), low_type),
            shaped((hidden_units // 2, model), low_type),
            shaped((hidden_units // 2, model), low_type),
        ),
        [
            pltpu.VMEM((blocks, model, model), low_type),
            pltpu.VMEM((blocks,) + down_shape + (model,), low_type),
            pltpu.VMEM((blocks, model, model), low_type),
            pltpu.VMEM((2, hidden_units // 2, model), low_type),
            dma((2 * blocks,)),
            dma((blocks + 2,)),
        ],
    )(core_word, after_cross, gain_rows, cotangent, weight_in, down_source)

    if not direct:
        whole = jnp.concatenate([down_mine, down_other], axis=0).reshape(devices // 2, 2, rows_down, model)
        down_mine, down_other = (
            lax.dynamic_index_in_dim(whole, place, 1, keepdims=False).reshape(-1, model) for place in (core, 1 - core)
        )
    summed_down = scatter_bits(core_sum(down_mine, down_other, devices), backward_orders[0], me, devices)
    in_chip = scatter_bits(core_sum(in_mine, in_other, devices), backward_orders[1], me, devices)
    summed_in = jnp.concatenate(core_rows(in_chip, core, devices), axis=1)

    grad_shapes = tuple(shaped((model, model), low_type) for n in range(4))
    (grad_after_self, gain_grads, encoded_grad, *cross_grads) = call(
        cross_backward_kernel,
        "cross_backward",
        25_000_000_000,
        [SMEM, SMEM, SMEM] + [VMEM] * 6 + [HBM] + [VMEM] * 3 + [HBM] * 4,
        [VMEM] * 2 + [HBM] * 5,
        (
            shaped((count, model), wide_type),
            shaped((8, model), wide_type),
            shaped(encoded.shape, wide_type),
        )
        + grad_shapes,
        [
            pltpu.VMEM(encoded.shape, low_type),
            pltpu.VMEM(per_token, low_type),
            pltpu.VMEM(per_token, low_type),
            pltpu.VMEM((2, encoder_count // segs, model), wide_type),
            weights_kept,
            weights_kept,
            dma((segs,)),
            dma((2,)),
            dma((8,)),
            dma((8,)),
        ],
    )(
        core_word, segment_ids, passage_group, grad_after_cross, after_self, gain_rows, ffn_gain_grad,
        queries_two, context_two, encoded, probs, mixed, spread, *cross_flat,
    )

    def reduce_group(grads):
        answers = []
        for side, order in enumerate(backward_orders):
            mine, other = grads[2 * side], grads[2 * side + 1]
            total = scatter_bits(core_sum(mine, other, devices), order, me, devices)
            pair = core_rows(total, core, devices)
            answers += [
                jnp.concatenate([piece[:, n * half : (n + 1) * half] for piece in pair], axis=1) for n in range(2)
            ]
            if mine.shape[1] > model:
                answers.append(jnp.where(core == 0, pair[0][:, model:], pair[1][:, model:]))
        return answers

    summed_cq, summed_ck, summed_cv, summed_co = reduce_group(cross_grads)

    with_gains = shaped((model, model + PAIR), low_type)
    (tokens_grad, *self_grads) = call(
        self_backward_kernel,
        "self_backward",
        2 * count * model * model * 10,
        [SMEM] + [VMEM] * 7 + [HBM] * 4,
        [VMEM] + [HBM] * 4,
        (shaped((count, model), wide_type), with_gains, with_gains, grad_shapes[0], grad_shapes[0]),
        [weights_kept, weights_kept, pltpu.VMEM((model, PAIR), low_type), dma((8,)), dma((10,))],
    )(
        core_word, segment_ids, tokens, gain_rows, grad_after_self, gain_grads, projected, context_one,
        *self_flat,
    )
    summed_query, summed_key, own_gains, summed_value, summed_out = reduce_group(self_grads)
    return (
        block_out,
        tokens_grad,
        encoded_grad,
        own_gains[:, 0],
        own_gains[:, 1],
        own_gains[:, 2],
        summed_query,
        summed_key,
        summed_value,
        summed_out,
        summed_cq,
        summed_ck,
        summed_cv,
        summed_co,
        summed_in,
        summed_down,
    )


def solution(mesh):
    return jax.shard_map(
        functools.partial(per_device, mesh.shape["fsdp"], mesh.size),
        mesh=mesh,
        in_specs=(
            P(("dp", "fsdp"), None),
            P(("dp", "fsdp"), None),
            P(("dp", "fsdp"), None),
            P(("dp", "fsdp"), None),
            P(("dp", "fsdp"), None),
            P(("dp", "fsdp")),
            P(("dp", "fsdp")),
            P(("dp", "fsdp")),
            P(("dp", "fsdp"), None),
            P(("dp", "fsdp"), None),
            P(("dp", "fsdp"), None),
            P(("dp", "fsdp"), None),
            P(("dp", "fsdp"), None),
            P(("dp", "fsdp"), None),
            P(("dp", "fsdp"), None),
            P(("dp", "fsdp"), None),
            P(("dp", "fsdp"), None),
            P(("dp", "fsdp"), None),
        ),
        out_specs=(
            P(("dp", "fsdp"), None),
            P(("dp", "fsdp"), None),
            P(("dp", "fsdp"), None),
            P(("dp", "fsdp")),
            P(("dp", "fsdp")),
            P(("dp", "fsdp")),
            P(("dp", "fsdp"), None),
            P(("dp", "fsdp"), None),
            P(("dp", "fsdp"), None),
            P(("dp", "fsdp"), None),
            P(("dp", "fsdp"), None),
            P(("dp", "fsdp"), None),
            P(("dp", "fsdp"), None),
            P(("dp", "fsdp"), None),
            P(("dp", "fsdp"), None),
            P(("dp", "fsdp"), None),
        ),
        check_vma=False,
    )
```

time: 523 us -> 382 us (0.73)
  matrix products: 154 us -> 0 us
  Pallas kernels: 0 us -> 98.8 us
  other arithmetic: 68.2 us -> 19.3 us
  local copies, waits for them, and re-layouts: 61.8 us -> 18.8 us
  waiting for transfers between devices: 134 us -> 155 us
  starting transfers between devices: 81.5 us -> 67.7 us
    dot_general x52 -> x0, matrix products: 154 us -> none  [the longest x10 30.3 us: product_right(): jnp.einsum('td,id->ti', left_side, right_side, preferred_element_type=jnp...]
    pallas_call x0 -> x5, Pallas kernels: none -> 98.8 us  [the longest x1 40 us: per_device(): call(cross_backward_kernel, 'cross_backward', 25000000000, [SMEM, SMEM, S...]
    ppermute x69 -> x59, waiting for transfers between devices: 134 us -> 155 us  [swap_with(): return lax.ppermute(piece, AXES, pairs)]
    convert_element_type x7, other arithmetic: 23.4 us -> 6.32 us  [the longest x6 6.29 us: low(): return values.astype(jnp.bfloat16)]
    ppermute x69 -> x59, starting transfers between devices: 81.5 us -> 67.7 us  [swap_with(): return lax.ppermute(piece, AXES, pairs)]
    convert_element_type x38 -> x19, local copies, waits for them, and re-layouts: 13.5 us -> 1.36 us  [the longest x1 0.74 us: per_device(): self_weights[0][0][:, model:model + 8].T.astype(wide_type)]
    slice x25 -> x10, local copies, waits for them, and re-layouts: 15.9 us -> 3.87 us  [the longest x1 2.66 us: per_device(): gathered[:, n * rows_in:(n + 1) * rows_in].reshape(model, model)]
    unnamed x199 -> x39, local copies, waits for them, and re-layouts: 18.2 us -> 6.89 us
  transfers between devices with their start and end apart: 70 -> 60, of which waited for: 31 -> 31; matrix products, arithmetic and copies ran while one was open for 26% -> 7% of each run, Pallas kernels for 0% -> 12%
where the time goes in v2:
time: 382 us; the launch traced here: 376 us
  waiting for transfers between devices  155 us (41%)
  Pallas kernels  98.8 us (26%)
  starting transfers between devices  67.7 us (18%)
  other arithmetic  19.3 us (5%)
  local copies, waits for them, and re-layouts  18.8 us (5%)
  between operations  15.7 us (4%)
    ppermute x59, waiting for transfers between devices, swap_with(): return lax.ppermute(piece, AXES, pairs)  155 us
    ppermute x59, starting transfers between devices, swap_with(): return lax.ppermute(piece, AXES, pairs)  67.7 us
    pallas_call x1, Pallas kernels, per_device(): call(cross_backward_kernel, 'cross_backward', 25000000000, [SMEM, SMEM, S...  40 us
    pallas_call x1, Pallas kernels, per_device(): call(cross_forward_kernel, 'cross_forward', 12000000000, [SMEM, SMEM, SME...  27.6 us
    pallas_call x1, Pallas kernels, per_device(): call(functools.partial(ffn_kernel, direct), 'ffn', 2 * count * model * hi...  14.6 us
    pallas_call x1, Pallas kernels, per_device(): call(self_backward_kernel, 'self_backward', 2 * count * model * model * 1...  11.3 us
  transfers between devices with their start and end apart: 60, of which 31 were waited for; matrix products, arithmetic and copies ran while one was open for 7% of the time, Pallas kernels for 12%

profile of v2, /device:TPU:0, one launch (start us, length us, event | category | flops | bytes accessed | tf_op | source)
XLA Modules:
  0.0 375.7 jit_solution(18060396324898737824)
XLA Ops:
  15.2 4.1 %collective-permute-start.19 = (bf16[48,768]{1,0:T(8,128)(2,1)S(1)}, bf16[48,768]{1,0:T(8,128)(2,1)S(1)}, u32[]{:S(2)}, u32[]{:S(2)}) collective-permute-start(bf16[48,768]{1,0:T(8,128)(2,1)S(1)} %bitcast.279), channel_id=1, source_target_pairs={{0,16},{1,17},{2,18},{3,19},{4,20},{5,21},{6,22},{7,23},{8,24},{9,... | collective-permute-start | bytes 221192 | tf_op jit(solution)/shard_map/ppermute | solution.py:498
  19.5 3.0 collective-permute-start.7
  23.7 8.6 %collective-permute-start.20 = (bf16[2,48,768]{2,1,0:T(8,128)(2,1)S(1)}, bf16[2,48,768]{2,1,0:T(8,128)(2,1)S(1)}, u32[]{:S(2)}, u32[]{:S(2)}) collective-permute-start(bf16[2,48,768]{2,1,0:T(8,128)(2,1)S(1)} %pad_maximum_fusion.17), channel_id=1, source_target_pairs={{0,8},{1,9},{2,10},{3,11},{4,12},{5,13},{6,14},{7,15},{8,0},{9,1},... | collective-permute-start | bytes 442376 | tf_op jit(solution)/shard_map/ppermute | solution.py:498
  40.5 2.3 collective-permute-done.20
  50.9 7.8 %collective-permute-done.2 = bf16[2,48,896]{2,1,0:T(8,128)(2,1)S(1)} collective-permute-done((bf16[2,48,896]{2,1,0:T(8,128)(2,1)S(1)}, bf16[2,48,896]{2,1,0:T(8,128)(2,1)S(1)}, u32[]{:S(2)}, u32[]{:S(2)}) %collective-permute-start.2) | collective-permute-done | bytes 172064 | tf_op jit(solution)/shard_map/ppermute | solution.py:498
  65.2 5.9 %collective-permute-done.3 = bf16[2,2,48,896]{3,2,1,0:T(8,128)(2,1)S(1)} collective-permute-done((bf16[2,2,48,896]{3,2,1,0:T(8,128)(2,1)S(1)}, bf16[2,2,48,896]{3,2,1,0:T(8,128)(2,1)S(1)}, u32[]{:S(2)}, u32[]{:S(2)}) %collective-permute-start.3) | collective-permute-done | bytes 344096 | tf_op jit(solution)/shard_map/ppermute | solution.py:498
  73.0 15.2 %collective-permute-done.22 = bf16[2,2,2,48,768]{4,3,2,1,0:T(8,128)(2,1)S(1)} collective-permute-done((bf16[2,2,2,48,768]{4,3,2,1,0:T(8,128)(2,1)S(1)}, bf16[2,2,2,48,768]{4,3,2,1,0:T(8,128)(2,1)S(1)}, u32[]{:S(2)}, u32[]{:S(2)}) %collective-permute-start.22) | collective-permute-done | bytes 589856 | tf_op jit(solution)/shard_map/ppermute | solution.py:498
  89.6 23.3 %collective-permute-done.10 = bf16[2,2,2,48,768]{4,3,2,1,0:T(8,128)(2,1)S(1)} collective-permute-done((bf16[2,2,2,48,768]{4,3,2,1,0:T(8,128)(2,1)S(1)}, bf16[2,2,2,48,768]{4,3,2,1,0:T(8,128)(2,1)S(1)}, u32[]{:S(2)}, u32[]{:S(2)}) %collective-permute-start.10) | collective-permute-done | bytes 589856 | tf_op jit(solution)/shard_map/ppermute | solution.py:498
  118.8 5.3 %self_forward.1 = (bf16[3,128,768]{2,1,0:T(8,128)(2,1)}, bf16[128,768]{1,0:T(8,128)(2,1)}, f32[128,768]{1,0:T(8,128)}) custom-call(s32[1]{0:T(128)} %bitcast.core_ref, s32[1,128]{1,0:T(1,128)} %ids.7, bf16[128,768]{1,0:T(8,128)(2,1)} %tokens.3, f32[8,768]{1,0:T(8,128)} %copy.74.gains, bf16[768,896]{1,0:T(8,128)(2,1)} %bitcast.255, ...), custom_call_target="tpu_custom_call" | custom-call | flops 754974720 | bytes 10000000 | tf_op jit(solution)/shard_map/self_forward/pallas_call | solution.py:651
  125.2 27.6 %cross_forward.1 = (bf16[128,768]{1,0:T(8,128)(2,1)}, bf16[128,768]{1,0:T(8,128)(2,1)}, f32[128,768]{1,0:T(8,128)}, bf16[12,128,1024]{2,1,0:T(8,128)(2,1)}, bf16...) custom-call(s32[1]{0:T(128)} %bitcast.core_ref, s32[1,128]{1,0:T(1,128)} %ids.7, s32[1,4]{1,0:T(1,128)} %groups.3, ...), custom_call_target="tpu_custom_call" | custom-call | flops 12000000000 | bytes 10000000 | tf_op jit(solution)/shard_map/cross_forward/pallas_call | solution.py:667
  152.8 2.7 fusion.21
  155.4 2.5 pad_maximum_fusion.weight_in
  157.9 14.6 %ffn.1 = (bf16[128,768]{1,0:T(8,128)(2,1)}, f32[128,768]{1,0:T(8,128)}, f32[8,768]{1,0:T(8,128)}, bf16[768,1536]{1,0:T(8,128)(2,1)}, bf16[768,1536]{1,0:T(8,128)...) custom-call(s32[1]{0:T(128)} %bitcast.core_ref, f32[128,768]{1,0:T(8,128)} %get-tuple-element.45.after_cross, ...), custom_call_target="tpu_custom_call" | custom-call | flops 3623878656 | bytes 10000000 | tf_op jit(solution)/shard_map/ffn/pallas_call | solution.py:684
  172.6 40.0 %cross_backward.1 = (f32[128,768]{1,0:T(8,128)}, f32[8,768]{1,0:T(8,128)}, f32[4096,768]{1,0:T(8,128)}, bf16[768,768]{1,0:T(8,128)(2,1)}, bf16[768,768]{1,0:T(8,...) custom-call(s32[1]{0:T(128)} %bitcast.core_ref, s32[1,128]{1,0:T(1,128)} %ids.7, s32[1,4]{1,0:T(1,128)} %groups.3, ...), custom_call_target="tpu_custom_call" | custom-call | flops 24999999488 | bytes 10000000 | tf_op jit(solution)/shard_map/cross_backward/pallas_call | solution.py:719
  213.1 11.3 %self_backward.1 = (f32[128,768]{1,0:T(8,128)}, bf16[768,896]{1,0:T(8,128)(2,1)}, bf16[768,896]{1,0:T(8,128)(2,1)}, bf16[768,768]{1,0:T(8,128)(2,1)}, bf16[768,768]{1,0:T(8,128)(2,1)}) custom-call(s32[1]{0:T(128)} %bitcast.core_ref, s32[1,128]{1,0:T(1,128)} %ids.7, bf16[128,768]{1,0:T(8,128)(2,1)} %tokens.3, f32[8,768]{1,0:T(8,128)} %copy.74.gains, ...), custom_call_target="tpu_custom_call" | custom-call | flops 1509949440 | bytes 10000000 | tf_op jit(solution)/shard_map/self_backward/pallas_call | solution.py:764
  235.8 7.7 %collective-permute-done.43 = bf16[2,2,2,48,768]{4,3,0,1,2:T(8,128)(2,1)S(1)} collective-permute-done((bf16[2,2,2,48,768]{4,3,0,1,2:T(8,128)(2,1)S(1)}, bf16[2,2,2,48,768]{4,3,0,1,2:T(8,128)(2,1)S(1)}, u32[]{:S(2)}, u32[]{:S(2)}) %collective-permute-start.43) | collective-permute-done | bytes 589856 | tf_op jit(solution)/shard_map/ppermute | solution.py:498
  248.6 6.7 %collective-permute-done.31 = bf16[2,2,2,48,768]{4,3,0,1,2:T(8,128)(2,1)S(1)} collective-permute-done((bf16[2,2,2,48,768]{4,3,0,1,2:T(8,128)(2,1)S(1)}, bf16[2,2,2,48,768]{4,3,0,1,2:T(8,128)(2,1)S(1)}, u32[]{:S(2)}, u32[]{:S(2)}) %collective-permute-start.31) | collective-permute-done | bytes 589856 | tf_op jit(solution)/shard_map/ppermute | solution.py:498
  257.1 9.8 %collective-permute-done.44 = bf16[2,2,48,768]{3,2,0,1:T(8,128)(2,1)S(1)} collective-permute-done((bf16[2,2,48,768]{3,2,0,1:T(8,128)(2,1)S(1)}, bf16[2,2,48,768]{3,2,0,1:T(8,128)(2,1)S(1)}, u32[]{:S(2)}, u32[]{:S(2)}) %collective-permute-start.44) | collective-permute-done | bytes 294944 | tf_op jit(solution)/shard_map/ppermute | solution.py:498
  268.7 6.0 %collective-permute-done.32 = bf16[2,2,48,768]{3,2,0,1:T(8,128)(2,1)S(1)} collective-permute-done((bf16[2,2,48,768]{3,2,0,1:T(8,128)(2,1)S(1)}, bf16[2,2,48,768]{3,2,0,1:T(8,128)(2,1)S(1)}, u32[]{:S(2)}, u32[]{:S(2)}) %collective-permute-start.32) | collective-permute-done | bytes 294944 | tf_op jit(solution)/shard_map/ppermute | solution.py:498
  279.8 3.9 %collective-permute-start.46 = (bf16[48,768]{1,0:T(8,128)(2,1)S(1)}, bf16[48,768]{1,0:T(8,128)(2,1)S(1)}, u32[]{:S(2)}, u32[]{:S(2)}) collective-permute-start(bf16[48,768]{1,0:T(8,128)(2,1)S(1)} %fusion.18), channel_id=1, source_target_pairs={{0,16},{1,17},{2,18},{3,19},{4,20},{5,21},{6,22},{7,23},{8,24},{9,... | collective-permute-start | bytes 221192 | tf_op jit(solution)/shard_map/ppermute | solution.py:498
  283.8 2.2 collective-permute-start.40
  286.1 2.4 collective-permute-done.46
  290.4 4.2 %collective-permute-done.34 = bf16[48,768]{1,0:T(8,128)(2,1)S(1)} collective-permute-done((bf16[48,768]{1,0:T(8,128)(2,1)S(1)}, bf16[48,768]{1,0:T(8,128)(2,1)S(1)}, u32[]{:S(2)}, u32[]{:S(2)}) %collective-permute-start.34) | collective-permute-done | bytes 73760 | tf_op jit(solution)/shard_map/ppermute | solution.py:498
  303.5 4.9 %collective-permute-done.27 = bf16[2,48,896]{2,1,0:T(8,128)(2,1)S(1)} collective-permute-done((bf16[2,48,896]{2,1,0:T(8,128)(2,1)S(1)}, bf16[2,48,896]{2,1,0:T(8,128)(2,1)S(1)}, u32[]{:S(2)}, u32[]{:S(2)}) %collective-permute-start.27) | collective-permute-done | bytes 172064 | tf_op jit(solution)/shard_map/ppermute | solution.py:498
  308.5 2.4 collective-permute-start.28
  311.5 3.4 collective-permute-done.28
  317.0 9.8 %collective-permute-done.49 = bf16[2,2,2,48,1536]{4,3,0,1,2:T(8,128)(2,1)S(1)} collective-permute-done((bf16[2,2,2,48,1536]{4,3,0,1,2:T(8,128)(2,1)S(1)}, bf16[2,2,2,48,1536]{4,3,0,1,2:T(8,128)(2,1)S(1)}, u32[]{:S(2)}, u32[]{:S(2)}) %collective-permute-start.49) | collective-permute-done | bytes 1179680 | tf_op jit(solution)/shard_map/ppermute | solution.py:498
  331.4 10.2 %collective-permute-done.50 = bf16[2,2,48,1536]{3,2,0,1:T(8,128)(2,1)S(1)} collective-permute-done((bf16[2,2,48,1536]{3,2,0,1:T(8,128)(2,1)S(1)}, bf16[2,2,48,1536]{3,2,0,1:T(8,128)(2,1)S(1)}, u32[]{:S(2)}, u32[]{:S(2)}) %collective-permute-start.50) | collective-permute-done | bytes 589856 | tf_op jit(solution)/shard_map/ppermute | solution.py:498
  341.9 2.1 collective-permute-done.56
  345.1 8.3 %collective-permute-done.51 = bf16[2,48,1536]{2,1,0:T(8,128)(2,1)S(1)} collective-permute-done((bf16[2,48,1536]{2,1,0:T(8,128)(2,1)S(1)}, bf16[2,48,1536]{2,1,0:T(8,128)(2,1)S(1)}, u32[]{:S(2)}, u32[]{:S(2)}) %collective-permute-start.51) | collective-permute-done | bytes 294944 | tf_op jit(solution)/shard_map/ppermute | solution.py:498
  354.0 3.0 collective-permute-done.57
  358.1 7.2 %collective-permute-done.52 = bf16[48,1536]{1,0:T(8,128)(2,1)S(1)} collective-permute-done((bf16[48,1536]{1,0:T(8,128)(2,1)S(1)}, bf16[48,1536]{1,0:T(8,128)(2,1)S(1)}, u32[]{:S(2)}, u32[]{:S(2)}) %collective-permute-start.52) | collective-permute-done | bytes 147488 | tf_op jit(solution)/shard_map/ppermute | solution.py:498
  (279 shorter events, 91.8 us)
Async XLA Ops:
  7.3 145.5 %all-gather.3.cloned.1.call-start = ((), (), s32[]{:S(2)}) async-start(), calls=%async_computation | async-start | bytes 9732096 | tf_op jit(solution)/shard_map/all_gather | solution.py:641
  19.4 14.2 %collective-permute-start.13 = (bf16[48,768]{1,0:T(8,128)(2,1)S(1)}, bf16[48,768]{1,0:T(8,128)(2,1)S(1)}, u32[]{:S(2)}, u32[]{:S(2)}) collective-permute-start(bf16[48,768]{1,0:T(8,128)(2,1)S(1)} %bitcast.280), channel_id=1, source_target_pairs={{0,16},{1,17},{2,18},{3,19},{4,20},{5,21},{6,22},{7,23},{8,24},{9,... | collective-permute-start | bytes 221192 | tf_op jit(solution)/shard_map/ppermute | solution.py:498
  19.5 17.6 %collective-permute-start.7 = (bf16[48,768]{1,0:T(8,128)(2,1)S(1)}, bf16[48,768]{1,0:T(8,128)(2,1)S(1)}, u32[]{:S(2)}, u32[]{:S(2)}) collective-permute-start(bf16[48,768]{1,0:T(8,128)(2,1)S(1)} %bitcast.281), channel_id=1, source_target_pairs={{0,16},{1,17},{2,18},{3,19},{4,20},{5,21},{6,22},{7,23},{8,24},{9,... | collective-permute-start | bytes 221192 | tf_op jit(solution)/shard_map/ppermute | solution.py:498
  22.5 16.9 %collective-permute-start.1 = (bf16[48,896]{1,0:T(8,128)(2,1)S(1)}, bf16[48,896]{1,0:T(8,128)(2,1)S(1)}, u32[]{:S(2)}, u32[]{:S(2)}) collective-permute-start(bf16[48,896]{1,0:T(8,128)(2,1)S(1)} %bitcast.278), channel_id=1, source_target_pairs={{0,16},{1,17},{2,18},{3,19},{4,20},{5,21},{6,22},{7,23},{8,24},{9,... | collective-permute-start | bytes 258056 | tf_op jit(solution)/shard_map/ppermute | solution.py:498
  23.7 19.0 %collective-permute-start.20 = (bf16[2,48,768]{2,1,0:T(8,128)(2,1)S(1)}, bf16[2,48,768]{2,1,0:T(8,128)(2,1)S(1)}, u32[]{:S(2)}, u32[]{:S(2)}) collective-permute-start(bf16[2,48,768]{2,1,0:T(8,128)(2,1)S(1)} %pad_maximum_fusion.17), channel_id=1, source_target_pairs={{0,8},{1,9},{2,10},{3,11},{4,12},{5,13},{6,14},{7,15},{8,0},{9,1},... | collective-permute-start | bytes 442376 | tf_op jit(solution)/shard_map/ppermute | solution.py:498
  33.6 12.3 %collective-permute-start.14 = (bf16[2,48,768]{2,1,0:T(8,128)(2,1)S(1)}, bf16[2,48,768]{2,1,0:T(8,128)(2,1)S(1)}, u32[]{:S(2)}, u32[]{:S(2)}) collective-permute-start(bf16[2,48,768]{2,1,0:T(8,128)(2,1)S(1)} %pad_maximum_fusion.16), channel_id=1, source_target_pairs={{0,8},{1,9},{2,10},{3,11},{4,12},{5,13},{6,14},{7,15},{8,0},{9,1},... | collective-permute-start | bytes 442376 | tf_op jit(solution)/shard_map/ppermute | solution.py:498
  39.5 19.2 %collective-permute-start.2 = (bf16[2,48,896]{2,1,0:T(8,128)(2,1)S(1)}, bf16[2,48,896]{2,1,0:T(8,128)(2,1)S(1)}, u32[]{:S(2)}, u32[]{:S(2)}) collective-permute-start(bf16[2,48,896]{2,1,0:T(8,128)(2,1)S(1)} %pad_maximum_fusion.14), channel_id=1, source_target_pairs={{0,8},{1,9},{2,10},{3,11},{4,12},{5,13},{6,14},{7,15},{8,0},{9,1},... | collective-permute-start | bytes 516104 | tf_op jit(solution)/shard_map/ppermute | solution.py:498
  42.8 17.9 %collective-permute-start.21 = (bf16[2,2,48,768]{3,2,1,0:T(8,128)(2,1)S(1)}, bf16[2,2,48,768]{3,2,1,0:T(8,128)(2,1)S(1)}, u32[]{:S(2)}, u32[]{:S(2)}) collective-permute-start(bf16[2,2,48,768]{3,2,1,0:T(8,128)(2,1)S(1)} %pad_maximum_fusion.12), channel_id=1, source_target_pairs={{0,2},{1,3},{2,0},{3,1},{4,6},{5,7},{6,4},{7,5},{8,10},{9,11},{10,... | collective-permute-start | bytes 884744 | tf_op jit(solution)/shard_map/ppermute | solution.py:498
  46.0 15.1 %collective-permute-start.15 = (bf16[2,2,48,768]{3,2,0,1:T(8,128)(2,1)S(1)}, bf16[2,2,48,768]{3,2,0,1:T(8,128)(2,1)S(1)}, u32[]{:S(2)}, u32[]{:S(2)}) collective-permute-start(bf16[2,2,48,768]{3,2,0,1:T(8,128)(2,1)S(1)} %pad_maximum_fusion.11), channel_id=1, source_target_pairs={{0,4},{1,5},{2,6},{3,7},{4,0},{5,1},{6,2},{7,3},{8,12},{9,13},{10,... | collective-permute-start | bytes 884744 | tf_op jit(solution)/shard_map/ppermute | solution.py:498
  49.2 14.1 %collective-permute-start.9 = (bf16[2,2,48,768]{3,2,1,0:T(8,128)(2,1)S(1)}, bf16[2,2,48,768]{3,2,1,0:T(8,128)(2,1)S(1)}, u32[]{:S(2)}, u32[]{:S(2)}) collective-permute-start(bf16[2,2,48,768]{3,2,1,0:T(8,128)(2,1)S(1)} %pad_maximum_fusion.10), channel_id=1, source_target_pairs={{0,2},{1,3},{2,0},{3,1},{4,6},{5,7},{6,4},{7,5},{8,10},{9,11},{10,... | collective-permute-start | bytes 884744 | tf_op jit(solution)/shard_map/ppermute | solution.py:498
  58.8 12.2 %collective-permute-start.3 = (bf16[2,2,48,896]{3,2,1,0:T(8,128)(2,1)S(1)}, bf16[2,2,48,896]{3,2,1,0:T(8,128)(2,1)S(1)}, u32[]{:S(2)}, u32[]{:S(2)}) collective-permute-start(bf16[2,2,48,896]{3,2,1,0:T(8,128)(2,1)S(1)} %pad_maximum_fusion.9), channel_id=1, source_target_pairs={{0,4},{1,5},{2,6},{3,7},{4,0},{5,1},{6,2},{7,3},{8,12},{9,13},{10,... | collective-permute-start | bytes 1032200 | tf_op jit(solution)/shard_map/ppermute | solution.py:498
  60.9 27.4 %collective-permute-start.22 = (bf16[2,2,2,48,768]{4,3,2,1,0:T(8,128)(2,1)S(1)}, bf16[2,2,2,48,768]{4,3,2,1,0:T(8,128)(2,1)S(1)}, u32[]{:S(2)}, u32[]{:S(2)}) collective-permute-start(bf16[2,2,2,48,768]{4,3,2,1,0:T(8,128)(2,1)S(1)} %pad_maximum_fusion.8), channel_id=1, source_target_pairs={{0,4},{1,5},{2,6},{3,7},{4,0},{5,1},{6,2},{7,3},{8,12},{9,13},{10,... | collective-permute-start | bytes 1769480 | tf_op jit(solution)/shard_map/ppermute | solution.py:498
  61.2 52.0 %collective-permute-start.16 = (bf16[2,2,2,48,768]{4,3,0,1,2:T(8,128)(2,1)S(1)}, bf16[2,2,2,48,768]{4,3,0,1,2:T(8,128)(2,1)S(1)}, u32[]{:S(2)}, u32[]{:S(2)}) collective-permute-start(bf16[2,2,2,48,768]{4,3,0,1,2:T(8,128)(2,1)S(1)} %pad_maximum_fusion.7), channel_id=1, source_target_pairs={{0,2},{1,3},{2,0},{3,1},{4,6},{5,7},{6,4},{7,5},{8,10},{9,11},{10,... | collective-permute-start | bytes 1769480 | tf_op jit(solution)/shard_map/ppermute | solution.py:498
  63.4 49.5 %collective-permute-start.10 = (bf16[2,2,2,48,768]{4,3,2,1,0:T(8,128)(2,1)S(1)}, bf16[2,2,2,48,768]{4,3,2,1,0:T(8,128)(2,1)S(1)}, u32[]{:S(2)}, u32[]{:S(2)}) collective-permute-start(bf16[2,2,2,48,768]{4,3,2,1,0:T(8,128)(2,1)S(1)} %pad_maximum_fusion.6), channel_id=1, source_target_pairs={{0,4},{1,5},{2,6},{3,7},{4,0},{5,1},{6,2},{7,3},{8,12},{9,13},{10,... | collective-permute-start | bytes 1769480 | tf_op jit(solution)/shard_map/ppermute | solution.py:498
  71.2 42.9 %collective-permute-start.4 = (bf16[2,2,2,48,896]{4,3,2,1,0:T(8,128)(2,1)S(1)}, bf16[2,2,2,48,896]{4,3,2,1,0:T(8,128)(2,1)S(1)}, u32[]{:S(2)}, u32[]{:S(2)}) collective-permute-start(bf16[2,2,2,48,896]{4,3,2,1,0:T(8,128)(2,1)S(1)} %pad_maximum_fusion.5), channel_id=1, source_target_pairs={{0,2},{1,3},{2,0},{3,1},{4,6},{5,7},{6,4},{7,5},{8,10},{9,11},{10,... | collective-permute-start | bytes 2064392 | tf_op jit(solution)/shard_map/ppermute | solution.py:498
  89.6 34.5 %collective-permute-start.23 = (bf16[768,768]{1,0:T(8,128)(2,1)}, bf16[768,768]{1,0:T(8,128)(2,1)S(1)}, u32[]{:S(2)}, u32[]{:S(2)}) collective-permute-start(bf16[768,768]{1,0:T(8,128)(2,1)} %bitcast.62.second_mine), channel_id=1, source_target_pairs={{0,1},{1,0},{2,3},{3,2},{4,5},{5,4},{6,7},{7,6},{8,9},{9,8},{10,11... | collective-permute-start | bytes 3538952 | tf_op jit(solution)/shard_map/ppermute | solution.py:498
  212.6 12.5 %collective-permute-start.42 = (bf16[768,768]{1,0:T(8,128)(2,1)}, bf16[768,768]{1,0:T(8,128)(2,1)}, u32[]{:S(2)}, u32[]{:S(2)}) collective-permute-start(bf16[768,768]{1,0:T(8,128)(2,1)} %get-tuple-element.67), channel_id=1, source_target_pairs={{0,1},{1,0},{2,3},{3,2},{4,5},{5,4},{6,7},{7,6},{8,9},{9,8},{10,11... | collective-permute-start | bytes 3538952 | tf_op jit(solution)/shard_map/ppermute | solution.py:498
  212.6 14.6 %collective-permute-start.36 = (bf16[768,768]{1,0:T(8,128)(2,1)}, bf16[768,768]{1,0:T(8,128)(2,1)}, u32[]{:S(2)}, u32[]{:S(2)}) collective-permute-start(bf16[768,768]{1,0:T(8,128)(2,1)} %get-tuple-element.65), channel_id=1, source_target_pairs={{0,1},{1,0},{2,3},{3,2},{4,5},{5,4},{6,7},{7,6},{8,9},{9,8},{10,11... | collective-permute-start | bytes 3538952 | tf_op jit(solution)/shard_map/ppermute | solution.py:498
  225.0 69.9 %collective-permute-start.54 = (bf16[1536,768]{1,0:T(8,128)(2,1)}, bf16[1536,768]{1,0:T(8,128)(2,1)S(1)}, u32[]{:S(2)}, u32[]{:S(2)}) collective-permute-start(bf16[1536,768]{1,0:T(8,128)(2,1)} %get-tuple-element.71), channel_id=1, source_target_pairs={{0,1},{1,0},{2,3},{3,2},{4,5},{5,4},{6,7},{7,6},{8,9},{9,8},{10,11... | collective-permute-start | bytes 7077896 | tf_op jit(solution)/shard_map/ppermute | solution.py:498
  225.1 71.2 %collective-permute-start.48 = (bf16[768,1536]{1,0:T(8,128)(2,1)}, bf16[768,1536]{1,0:T(8,128)(2,1)S(1)}, u32[]{:S(2)}, u32[]{:S(2)}) collective-permute-start(bf16[768,1536]{1,0:T(8,128)(2,1)} %get-tuple-element.69), channel_id=1, source_target_pairs={{0,1},{1,0},{2,3},{3,2},{4,5},{5,4},{6,7},{7,6},{8,9},{9,8},{10,11... | collective-permute-start | bytes 7077896 | tf_op jit(solution)/shard_map/ppermute | solution.py:498
  227.2 16.3 %collective-permute-start.43 = (bf16[2,2,2,48,768]{4,3,0,1,2:T(8,128)(2,1)S(1)}, bf16[2,2,2,48,768]{4,3,0,1,2:T(8,128)(2,1)S(1)}, u32[]{:S(2)}, u32[]{:S(2)}) collective-permute-start(bf16[2,2,2,48,768]{4,3,0,1,2:T(8,128)(2,1)S(1)} %bitcast.275), channel_id=1, source_target_pairs={{0,2},{1,3},{2,0},{3,1},{4,6},{5,7},{6,4},{7,5},{8,10},{9,11},{10,... | collective-permute-start | bytes 1769480 | tf_op jit(solution)/shard_map/ppermute | solution.py:498
  230.3 16.2 %collective-permute-start.37 = (bf16[2,2,2,48,768]{4,3,0,1,2:T(8,128)(2,1)S(1)}, bf16[2,2,2,48,768]{4,3,0,1,2:T(8,128)(2,1)S(1)}, u32[]{:S(2)}, u32[]{:S(2)}) collective-permute-start(bf16[2,2,2,48,768]{4,3,0,1,2:T(8,128)(2,1)S(1)} %bitcast.276), channel_id=1, source_target_pairs={{0,4},{1,5},{2,6},{3,7},{4,0},{5,1},{6,2},{7,3},{8,12},{9,13},{10,... | collective-permute-start | bytes 1769480 | tf_op jit(solution)/shard_map/ppermute | solution.py:498
  234.0 21.2 %collective-permute-start.31 = (bf16[2,2,2,48,768]{4,3,0,1,2:T(8,128)(2,1)S(1)}, bf16[2,2,2,48,768]{4,3,0,1,2:T(8,128)(2,1)S(1)}, u32[]{:S(2)}, u32[]{:S(2)}) collective-permute-start(bf16[2,2,2,48,768]{4,3,0,1,2:T(8,128)(2,1)S(1)} %bitcast.277), channel_id=1, source_target_pairs={{0,2},{1,3},{2,0},{3,1},{4,6},{5,7},{6,4},{7,5},{8,10},{9,11},{10,... | collective-permute-start | bytes 1769480 | tf_op jit(solution)/shard_map/ppermute | solution.py:498
  243.5 31.2 %collective-permute-start.25 = (bf16[2,2,2,48,896]{4,3,0,1,2:T(8,128)(2,1)S(1)}, bf16[2,2,2,48,896]{4,3,0,1,2:T(8,128)(2,1)S(1)}, u32[]{:S(2)}, u32[]{:S(2)}) collective-permute-start(bf16[2,2,2,48,896]{4,3,0,1,2:T(8,128)(2,1)S(1)} %bitcast.274), channel_id=1, source_target_pairs={{0,4},{1,5},{2,6},{3,7},{4,0},{5,1},{6,2},{7,3},{8,12},{9,13},{10,... | collective-permute-start | bytes 2064392 | tf_op jit(solution)/shard_map/ppermute | solution.py:498
  246.6 20.3 %collective-permute-start.44 = (bf16[2,2,48,768]{3,2,0,1:T(8,128)(2,1)S(1)}, bf16[2,2,48,768]{3,2,0,1:T(8,128)(2,1)S(1)}, u32[]{:S(2)}, u32[]{:S(2)}) collective-permute-start(bf16[2,2,48,768]{3,2,0,1:T(8,128)(2,1)S(1)} %fusion.5), channel_id=1, source_target_pairs={{0,4},{1,5},{2,6},{3,7},{4,0},{5,1},{6,2},{7,3},{8,12},{9,13},{10,... | collective-permute-start | bytes 884744 | tf_op jit(solution)/shard_map/ppermute | solution.py:498
  255.2 13.2 %collective-permute-start.38 = (bf16[2,2,48,768]{3,2,0,1:T(8,128)(2,1)S(1)}, bf16[2,2,48,768]{3,2,0,1:T(8,128)(2,1)S(1)}, u32[]{:S(2)}, u32[]{:S(2)}) collective-permute-start(bf16[2,2,48,768]{3,2,0,1:T(8,128)(2,1)S(1)} %fusion.4), channel_id=1, source_target_pairs={{0,2},{1,3},{2,0},{3,1},{4,6},{5,7},{6,4},{7,5},{8,10},{9,11},{10,... | collective-permute-start | bytes 884744 | tf_op jit(solution)/shard_map/ppermute | solution.py:498
  277.0 25.5 %collective-permute-start.26 = (bf16[2,2,48,896]{3,2,0,1:T(8,128)(2,1)S(1)}, bf16[2,2,48,896]{3,2,0,1:T(8,128)(2,1)S(1)}, u32[]{:S(2)}, u32[]{:S(2)}) collective-permute-start(bf16[2,2,48,896]{3,2,0,1:T(8,128)(2,1)S(1)} %fusion.2), channel_id=1, source_target_pairs={{0,2},{1,3},{2,0},{3,1},{4,6},{5,7},{6,4},{7,5},{8,10},{9,11},{10,... | collective-permute-start | bytes 1032200 | tf_op jit(solution)/shard_map/ppermute | solution.py:498
  296.3 33.0 %collective-permute-start.55 = (bf16[2,2,2,96,768]{4,3,0,1,2:T(8,128)(2,1)S(1)}, bf16[2,2,2,96,768]{4,3,0,1,2:T(8,128)(2,1)S(1)}, u32[]{:S(2)}, u32[]{:S(2)}) collective-permute-start(bf16[2,2,2,96,768]{4,3,0,1,2:T(8,128)(2,1)S(1)} %bitcast.272), channel_id=1, source_target_pairs={{0,4},{1,5},{2,6},{3,7},{4,0},{5,1},{6,2},{7,3},{8,12},{9,13},{10,... | collective-permute-start | bytes 3538952 | tf_op jit(solution)/shard_map/ppermute | solution.py:498
  298.8 28.0 %collective-permute-start.49 = (bf16[2,2,2,48,1536]{4,3,0,1,2:T(8,128)(2,1)S(1)}, bf16[2,2,2,48,1536]{4,3,0,1,2:T(8,128)(2,1)S(1)}, u32[]{:S(2)}, u32[]{:S(2)}) collective-permute-start(bf16[2,2,2,48,1536]{4,3,0,1,2:T(8,128)(2,1)S(1)} %bitcast.273), channel_id=1, source_target_pairs={{0,2},{1,3},{2,0},{3,1},{4,6},{5,7},{6,4},{7,5},{8,10},{9,11},{10,... | collective-permute-start | bytes 3538952 | tf_op jit(solution)/shard_map/ppermute | solution.py:498
  327.2 14.5 %collective-permute-start.50 = (bf16[2,2,48,1536]{3,2,0,1:T(8,128)(2,1)S(1)}, bf16[2,2,48,1536]{3,2,0,1:T(8,128)(2,1)S(1)}, u32[]{:S(2)}, u32[]{:S(2)}) collective-permute-start(bf16[2,2,48,1536]{3,2,0,1:T(8,128)(2,1)S(1)} %fusion), channel_id=1, source_target_pairs={{0,4},{1,5},{2,6},{3,7},{4,0},{5,1},{6,2},{7,3},{8,12},{9,13},{10,... | collective-permute-start | bytes 1769480 | tf_op jit(solution)/shard_map/ppermute | solution.py:498
  329.6 14.4 %collective-permute-start.56 = (bf16[2,2,96,768]{3,2,0,1:T(8,128)(2,1)S(1)}, bf16[2,2,96,768]{3,2,0,1:T(8,128)(2,1)S(1)}, u32[]{:S(2)}, u32[]{:S(2)}) collective-permute-start(bf16[2,2,96,768]{3,2,0,1:T(8,128)(2,1)S(1)} %fusion.1), channel_id=1, source_target_pairs={{0,2},{1,3},{2,0},{3,1},{4,6},{5,7},{6,4},{7,5},{8,10},{9,11},{10,... | collective-permute-start | bytes 1769480 | tf_op jit(solution)/shard_map/ppermute | solution.py:498
  344.2 12.7 %collective-permute-start.57 = (bf16[2,96,768]{2,1,0:T(8,128)(2,1)S(1)}, bf16[2,96,768]{2,1,0:T(8,128)(2,1)S(1)}, u32[]{:S(2)}, u32[]{:S(2)}) collective-permute-start(bf16[2,96,768]{2,1,0:T(8,128)(2,1)S(1)} %fusion.7), channel_id=1, source_target_pairs={{0,8},{1,9},{2,10},{3,11},{4,12},{5,13},{6,14},{7,15},{8,0},{9,1},... | collective-permute-start | bytes 884744 | tf_op jit(solution)/shard_map/ppermute | solution.py:498
  (45 other events, 281.0 us)
Sparse Core Ops, SparseCore 0:
  12.2 113.3 all-gather.2

commit v3 on v2

--- a/solution.py
+++ b/solution.py
@@ -85,16 +85,27 @@
 def grad_copies(core, targets, held, number, sems):
     half = held.shape[-1]
     copies = []
-    for side, target in enumerate(targets[number // 2]):
+    for side, target in enumerate(targets):
         place = core if side == 0 else 1 - core
         copies.append(
             pltpu.make_async_copy(
                 held.at[number, place],
-                target.at[:, (number % 2) * half : (number % 2 + 1) * half],
+                target.at[:, number * half : (number + 1) * half],
                 sems.at[2 * number + side],
             )
         )
     return copies
+
+
+def pack_kernel(core_ref, *refs):
+    shards, gains, (send, keep) = refs[:-3], refs[-3], refs[-2:]
+    core = core_ref[0]
+    half = shards[0].shape[1] // 2
+    for number, shard in enumerate(shards):
+        for target, place in ((send, 1 - core), (keep, core)):
+            target[:, number * half : (number + 1) * half] = shard[:, pl.ds(pl.multiple_of(place * half, PAIR), half)]
+    for target in (send, keep):
+        target[:, len(shards) * half :] = gains[...]
 
 
 def self_mask(ids_row):
@@ -142,7 +153,7 @@
 def self_backward_kernel(
     core_ref, ids, tokens, gains, grad_after, gain_grads, projected, context,
     first_mine, first_sibling, second_mine, second_sibling,
-    tokens_grad, first_grad, first_other, second_grad, second_other,
+    tokens_grad, grad_mine, grad_other,
     kept, held, gain_held, sems, out_sems,
 ):
     core = core_ref[0]
@@ -156,11 +167,10 @@
     hidden = tokens[...].astype(jnp.float32)
     normed = low(normalize(hidden, gains[0:1, :]))
     branch = low(grad_after[...])
-    targets = ((first_grad, first_other), (second_grad, second_other))
     started = []
 
     def send(number):
-        for copy in grad_copies(core, targets, held, number, out_sems):
+        for copy in grad_copies(core, (grad_mine, grad_other), held, number, out_sems):
             copy.start()
             started.append(copy)
 
@@ -197,8 +207,8 @@
         row == 0, grad_gain, jnp.where(row == 1, others[0:1], jnp.where(row == 2, others[1:2], 0.0))
     )
     gain_held[...] = low(wide.T)
-    for slot, target in enumerate((first_grad, first_other)):
-        copy = pltpu.make_async_copy(gain_held, target.at[:, model : model + PAIR], out_sems.at[8 + slot])
+    for slot, target in enumerate((grad_mine, grad_other)):
+        copy = pltpu.make_async_copy(gain_held, target.at[:, 2 * model :], out_sems.at[8 + slot])
         copy.start()
         started.append(copy)
     for copy in started:
@@ -234,7 +244,7 @@
 def cross_forward_kernel(
     core_ref, ids, groups, after_self, gains, encoded,
     first_mine, first_sibling, second_mine, second_sibling,
-    queries, context, after_cross, probs_out, mixed_out, spread_out,
+    queries, context, after_cross, normed_out, probs_out, mixed_out, spread_out,
     rows_ref, kept, sems, weight_sems,
 ):
     core = core_ref[0]
@@ -295,66 +305,80 @@
         found = contract(both, pair_weight(kept, 2, j), 1, 0)
         context[:, j * PAIR : (j + 1) * PAIR] = low(pair_lanes(found))
     after_cross[...] = after_self[...] + times(context[...], kept, 3)
-
-
-def cross_backward_kernel(
-    core_ref, ids, groups, grad_after, after_self, gains, ffn_gain_grad, queries, context, encoded,
-    probs_ref, mixed, spread, first_mine, first_sibling, second_mine, second_sibling,
-    grad_self, gain_grads, grad_rows, first_grad, first_other, second_grad, second_other,
-    rows_ref, pulled_ref, moved_ref, sum_ref, kept, held, sems, row_sems, weight_sems, out_sems,
+    normed_out[...] = low(normalize(after_cross[...], gains[2:3, :]))
+
+
+def cross_backward_first(
+    core_ref, after_cross, gains, cotangent, pull_mine, pull_theirs, context, mixed, second_mine, second_sibling,
+    grad_after, gain_grad, grad_context_out, pulled_ref, grad_mine, grad_other,
+    kept, held, weight_sems, out_sems,
 ):
     core = core_ref[0]
-    heads, tokens, model = spread.shape
+    heads, tokens, model = pulled_ref.shape
+    copies = weight_copies(core, ((second_mine, second_sibling),), kept, weight_sems)
+    for copy in copies[2:] + copies[:2]:
+        copy.start()
+    grad_normed = pull_mine[...] + pull_theirs[...].astype(jnp.float32)
+    grad_values, found_gain = norm_backward(after_cross[...], gains[2:3, :], grad_normed)
+    grad_after[...] = cotangent[...].astype(jnp.float32) + grad_values
+    gain_grad[0:1, :] = found_gain
+    branch = low(grad_after[...])
+    grad_into(context[...], branch, held, 1)
+    started = []
+
+    def send(number):
+        for copy in grad_copies(core, (grad_mine, grad_other), held, number, out_sems):
+            copy.start()
+            started.append(copy)
+
+    send(1)
+    for copy in copies[2:] + copies[:2]:
+        copy.wait()
+    grad_context_out[...] = low(times_back(branch, kept, 1))
+    per_half = held.shape[-1] // PAIR
+    for j in range(heads // 2):
+        columns = slice((j % per_half) * PAIR, (j % per_half + 1) * PAIR)
+        rows = pair_rows(grad_context_out[:, j * PAIR : (j + 1) * PAIR])
+        both = jnp.concatenate([mixed[2 * j], mixed[2 * j + 1]], axis=0)
+        held[0, j // per_half, :, columns] = low(contract(both, rows, 0, 0))
+        pulled = low(contract(rows, pair_weight(kept, 0, j), 1, 1))
+        pulled_ref[2 * j] = pulled[:tokens]
+        pulled_ref[2 * j + 1] = pulled[tokens:]
+    send(0)
+    for copy in started:
+        copy.wait()
+
+
+def cross_backward_second(
+    core_ref, ids, groups, grad_after, after_self, gains, ffn_gain_grad, queries, encoded,
+    probs_ref, pulled_ref, first_mine, first_sibling,
+    grad_self, gain_grads, score_out, grad_mine, grad_other,
+    rows_ref, moved_ref, kept, held, sems, weight_sems, out_sems,
+):
+    core = core_ref[0]
+    heads, tokens, model = pulled_ref.shape
     segs = groups.shape[1]
     block_rows = encoded.shape[0] // segs
     half = kept.shape[-1]
-    copies = weight_copies(
-        core, ((first_mine, first_sibling), (second_mine, second_sibling)), kept, weight_sems
-    )
-    for copy in copies[4:] + copies[:4]:
-        copy.start()
     row_moves = row_copies(encoded, rows_ref, sems, segs)
     for copy in row_moves:
         copy.start()
-    targets = ((first_grad, first_other), (second_grad, second_other))
+    copies = weight_copies(core, ((first_mine, first_sibling),), kept, weight_sems)
+    for copy in copies:
+        copy.start()
     started = []
 
     def send(number):
-        for copy in grad_copies(core, targets, held, number, out_sems):
+        for copy in grad_copies(core, (grad_mine, grad_other), held, number, out_sems):
             copy.start()
             started.append(copy)
 
-    branch = low(grad_after[...])
-    grad_into(context[...], branch, held, 3)
-    send(3)
-    for copy in copies:
-        copy.wait()
-    grad_context = low(times_back(branch, kept, 3))
-    for j in range(heads // 2):
-        block = grad_context[:, j * PAIR : (j + 1) * PAIR]
-        pulled = low(contract(pair_rows(block), pair_weight(kept, 2, j), 1, 1))
-        pulled_ref[2 * j] = pulled[:tokens]
-        pulled_ref[2 * j + 1] = pulled[tokens:]
     for copy in row_moves:
         copy.wait()
-
-    def write_out(s):
-        slot = s & 1
-        base = pl.multiple_of(groups[0, s] * block_rows, block_rows)
-        return pltpu.make_async_copy(
-            sum_ref.at[slot], grad_rows.at[pl.ds(base, block_rows)], row_sems.at[slot]
-        )
 
     def segment(s, begin):
         end = begin + segment_length(ids, s)
         base = pl.multiple_of(groups[0, s] * block_rows, block_rows)
-        slot = s & 1
-
-        @pl.when(s >= 2)
-        def _():
-            write_out(s - 2).wait()
-
-        sum_ref[slot] = jnp.zeros((block_rows, model), jnp.float32)
 
         def chunk(c, carry):
             token = pl.multiple_of(c * CHUNK, CHUNK)
@@ -370,16 +394,16 @@
             score_grad = low(wide * (prob_grad - inner))
             moved = low(contract(score_grad, rows, 1, 0)).reshape(heads, CHUNK, model)
             moved_ref[at] = jnp.where(inside, moved, moved_ref[at])
-            left = jnp.concatenate([score_grad, probs], axis=0)
-            right = jnp.concatenate([spread[at].reshape(heads * CHUNK, model), pulled], axis=0)
-            sum_ref[slot] += contract(left, right, 0, 0)
+            score_grad = score_grad.reshape(heads, CHUNK, block_rows)
+            score_out[at] = jnp.where(inside, score_grad, score_out[at])
             return carry
 
         lax.fori_loop(begin >> 4, (end + CHUNK - 1) >> 4, chunk, 0)
-        write_out(s).start()
         return end
 
     lax.fori_loop(0, segs, segment, 0)
+    for copy in copies:
+        copy.wait()
     found = []
     per_half = half // PAIR
     for j in range(heads // 2):
@@ -389,12 +413,6 @@
         block = queries[:, j * PAIR : (j + 1) * PAIR] * jnp.bfloat16(0.125)
         held[1, j // per_half, :, columns] = low(contract(both, pair_rows(block), 0, 0))
     send(1)
-    for j in range(heads // 2):
-        columns = slice((j % per_half) * PAIR, (j % per_half + 1) * PAIR)
-        block = grad_context[:, j * PAIR : (j + 1) * PAIR]
-        both = jnp.concatenate([mixed[2 * j], mixed[2 * j + 1]], axis=0)
-        held[2, j // per_half, :, columns] = low(contract(both, pair_rows(block), 0, 0))
-    send(2)
     grad_queries = jnp.concatenate(found, axis=1)
     values = after_self[...]
     grad_into(low(normalize(values, gains[1:2, :])), grad_queries, held, 0)
@@ -405,6 +423,54 @@
     gain_grads[1:2, :] = ffn_gain_grad[0:1, :]
     for copy in started:
         copy.wait()
+
+
+def rows_backward_kernel(
+    ids, groups, score_grads, probs_ref, spread, pulled_ref, grad_rows, sum_ref, row_sems,
+):
+    heads, tokens, model = spread.shape
+    segs = groups.shape[1]
+    block_rows = grad_rows.shape[0] // segs
+
+    def write_out(s):
+        slot = s & 1
+        base = pl.multiple_of(groups[0, s] * block_rows, block_rows)
+        return pltpu.make_async_copy(
+            sum_ref.at[slot], grad_rows.at[pl.ds(base, block_rows)], row_sems.at[slot]
+        )
+
+    def segment(s, begin):
+        end = begin + segment_length(ids, s)
+        slot = s & 1
+
+        @pl.when(s >= 2)
+        def _():
+            write_out(s - 2).wait()
+
+        def terms(c):
+            token = pl.multiple_of(c * CHUNK, CHUNK)
+            at = (slice(None), pl.ds(token, CHUNK), slice(None))
+            inside = in_segment(token, begin, end, heads)
+            zero = jnp.zeros((), jnp.bfloat16)
+            scores = jnp.where(inside, score_grads[at], zero).reshape(heads * CHUNK, block_rows)
+            left = jnp.concatenate([scores, probs_ref[at].reshape(heads * CHUNK, block_rows)], axis=0)
+            right = jnp.concatenate(
+                [jnp.where(inside, piece[at], zero).reshape(heads * CHUNK, model) for piece in (spread, pulled_ref)],
+                axis=0,
+            )
+            return contract(left, right, 0, 0)
+
+        def chunk(c, carry):
+            sum_ref[slot] += terms(c)
+            return carry
+
+        first = begin >> 4
+        sum_ref[slot] = terms(first)
+        lax.fori_loop(first + 1, (end + CHUNK - 1) >> 4, chunk, 0)
+        write_out(s).start()
+        return end
+
+    lax.fori_loop(0, segs, segment, 0)
     for s in range(segs - 2, segs):
         write_out(s).wait()
 
@@ -420,73 +486,82 @@
 
 def ffn_kernel(
     direct,
-    core_ref, after_cross, gains, cotangent, weight_in, gathered,
-    block_out, grad_after, gain_grad, in_mine, in_other, down_mine, down_other,
-    kept_in, kept_down, held_in, held_down, sems, out_sems,
+    core_ref, normed, normed_theirs, cotangent, cotangent_theirs, *refs,
 ):
+    if direct:
+        mine, sibling = refs[:2]
+        rows = mine.shape[1] // 2
+        sources = ((mine.at[:, :rows], sibling.at[:, :rows]), (mine.at[:, rows:], sibling.at[:, rows:]))
+    else:
+        sources = refs[:2]
+    out_mine, out_other, pull_mine, pull_other, grad_mine, grad_other = refs[2:8]
+    kept_in, kept_down, held_in, held_down, sems, out_sems = refs[8:]
     core = core_ref[0]
-    blocks, model, width = weight_in.shape
-    per_block, rows_down = kept_down.shape[1:3]
-    copies = []
-    for j in range(blocks):
-        copies.append(pltpu.make_async_copy(weight_in.at[j], kept_in.at[j], sems.at[2 * j]))
-        copies.append(
-            pltpu.make_async_copy(
-                gathered.at[pl.ds(j * per_block, per_block), pl.ds(gathered.shape[1] - rows_down, rows_down)]
-                if direct
-                else gathered.at[j],
-                kept_down.at[j],
-                sems.at[2 * j + 1],
+    blocks, groups, unused, width = kept_in.shape
+    model = kept_in.shape[1] * kept_in.shape[2]
+    count = normed.shape[0]
+    if direct:
+        copies = [
+            pltpu.make_async_copy(source, target, sems.at[n])
+            for n, (source, target) in enumerate(
+                (
+                    (sources[0][0], kept_in.at[core]),
+                    (sources[1][0], kept_down.at[:, core]),
+                    (sources[0][1], kept_in.at[1 - core]),
+                    (sources[1][1], kept_down.at[:, 1 - core]),
+                )
             )
-        )
+        ]
+    else:
+        copies = [
+            pltpu.make_async_copy(source, target, sems.at[n])
+            for n, (source, target) in enumerate(zip(sources, (kept_in, kept_down)))
+        ]
     for copy in copies:
         copy.start()
-    values = after_cross[...]
-    normed = low(normalize(values, gains[2:3, :]))
-    pull = cotangent[...]
-    total = values
-    grad_normed = jnp.zeros(values.shape, jnp.float32)
-    chips = per_block // 2
+    tokens = jnp.concatenate([normed[...], normed_theirs[...]], axis=0)
+    pull = jnp.concatenate([cotangent[...], cotangent_theirs[...]], axis=0)
+    for copy in copies:
+        copy.wait()
+    total = grad_tokens = None
     started = []
-    for j in range(blocks):
-        copies[2 * j].wait()
-        copies[2 * j + 1].wait()
-        weight_up = kept_in[j]
-        weight_down = kept_down[j].reshape(width, model)
-        activated, slope = gelu_both(contract(normed, weight_up, 1, 0))
+    for b in range(blocks):
+        weight_up = kept_in[b].reshape(model, width)
+        part = slice(b * groups // blocks, (b + 1) * groups // blocks) if direct else slice(0, 1)
+        if direct:
+            weight_down = kept_down[part].reshape(width, model)
+        else:
+            weight_down = kept_down[0, 0, b * width : (b + 1) * width]
+        activated, slope = gelu_both(contract(tokens, weight_up, 1, 0))
         activated = low(activated)
-        total = total + contract(activated, weight_down, 1, 0)
         grad_act = low(contract(pull, weight_down, 1, 1)).astype(jnp.float32)
         grad_pre = low(slope * grad_act)
-        grad_normed = grad_normed + contract(grad_pre, weight_up, 1, 1)
-        held_in[j] = low(contract(normed, grad_pre, 0, 0))
+        added = contract(grad_pre, weight_up, 1, 1)
+        grad_tokens = added if b == 0 else grad_tokens + added
+        added = contract(activated, weight_down, 1, 0)
+        total = added if b == 0 else total + added
+        held_in[b] = low(contract(tokens, grad_pre, 0, 0)).reshape(held_in.shape[1:])
         grad_down = low(contract(activated, pull, 0, 0))
         if direct:
-            for k in range(per_block):
-                at = (j * chips + k // 2) * rows_down
-                held_down[k % 2, at : at + rows_down] = grad_down[k * rows_down : (k + 1) * rows_down]
+            held_down[part] = grad_down.reshape((groups // blocks,) + held_down.shape[1:])
         else:
-            held_down[j // 2, (j % 2) * width : (j % 2 + 1) * width] = grad_down
-    half = blocks // 2
-    for side, target in enumerate((in_mine, in_other)):
-        place = core if side == 0 else 1 - core
-        for j in range(half):
-            copy = pltpu.make_async_copy(
-                held_in.at[place * half + j],
-                target.at[:, j * width : (j + 1) * width],
-                out_sems.at[side * half + j],
-            )
-            copy.start()
-            started.append(copy)
-    for side, target in enumerate((down_mine, down_other)):
-        place = (core if side == 0 else 1 - core) if direct else side
-        copy = pltpu.make_async_copy(held_down.at[place], target, out_sems.at[2 * half + side])
+            held_down[0, 0, b * width : (b + 1) * width] = grad_down
+    if direct:
+        targets = (
+            (held_in.at[1 - core], grad_other.at[:, :rows]),
+            (held_down.at[:, 1 - core], grad_other.at[:, rows:]),
+            (held_in.at[core], grad_mine.at[:, :rows]),
+            (held_down.at[:, core], grad_mine.at[:, rows:]),
+        )
+    else:
+        targets = ((held_in, grad_mine), (held_down, grad_other))
+    started = [pltpu.make_async_copy(source, target, out_sems.at[n]) for n, (source, target) in enumerate(targets)]
+    for copy in started:
         copy.start()
-        started.append(copy)
-    block_out[...] = low(total)
-    grad_values, grad_gain = norm_backward(values, gains[2:3, :], grad_normed)
-    grad_after[...] = pull.astype(jnp.float32) + grad_values
-    gain_grad[0:1, :] = grad_gain
+    out_mine[...] = total[:count]
+    out_other[...] = low(total[count:])
+    pull_mine[...] = grad_tokens[:count]
+    pull_other[...] = low(grad_tokens[count:])
     for copy in started:
         copy.wait()
 
@@ -508,34 +583,88 @@
     return jnp.stack([first, second], axis=axis)
 
 
-def gather_bits(block, order, me, devices):
-    held = block
-    done = []
-    for bit in order:
-        theirs = swap_with(held, 1 << bit, devices)
-        place = sum(1 for other in done if other > bit)
-        held = pair_up(held, theirs, bit_of(me, bit), place)
-        done.append(bit)
-    return held.reshape(-1, block.shape[-1])
-
-
-def core_sum(mine, other, devices):
-    theirs = swap_with(other, 1, devices)
-    return low(mine.astype(jnp.float32) + theirs.astype(jnp.float32))
-
-
-def scatter_bits(partial, order, me, devices):
-    rows = partial.shape[0] >> len(order)
-    held = partial.reshape((2,) * len(order) + (rows, partial.shape[-1]))
-    left = sorted(order, reverse=True)
-    for bit in order:
-        place = left.index(bit)
-        mine = lax.dynamic_index_in_dim(held, bit_of(me, bit), place, keepdims=False)
-        other = lax.dynamic_index_in_dim(held, 1 - bit_of(me, bit), place, keepdims=False)
-        theirs = swap_with(low(other), 1 << bit, devices)
-        held = mine.astype(jnp.float32) + theirs.astype(jnp.float32)
-        left.remove(bit)
-    return held
+def arranged(found, bits, me):
+    found = {mask: [block] for mask, block in found.items()}
+    for n, bit in enumerate(sorted(bits)):
+        low_side = bit_of(me, bit) == 0
+        merged = {}
+        for mask in found:
+            if not mask >> n & 1:
+                both = list(zip(found[mask], found[mask | 1 << n]))
+                merged[mask] = [jnp.where(low_side, x, y) for x, y in both] + [
+                    jnp.where(low_side, y, x) for x, y in both
+                ]
+        found = merged
+    return jnp.stack(found[0])
+
+
+def wide_mask(mask, bits):
+    return sum(1 << bit for n, bit in enumerate(sorted(bits)) if mask >> n & 1)
+
+
+def exchange(send, bits, me, devices):
+    found = {0: send(0)}
+    for mask in range(1, 1 << len(bits)):
+        found[mask] = swap_with(send(mask), wide_mask(mask, bits), devices)
+    return arranged(found, bits, me)
+
+
+def gather_line(block, bits, me, devices):
+    if len(bits) > 2:
+        held = block[None]
+        for bit in sorted(bits):
+            theirs = swap_with(held, 1 << bit, devices)
+            held = pair_up(held, theirs, bit_of(me, bit), 0).reshape((-1,) + block.shape)
+        return held
+    return exchange(lambda mask: block, bits, me, devices)
+
+
+def taken(source, places, columns):
+    array, bits, offset = source
+    begin = [places[bit] if bit in places else 0 for bit in bits] + [0, offset + columns[0]]
+    size = [1 if bit in places else 2 for bit in bits] + [array.shape[-2], columns[1] - columns[0]]
+    part = lax.dynamic_slice(array, begin, size)
+    return part.reshape([2 for bit in bits if bit not in places] + size[-2:])
+
+
+def summed(entry, places):
+    sources, columns = entry
+    total = None
+    for source in sources:
+        part = taken(source, places, columns).astype(jnp.float32)
+        total = part if total is None else total + part
+    return total
+
+
+def sum_over(entries, bit, done, me, devices):
+    places = {other: bit_of(me, other) for other in done}
+    send = [low(summed(entry, {**places, bit: 1 - bit_of(me, bit)})) for entry in entries]
+    theirs = swap_with(jnp.concatenate(send, axis=-1), 1 << bit, devices)
+    found, at = [], 0
+    for sources, columns in entries:
+        bits = [other for other in sources[0][1] if other not in done and other != bit]
+        found.append((sources + [(theirs, bits, at - columns[0])], columns))
+        at += columns[1] - columns[0]
+    return found
+
+
+def sum_line(stacks, bits, done, me, devices):
+    places = {bit: bit_of(me, bit) for bit in done}
+
+    def block(line):
+        return jnp.concatenate(
+            [jnp.concatenate([summed(entry, {**places, **line}) for entry in entries], axis=-1) for entries in stacks],
+            axis=-2,
+        )
+
+    mine = {bit: bit_of(me, bit) for bit in bits}
+    total = None
+    for mask in range(1, 1 << len(bits)):
+        wide = wide_mask(mask, bits)
+        send = low(block({bit: mine[bit] ^ (wide >> bit & 1) for bit in bits}))
+        theirs = swap_with(send, wide, devices).astype(jnp.float32)
+        total = theirs if total is None else total + theirs
+    return block(mine) + total
 
 
 def core_rows(total, core, devices):
@@ -555,7 +684,7 @@
     return jax.ShapeDtypeStruct(shape, dtype)
 
 
-def call(kernel, name, flops, in_specs, out_specs, out_shape, scratch):
+def call(kernel, name, flops, in_specs, out_specs, out_shape, scratch, aliases={}):
     return pl.pallas_call(
         kernel,
         out_shape=out_shape,
@@ -563,8 +692,9 @@
         out_specs=out_specs,
         scratch_shapes=scratch,
         compiler_params=pltpu.CompilerParams(vmem_limit_bytes=VMEM_BYTES),
-        cost_estimate=pl.CostEstimate(flops=flops, bytes_accessed=10_000_000, transcendentals=0),
+        cost_estimate=pl.CostEstimate(flops=flops, bytes_accessed=1_000_000, transcendentals=0),
         name=name,
+        input_output_aliases=aliases,
     )
 
 
@@ -595,8 +725,7 @@
     core_word = core.reshape(1).astype(jnp.int32)
     chip_bits = list(range(1, devices.bit_length() - 1))
     line_bits = [bit for bit in reversed(chip_bits) if bit > 2]
-    forward_orders = (line_bits + [2, 1], line_bits + [1, 2])
-    backward_orders = ([2, 1] + line_bits[::-1], [1, 2] + line_bits[::-1])
+    pair_orders = ([2, 1], [1, 2])
     count, model = tokens.shape
     encoder_count = encoded.shape[0]
     hidden_units = ffn_in.shape[1]
@@ -609,42 +738,70 @@
         width = matrix.shape[-1] // 2
         return lax.dynamic_slice_in_dim(matrix, owner * width, width, axis=matrix.ndim - 1)
 
-    def gather_group(shards, extra):
-        first, second = shards[:2], shards[2:]
-
-        def chip_block(pair, also):
-            send = jnp.concatenate([my_columns(shard, 1 - core) for shard in pair] + also, axis=1)
-            keep = jnp.concatenate([my_columns(shard, core) for shard in pair] + also, axis=1)
-            theirs = swap_with(send, 1, devices)
-            return pair_up(keep, theirs, core, 0).reshape(-1, keep.shape[1])
-
-        wholes = []
-        for pair, also, order in zip((first, second), (extra, []), forward_orders):
-            mine = gather_bits(chip_block(pair, also), order, me, devices)
-            wholes.append((mine, swap_with(mine[:, :model], 1, devices)))
-        return wholes
-
+    barrier = lax.optimization_barrier
     gains = jnp.stack([self_gain, cross_gain, ffn_gain], axis=1)
     gains = jnp.pad(gains, ((0, 0), (0, PAIR - 3)))
-    self_weights = gather_group([self_query, self_key, self_value, self_out], [gains])
-    cross_weights = gather_group([cross_query, cross_key, cross_value, cross_out], [])
-    gain_rows = jnp.pad(self_weights[0][0][:, model : model + 8].T.astype(wide_type), ((0, 0), (0, 0)))
-    self_flat = self_weights[0] + self_weights[1]
-    cross_flat = cross_weights[0] + cross_weights[1]
-
-    blocks = hidden_units // model
+    shards = [self_query, self_key, self_value, self_out, cross_query, cross_key, cross_value, cross_out]
+    packed = shaped((self_query.shape[0], len(shards) * half + PAIR), low_type)
+    send, keep = call(
+        pack_kernel, "pack", 0, [SMEM] + [VMEM] * 9, [VMEM] * 2, (packed, packed), []
+    )(core_word, *shards, gains)
+    theirs = swap_with(send, 1, devices)
+    chip_block = pair_up(keep, theirs, core, 0).reshape(-1, keep.shape[1])
+    self_block = jnp.concatenate([chip_block[:, : 2 * model], chip_block[:, 4 * model :]], axis=1)
+    cross_block = chip_block[:, 2 * model : 4 * model]
+
+    def double(held, bit, first_bit, me):
+        place = 1 if first_bit is None or bit > first_bit else 2
+        return pair_up(held, swap_with(held, 1 << bit, devices), bit_of(me, bit), place)
+
+    def first_step(line, width):
+        return [double(part, order[0], None, me) for part, order in zip((line[:, :, :width], line[:, :, width:]), pair_orders)]
+
+    def second_step(parts):
+        return [
+            double(part, order[1], order[0], me).reshape(-1, part.shape[-1])
+            for part, order in zip(parts, pair_orders)
+        ]
+
     rows_in = ffn_in.shape[0]
     rows_down = ffn_out.shape[0]
-    ffn_shard = jnp.concatenate(
-        [ffn_in[:, n * model : (n + 1) * model] for n in range(blocks)] + [ffn_out], axis=0
-    )
-    gathered = lax.all_gather(ffn_shard, AXES, axis=0)
-    weight_in = jnp.stack(
-        [gathered[:, n * rows_in : (n + 1) * rows_in].reshape(model, model) for n in range(blocks)]
-    )
     direct = rows_down % 16 == 0
-    down_shape = (devices // blocks, rows_down) if direct else (1, model)
-    down_source = gathered if direct else gathered[:, blocks * rows_in :].reshape(blocks, 1, model, model)
+    chip_groups = devices // 4
+    group_bits = [0, 1]
+    cotangent_theirs = swap_with(cotangent, 2, devices)
+    in_blocks = ffn_in.reshape(rows_in, 2, chip_groups // 2, 2, 2 * rows_down)
+    in_blocks = in_blocks.transpose(3, 1, 0, 2, 4).reshape(2, 2, rows_in, model)
+
+    def block_for(array, mask):
+        first = [bit_of(me, 1) ^ (mask >> 1 & 1), core ^ (mask & 1)]
+        return lax.dynamic_slice(array, first + [0, 0], (1, 1) + array.shape[2:]).reshape(array.shape[2:])
+
+    self_line = gather_line(self_block, line_bits, me, devices)
+    self_line, cross_block, in_blocks = barrier((self_line, cross_block, in_blocks))
+    in_rows = exchange(lambda mask: block_for(in_blocks, mask), group_bits, me, devices)
+    ffn_block = jnp.concatenate([in_rows.reshape(4 * rows_in, model), ffn_out], axis=0)
+    self_parts = first_step(self_line, model)
+    cross_line = gather_line(cross_block, line_bits, me, devices)
+    ffn_steps = line_bits + [2]
+
+    def ffn_step(held, number):
+        bit = ffn_steps[number]
+        place = sum(1 for other in ffn_steps[:number] if other > bit)
+        return pair_up(held, swap_with(held, 1 << bit, devices), bit_of(me, bit), place)
+
+    self_parts, cross_line, ffn_held = barrier((self_parts, cross_line, ffn_block))
+    self_mine = second_step(self_parts)
+    cross_parts = first_step(cross_line, model)
+    for number in range(len(line_bits) - 1):
+        ffn_held = ffn_step(ffn_held, number)
+    cross_parts, ffn_held, self_mine = barrier((cross_parts, ffn_held, self_mine))
+    cross_mine = second_step(cross_parts)
+    ffn_held = ffn_step(ffn_held, len(line_bits) - 1)
+    self_weights = [(mine, swap_with(mine[:, :model], 1, devices)) for mine in self_mine]
+
+    gain_rows = self_weights[1][0][:, model : model + 8].T.astype(wide_type)
+    self_flat = self_weights[0] + self_weights[1]
 
     dma = pltpu.SemaphoreType.DMA
     weights_kept = pltpu.VMEM((4, 2, model, half), low_type)
@@ -662,18 +819,26 @@
         [weights_kept, dma((8,))],
     )(core_word, segment_ids, tokens, gain_rows, *self_flat)
 
+    cross_mine, ffn_held, after_self, cotangent_theirs = barrier(
+        (cross_mine, ffn_held, after_self, cotangent_theirs)
+    )
+    ffn_theirs = swap_with(ffn_held, 4, devices)
+    cross_weights = [(mine, swap_with(mine, 1, devices)) for mine in cross_mine]
+    cross_flat = cross_weights[0] + cross_weights[1]
+
     per_token = (heads, count, model)
     probs_shape = (heads, count, encoder_count // segs)
-    queries_two, context_two, after_cross, probs, mixed, spread = call(
+    queries_two, context_two, after_cross, normed_three, probs, mixed, spread = call(
         cross_forward_kernel,
         "cross_forward",
         12_000_000_000,
         [SMEM, SMEM, SMEM, VMEM, VMEM] + [HBM] * 5,
-        [VMEM] * 6,
+        [VMEM] * 7,
         (
             shaped((count, model), low_type),
             shaped((count, model), low_type),
             shaped((count, model), wide_type),
+            shaped((count, model), low_type),
             shaped(probs_shape, low_type),
             shaped(per_token, low_type),
             shaped(per_token, low_type),
@@ -681,99 +846,191 @@
         [pltpu.VMEM(encoded.shape, low_type), weights_kept, dma((segs,)), dma((8,))],
     )(core_word, segment_ids, passage_group, after_self, gain_rows, encoded, *cross_flat)
 
-    (block_out, grad_after_cross, ffn_gain_grad, in_mine, in_other, down_mine, down_other) = call(
+    ffn_theirs, normed_three = barrier((ffn_theirs, normed_three))
+    normed_theirs = swap_with(normed_three, 2, devices)
+    ffn_mine = pair_up(ffn_held, ffn_theirs, bit_of(me, 2), len(line_bits)).reshape(chip_groups, -1, model)
+    ffn_sibling = swap_with(ffn_mine, 1, devices)
+    half_units = hidden_units // 2
+    if direct:
+        in_shape = (2, chip_groups, rows_down, model)
+        down_shape = (chip_groups, 2, rows_down, model)
+        ffn_weights = (ffn_mine, ffn_sibling)
+        grad_shapes = (shaped(ffn_mine.shape, low_type),) * 2
+    else:
+        in_shape, down_shape = (2, 1, model, model), (1, 1, half_units, model)
+        both = pair_up(ffn_mine, ffn_sibling, core, 0)
+        ffn_weights = (
+            both[:, :, : 4 * rows_in].reshape(in_shape),
+            both[:, :, 4 * rows_in :].swapaxes(0, 1).reshape(down_shape),
+        )
+        grad_shapes = (shaped(in_shape, low_type), shaped(down_shape, low_type))
+    token_shapes = (shaped((count, model), wide_type), shaped((count, model), low_type))
+    out_mine, out_other, pull_mine, pull_other, ffn_grad, ffn_other = call(
         functools.partial(ffn_kernel, direct),
         "ffn",
-        2 * count * model * hidden_units * 6,
-        [SMEM, VMEM, VMEM, VMEM, HBM, HBM],
-        [VMEM] * 3 + [HBM] * 4,
-        (
-            shaped((count, model), low_type),
-            shaped((count, model), wide_type),
-            shaped((8, model), wide_type),
-            shaped((model, hidden_units // 2), low_type),
-            shaped((model, hidden_units // 2), low_type),
-            shaped((hidden_units // 2, model), low_type),
-            shaped((hidden_units // 2, model), low_type),
-        ),
+        4_000_000_000,
+        [SMEM] + [VMEM] * 4 + [HBM] * 2,
+        [VMEM] * 4 + [HBM] * 2,
+        token_shapes + token_shapes + grad_shapes,
         [
-            pltpu.VMEM((blocks, model, model), low_type),
-            pltpu.VMEM((blocks,) + down_shape + (model,), low_type),
-            pltpu.VMEM((blocks, model, model), low_type),
-            pltpu.VMEM((2, hidden_units // 2, model), low_type),
-            dma((2 * blocks,)),
-            dma((blocks + 2,)),
+            pltpu.VMEM(in_shape, low_type),
+            pltpu.VMEM(down_shape, low_type),
+            pltpu.VMEM(in_shape, low_type),
+            pltpu.VMEM(down_shape, low_type),
+            dma((4,)),
+            dma((4,)),
         ],
-    )(core_word, after_cross, gain_rows, cotangent, weight_in, down_source)
-
+    )(core_word, normed_three, normed_theirs, cotangent, cotangent_theirs, *ffn_weights)
+    pull_theirs = swap_with(pull_other, 2, devices)
     if not direct:
-        whole = jnp.concatenate([down_mine, down_other], axis=0).reshape(devices // 2, 2, rows_down, model)
-        down_mine, down_other = (
-            lax.dynamic_index_in_dim(whole, place, 1, keepdims=False).reshape(-1, model) for place in (core, 1 - core)
+        in_parts = ffn_grad.reshape(2, chip_groups, 4 * rows_in, model)
+        down_parts = ffn_other.reshape(chip_groups, 2, rows_down, model).swapaxes(0, 1)
+        both = jnp.concatenate([in_parts, down_parts], axis=2)
+        ffn_grad, ffn_other = (
+            lax.dynamic_index_in_dim(both, place, 0, keepdims=False) for place in (core, 1 - core)
         )
-    summed_down = scatter_bits(core_sum(down_mine, down_other, devices), backward_orders[0], me, devices)
-    in_chip = scatter_bits(core_sum(in_mine, in_other, devices), backward_orders[1], me, devices)
-    summed_in = jnp.concatenate(core_rows(in_chip, core, devices), axis=1)
-
-    grad_shapes = tuple(shaped((model, model), low_type) for n in range(4))
-    (grad_after_self, gain_grads, encoded_grad, *cross_grads) = call(
-        cross_backward_kernel,
-        "cross_backward",
-        25_000_000_000,
-        [SMEM, SMEM, SMEM] + [VMEM] * 6 + [HBM] + [VMEM] * 3 + [HBM] * 4,
-        [VMEM] * 2 + [HBM] * 5,
+    ffn_theirs = swap_with(ffn_other, 1, devices)
+    pull_theirs, ffn_theirs = barrier((pull_theirs, ffn_theirs))
+    out_theirs = swap_with(out_other, 2, devices)
+    high_bits = [bit for bit in sorted(chip_bits, reverse=True) if bit > 1]
+
+    def group_source(array):
+        return (array.reshape((2,) * len(high_bits) + array.shape[-2:]), high_bits, 0)
+
+    ffn_sum = sum_over([([group_source(ffn_grad), group_source(ffn_theirs)], (0, model))], 2, [], me, devices)
+
+    all_bits = sorted(chip_bits, reverse=True)
+
+    def chips_of(array):
+        return array.reshape((2,) * len(all_bits) + (array.shape[0] >> len(all_bits), array.shape[-1]))
+
+    def entry_of(mine, theirs, begin, end):
+        return ([(chips_of(mine), all_bits, 0), (chips_of(theirs), all_bits, 0)], (begin, end))
+
+    def first_sum(sides):
+        return [sum_over(entries, order[0], [], me, devices) for entries, order in zip(sides, pair_orders)]
+
+    def second_sum(sides):
+        return [sum_over(entries, order[1], order[:1], me, devices) for entries, order in zip(sides, pair_orders)]
+
+    def received(sides):
+        return [entries[0][0][-1][0] for entries in sides]
+
+    def with_received(sides, arrays):
+        return [
+            [(sources[:-1] + [(array,) + sources[-1][1:]], columns) for sources, columns in entries]
+            for entries, array in zip(sides, arrays)
+        ]
+
+    grads_shape = shaped((model, model), low_type)
+    rows_kept = pltpu.VMEM(encoded.shape, low_type)
+    two_kept = pltpu.VMEM((2, 2, model, half), low_type)
+    grad_after_cross, ffn_gain_grad, grad_context, pulled, late_mine, late_other = call(
+        cross_backward_first,
+        "cross_backward_first",
+        1_000_000_000,
+        [SMEM] + [VMEM] * 7 + [HBM] * 2,
+        [VMEM] * 4 + [HBM] * 2,
         (
             shaped((count, model), wide_type),
             shaped((8, model), wide_type),
-            shaped(encoded.shape, wide_type),
-        )
-        + grad_shapes,
-        [
-            pltpu.VMEM(encoded.shape, low_type),
-            pltpu.VMEM(per_token, low_type),
-            pltpu.VMEM(per_token, low_type),
-            pltpu.VMEM((2, encoder_count // segs, model), wide_type),
-            weights_kept,
-            weights_kept,
-            dma((segs,)),
-            dma((2,)),
-            dma((8,)),
-            dma((8,)),
-        ],
+            shaped((count, model), low_type),
+            shaped(per_token, low_type),
+            grads_shape,
+            grads_shape,
+        ),
+        [two_kept, two_kept, dma((4,)), dma((4,))],
+    )(
+        core_word, after_cross, gain_rows, cotangent, pull_mine, pull_theirs, context_two, mixed, *cross_weights[1]
+    )
+    late_theirs = swap_with(late_other, 1, devices)
+    block_out = low(after_cross + (out_mine + out_theirs.astype(wide_type)))
+    grad_after_self, gain_grads, score_grads, early_mine, early_other = call(
+        cross_backward_second,
+        "cross_backward_second",
+        3_000_000_000,
+        [SMEM, SMEM, SMEM] + [VMEM] * 5 + [HBM] + [VMEM] * 2 + [HBM] * 2,
+        [VMEM] * 3 + [HBM] * 2,
+        (
+            shaped((count, model), wide_type),
+            shaped((8, model), wide_type),
+            shaped(probs_shape, low_type),
+            grads_shape,
+            grads_shape,
+        ),
+        [rows_kept, pltpu.VMEM(per_token, low_type), two_kept, two_kept, dma((segs,)), dma((4,)), dma((4,))],
     )(
         core_word, segment_ids, passage_group, grad_after_cross, after_self, gain_rows, ffn_gain_grad,
-        queries_two, context_two, encoded, probs, mixed, spread, *cross_flat,
-    )
-
-    def reduce_group(grads):
-        answers = []
-        for side, order in enumerate(backward_orders):
-            mine, other = grads[2 * side], grads[2 * side + 1]
-            total = scatter_bits(core_sum(mine, other, devices), order, me, devices)
-            pair = core_rows(total, core, devices)
-            answers += [
-                jnp.concatenate([piece[:, n * half : (n + 1) * half] for piece in pair], axis=1) for n in range(2)
-            ]
-            if mine.shape[1] > model:
-                answers.append(jnp.where(core == 0, pair[0][:, model:], pair[1][:, model:]))
-        return answers
-
-    summed_cq, summed_ck, summed_cv, summed_co = reduce_group(cross_grads)
-
-    with_gains = shaped((model, model + PAIR), low_type)
-    (tokens_grad, *self_grads) = call(
+        queries_two, encoded, probs, pulled, *cross_weights[0],
+    )
+    arrays, grad_after_self, early_mine, early_other = barrier(
+        (received([ffn_sum]), grad_after_self, early_mine, early_other)
+    )
+    ffn_sum = with_received([ffn_sum], arrays)[0]
+    ffn_done = [2]
+    for bit in sorted(line_bits)[:-1]:
+        ffn_sum = sum_over(ffn_sum, bit, ffn_done, me, devices)
+        ffn_done = ffn_done + [bit]
+    early_theirs = swap_with(early_other, 1, devices)
+
+    with_gains = shaped((model, 2 * model + PAIR), low_type)
+    tokens_grad, self_mine, self_other = call(
         self_backward_kernel,
         "self_backward",
         2 * count * model * model * 10,
         [SMEM] + [VMEM] * 7 + [HBM] * 4,
-        [VMEM] + [HBM] * 4,
-        (shaped((count, model), wide_type), with_gains, with_gains, grad_shapes[0], grad_shapes[0]),
+        [VMEM] + [HBM] * 2,
+        (shaped((count, model), wide_type), with_gains, with_gains),
         [weights_kept, weights_kept, pltpu.VMEM((model, PAIR), low_type), dma((8,)), dma((10,))],
     )(
         core_word, segment_ids, tokens, gain_rows, grad_after_self, gain_grads, projected, context_one,
         *self_flat,
     )
-    summed_query, summed_key, own_gains, summed_value, summed_out = reduce_group(self_grads)
+    arrays, late_theirs, early_theirs, self_mine, self_other = barrier(
+        (received([ffn_sum]), late_theirs, early_theirs, self_mine, self_other)
+    )
+    ffn_sum = with_received([ffn_sum], arrays)[0]
+    ffn_sum = sum_over(ffn_sum, max(line_bits), ffn_done, me, devices)
+    self_theirs = swap_with(self_other, 1, devices)
+    crossed = [
+        [entry_of(late_mine, late_theirs, *cut), entry_of(early_mine, early_theirs, *cut)]
+        for cut in ((0, half), (half, model))
+    ]
+    crossed = first_sum(crossed)
+    self_theirs, score_grads = barrier((self_theirs, score_grads))
+    attention = [
+        [entry_of(self_mine, self_theirs, *cut)] for cut in ((0, model), (model, 2 * model + PAIR))
+    ]
+    attention = first_sum(attention)
+    encoded_grad = call(
+        rows_backward_kernel,
+        "rows_backward",
+        3_000_000_000,
+        [SMEM, SMEM] + [VMEM] * 4,
+        HBM,
+        shaped(encoded.shape, wide_type),
+        [pltpu.VMEM((2, encoder_count // segs, model), wide_type), dma((2,))],
+    )(segment_ids, passage_group, score_grads, probs, spread, pulled)
+    crossed_arrays, arrays, ffn_arrays, encoded_grad = barrier(
+        (received(crossed), received(attention), received([ffn_sum]), encoded_grad)
+    )
+    ffn_sum = with_received([ffn_sum], ffn_arrays)[0]
+    ffn_rows = summed(ffn_sum[0], {bit: bit_of(me, bit) for bit in high_bits})
+    summed_down = ffn_rows[4 * rows_in :]
+    in_parts = ffn_rows[: 4 * rows_in].reshape(2, 2, rows_in, model)
+    in_parts = exchange(lambda mask: block_for(in_parts, mask), group_bits, me, devices)
+    in_parts = in_parts.reshape(2, 2, rows_in, chip_groups // 2, 2 * rows_down)
+    summed_in = in_parts.transpose(2, 1, 3, 0, 4).reshape(rows_in, hidden_units)
+    crossed, attention = with_received(crossed, crossed_arrays), with_received(attention, arrays)
+    attention = second_sum([crossed[side] + attention[side] for side in range(2)])
+    found = sum_line([attention[0] + attention[1]], line_bits, [2, 1], me, devices)
+    pair = core_rows(found, core, devices)
+    (
+        summed_cv, summed_cq, summed_query, summed_key, summed_co, summed_ck, summed_value, summed_out,
+    ) = (
+        jnp.concatenate([piece[:, n * half : (n + 1) * half] for piece in pair], axis=1) for n in range(8)
+    )
+    own_gains = jnp.where(core == 0, pair[0][:, 8 * half :], pair[1][:, 8 * half :])
     return (
         block_out,
         tokens_grad,

time: 382 us -> 327 us (0.86)
  waiting for transfers between devices: 155 us -> 101 us
  other arithmetic: 19.3 us -> 46.9 us
  between operations: 15.7 us -> 1.48 us
  starting transfers between devices: 67.7 us -> 54 us
  Pallas kernels: 98.8 us -> 109 us
  local copies, waits for them, and re-layouts: 18.8 us -> 9.35 us
    ppermute x59 -> x50, waiting for transfers between devices: 155 us -> 101 us  [swap_with(): return lax.ppermute(piece, AXES, pairs)]
    convert_element_type x6 -> x13, other arithmetic: 6.29 us -> 20.4 us  [low(): return values.astype(jnp.bfloat16)]
    ppermute x59 -> x50, starting transfers between devices: 67.7 us -> 54 us  [swap_with(): return lax.ppermute(piece, AXES, pairs)]
    pallas_call x2 -> x5, Pallas kernels: 54.6 us -> 67.4 us  [the longest x1 27 us: per_device(): call(cross_backward_second, 'cross_backward_second', 3000000000, [SMEM, S...]
    unnamed x0 -> x10, other arithmetic: none -> 9.36 us
    unnamed x39 -> x34, local copies, waits for them, and re-layouts: 6.89 us -> 1.41 us
    concatenate x13 -> x16, other arithmetic: 5.87 us -> 9.29 us  [the longest x8 5.1 us: per_device(): jnp.concatenate([piece[:, n * half:(n + 1) * half] for piece in pair], ax...]
  transfers between devices with their start and end apart: 60 -> 50, of which waited for: 31 -> 19; matrix products, arithmetic and copies ran while one was open for 7% -> 12% of each run, Pallas kernels for 12% -> 30%
where the time goes in v3:
time: 327 us; the launch traced here: 322 us
  Pallas kernels  109 us (33%)
  waiting for transfers between devices  101 us (31%)
  starting transfers between devices  54 us (17%)
  other arithmetic  46.9 us (14%)
  local copies, waits for them, and re-layouts  9.35 us (3%)
    ppermute x50, waiting for transfers between devices, swap_with(): return lax.ppermute(piece, AXES, pairs)  101 us
    ppermute x50, starting transfers between devices, swap_with(): return lax.ppermute(piece, AXES, pairs)  54 us
    pallas_call x1, Pallas kernels, per_device(): call(cross_backward_second, 'cross_backward_second', 3000000000, [SMEM, S...  27 us
    pallas_call x1, Pallas kernels, per_device(): call(cross_forward_kernel, 'cross_forward', 12000000000, [SMEM, SMEM, SME...  25.3 us
    convert_element_type x13, other arithmetic, low(): return values.astype(jnp.bfloat16)  20.4 us
    pallas_call x1, Pallas kernels, per_device(): call(rows_backward_kernel, 'rows_backward', 3000000000, [SMEM, SMEM] + [V...  19.7 us
    pallas_call x1, Pallas kernels, per_device(): call(self_backward_kernel, 'self_backward', 2 * count * model * model * 1...  11.2 us
    pallas_call x1, Pallas kernels, per_device(): call(functools.partial(ffn_kernel, direct), 'ffn', 4000000000, [SMEM] + [...  10.6 us
  transfers between devices with their start and end apart: 50, of which 19 were waited for; matrix products, arithmetic and copies ran while one was open for 12% of the time, Pallas kernels for 30%

profile of v3, /device:TPU:0, one launch (start us, length us, event | category | flops | bytes accessed | tf_op | source)
XLA Modules:
  0.0 322.2 jit_solution(2554528522107977378)
XLA Ops:
  6.4 3.0 collective-permute-start.1
  9.4 2.6 collective-permute-start.2
  12.6 4.0 %collective-permute-done.1 = bf16[48,1664]{1,0:T(8,128)(2,1)S(1)} collective-permute-done((bf16[48,1664]{1,0:T(8,128)(2,1)S(1)}, bf16[48,1664]{1,0:T(8,128)(2,1)S(1)}, u32[]{:S(2)}, u32[]{:S(2)}) %collective-permute-start.1) | collective-permute-done | bytes 159776 | tf_op jit(solution)/shard_map/ppermute | solution.py:573
  16.6 7.6 %collective-permute-done.2 = bf16[48,1664]{1,0:T(8,128)(2,1)S(1)} collective-permute-done((bf16[48,1664]{1,0:T(8,128)(2,1)S(1)}, bf16[48,1664]{1,0:T(8,128)(2,1)S(1)}, u32[]{:S(2)}, u32[]{:S(2)}) %collective-permute-start.2) | collective-permute-done | bytes 159776 | tf_op jit(solution)/shard_map/ppermute | solution.py:573
  26.7 2.9 collective-permute-start.6
  35.8 7.8 %collective-permute-done.7 = bf16[48,1536]{1,0:T(8,128)(2,1)S(1)} collective-permute-done((bf16[48,1536]{1,0:T(8,128)(2,1)S(1)}, bf16[48,1536]{1,0:T(8,128)(2,1)S(1)}, u32[]{:S(2)}, u32[]{:S(2)}) %collective-permute-start.7) | collective-permute-done | bytes 147488 | tf_op jit(solution)/shard_map/ppermute | solution.py:573
  44.0 3.5 %collective-permute-start.14 = (bf16[192,768]{1,0:T(8,128)(2,1)S(1)}, bf16[192,768]{1,0:T(8,128)(2,1)S(1)}, u32[]{:S(2)}, u32[]{:S(2)}) collective-permute-start(bf16[192,768]{1,0:T(8,128)(2,1)S(1)} %pad_maximum_fusion.18), channel_id=1, source_target_pairs={{0,16},{1,17},{2,18},{3,19},{4,20},{5,21},{6,22},{7,23},{8,24},{9,... | collective-permute-start | bytes 884744 | tf_op jit(solution)/shard_map/ppermute | solution.py:573
  51.7 8.3 %collective-permute-done.14 = bf16[192,768]{1,0:T(8,128)(2,1)S(1)} collective-permute-done((bf16[192,768]{1,0:T(8,128)(2,1)S(1)}, bf16[192,768]{1,0:T(8,128)(2,1)S(1)}, u32[]{:S(2)}, u32[]{:S(2)}) %collective-permute-start.14) | collective-permute-done | bytes 294944 | tf_op jit(solution)/shard_map/ppermute | solution.py:573
  60.4 8.8 %collective-permute-done.15 = bf16[4,2,48,768]{3,2,0,1:T(8,128)(2,1)S(1)} collective-permute-done((bf16[4,2,48,768]{3,2,0,1:T(8,128)(2,1)S(1)}, bf16[4,2,48,768]{3,2,0,1:T(8,128)(2,1)S(1)}, u32[]{:S(2)}, u32[]{:S(2)}) %collective-permute-start.15) | collective-permute-done | bytes 589856 | tf_op jit(solution)/shard_map/ppermute | solution.py:573
  76.3 7.2 %collective-permute-done.18 = bf16[4,2,48,768]{3,2,0,1:T(8,128)(2,1)} collective-permute-done((bf16[4,2,48,768]{3,2,0,1:T(8,128)(2,1)S(1)}, bf16[4,2,48,768]{3,2,0,1:T(8,128)(2,1)}, u32[]{:S(2)}, u32[]{:S(2)}) %collective-permute-start.18) | collective-permute-done | bytes 589856 | tf_op jit(solution)/shard_map/ppermute | solution.py:573
  84.9 5.6 %collective-permute-done.17 = bf16[4,2,48,768]{3,2,0,1:T(8,128)(2,1)} collective-permute-done((bf16[4,2,48,768]{3,2,0,1:T(8,128)(2,1)S(1)}, bf16[4,2,48,768]{3,2,0,1:T(8,128)(2,1)}, u32[]{:S(2)}, u32[]{:S(2)}) %collective-permute-start.17) | collective-permute-done | bytes 589856 | tf_op jit(solution)/shard_map/ppermute | solution.py:573
  92.9 2.7 collective-permute-done.19
  95.9 5.2 %self_forward.1 = (bf16[3,128,768]{2,1,0:T(8,128)(2,1)}, bf16[128,768]{1,0:T(8,128)(2,1)}, f32[128,768]{1,0:T(8,128)}) custom-call(s32[1]{0:T(128)} %bitcast.core_ref, s32[1,128]{1,0:T(1,128)} %ids.9, bf16[128,768]{1,0:T(8,128)(2,1)} %tokens.3, f32[8,768]{1,0:T(8,128)} %copy.122.gains, bf16[768,768]{1,0:T(8,128)(2,1)} %bitcast.569, ...), custom_call_target="tpu_custom_call" | custom-call | flops 754974720 | bytes 1000000 | tf_op jit(solution)/shard_map/self_forward/pallas_call | solution.py:808
  105.8 25.3 %cross_forward.1 = (bf16[128,768]{1,0:T(8,128)(2,1)}, bf16[128,768]{1,0:T(8,128)(2,1)}, f32[128,768]{1,0:T(8,128)}, bf16[128,768]{1,0:T(8,128)(2,1)}, bf16[12,12...) custom-call(s32[1]{0:T(128)} %bitcast.core_ref, s32[1,128]{1,0:T(1,128)} %ids.9, ...), custom_call_target="tpu_custom_call" | custom-call | flops 12000000000 | bytes 1000000 | tf_op jit(solution)/shard_map/cross_forward/pallas_call | solution.py:831
  133.4 2.0 collective-permute-start.26
  135.4 5.4 %collective-permute-done.26.normed_theirs = bf16[128,768]{1,0:T(8,128)(2,1)S(1)} collective-permute-done((bf16[128,768]{1,0:T(8,128)(2,1)S(1)}, bf16[128,768]{1,0:T(8,128)(2,1)S(1)}, u32[]{:S(2)}, u32[]{:S(2)}) %collective-permute-start.26) | collective-permute-done | bytes 196640 | tf_op jit(solution)/shard_map/ppermute | solution.py:573
  141.5 10.6 %ffn.1 = (f32[128,768]{1,0:T(8,128)}, bf16[128,768]{1,0:T(8,128)(2,1)}, f32[128,768]{1,0:T(8,128)}, bf16[128,768]{1,0:T(8,128)(2,1)}, bf16[8,192,768]{2,1,0:T(8,128)(2,1)}, /*index=5*/bf16[8,192,768]{2,1,0:T(8,128)(2,1)}) custom-call(s32[1]{0:T(128)} %bitcast.core_ref, bf16[128,768]{1,0:T(8,128)(2,1)} %get-tuple-element.106.normed, ...), custom_call_target="tpu_custom_call" | custom-call | flops 4000000000 | bytes 1000000 | tf_op jit(solution)/shard_map/ffn/pallas_call | solution.py:868
  153.8 5.9 %collective-permute-done.29.pull_theirs = bf16[128,768]{1,0:T(8,128)(2,1)S(1)} collective-permute-done((bf16[128,768]{1,0:T(8,128)(2,1)}, bf16[128,768]{1,0:T(8,128)(2,1)S(1)}, u32[]{:S(2)}, u32[]{:S(2)}) %collective-permute-start.29) | collective-permute-done | bytes 196640 | tf_op jit(solution)/shard_map/ppermute | solution.py:573
  160.4 2.8 fusion
  164.7 8.5 %cross_backward_first.1 = (f32[128,768]{1,0:T(8,128)}, f32[8,768]{1,0:T(8,128)}, bf16[128,768]{1,0:T(8,128)(2,1)}, bf16[12,128,768]{2,1,0:T(8,128)(2,1)}, bf16[7...) custom-call(s32[1]{0:T(128)} %bitcast.core_ref, f32[128,768]{1,0:T(8,128)} %get-tuple-element.103.after_cross, ...), custom_call_target="tpu_custom_call" | custom-call | flops 1000000000 | bytes 1000000 | tf_op jit(solution)/shard_map/cross_backward_first/pallas_call | solution.py:928
  173.3 27.0 %cross_backward_second.1 = (f32[128,768]{1,0:T(8,128)}, f32[8,768]{1,0:T(8,128)}, bf16[12,128,1024]{2,1,0:T(8,128)(2,1)}, bf16[768,768]{1,0:T(8,128)(2,1)}, bf16[768,768]{1,0:T(8,128)(2,1)}) custom-call(s32[1]{0:T(128)} %bitcast.core_ref, s32[1,128]{1,0:T(1,128)} %ids.9, s32[1,4]{1,0:T(1,128)} %groups.5, f32[128,768]{1,0:T(8,128)} %get-tuple-element.119.grad_after, ...), custom_call_target="tpu_custom_call" | custom-call | flops 3000000000 | bytes 1000000 | tf_op jit(solution)/shard_map/cross_backward_second/pallas_call | solution.py:948
  202.2 2.1 fusion.1
  204.4 11.2 %self_backward.1 = (f32[128,768]{1,0:T(8,128)}, bf16[768,1664]{1,0:T(8,128)(2,1)}, bf16[768,1664]{1,0:T(8,128)(2,1)}) custom-call(s32[1]{0:T(128)} %bitcast.core_ref, s32[1,128]{1,0:T(1,128)} %ids.9, bf16[128,768]{1,0:T(8,128)(2,1)} %tokens.3, f32[8,768]{1,0:T(8,128)} %copy.122.gains, f32[128,768]{1,0:T(8,128)} %get-tuple-element.127.grad_after, ...), custom_call_target="tpu_custom_call" | custom-call | flops 1509949440 | bytes 1000000 | tf_op jit(solution)/shard_map/self_backward/pallas_call | solution.py:977
  215.7 4.5 %collective-permute-done.32 = bf16[2,192,768]{2,1,0:T(8,128)(2,1)} collective-permute-done((bf16[2,192,768]{2,1,0:T(8,128)(2,1)}, bf16[2,192,768]{2,1,0:T(8,128)(2,1)}, u32[]{:S(2)}, u32[]{:S(2)}) %collective-permute-start.32) | collective-permute-done | bytes 589856 | tf_op jit(solution)/shard_map/ppermute | solution.py:573
  229.1 2.1 fusion.2
  232.5 2.0 fusion.4
  236.0 2.1 fusion.7
  239.6 19.7 %rows_backward.1 = f32[4096,768]{1,0:T(8,128)} custom-call(s32[1,128]{1,0:T(1,128)} %ids.9, s32[1,4]{1,0:T(1,128)} %groups.5, bf16[12,128,1024]{2,1,0:T(8,128)(2,1)} %get-tuple-element.146.score_grads, bf16[12,128,1024]{2,1,0:T(8,128)(2,1)} %get-tuple-element.122.probs_ref, bf16[12,128,768]{2,1,0:T(8,128)(2,1)} %get-tuple-element.147.spread, ...), custom_call_target="tpu_custom_call" | custom-call | flops 3000000000 | bytes 1000000 | tf_op jit(solution)/shard_map/rows_backward/pallas_call | solution.py:1005
  269.7 10.6 %collective-permute-done.41 = bf16[2,2,48,1536]{3,2,1,0:T(8,128)(2,1)S(1)} collective-permute-done((bf16[2,2,48,1536]{3,2,1,0:T(8,128)(2,1)S(1)}, bf16[2,2,48,1536]{3,2,1,0:T(8,128)(2,1)S(1)}, u32[]{:S(2)}, u32[]{:S(2)}) %collective-permute-start.41) | collective-permute-done | bytes 589856 | tf_op jit(solution)/shard_map/ppermute | solution.py:573
  291.6 2.2 collective-permute-start.45
  296.4 5.5 %collective-permute-done.43 = bf16[48,3200]{1,0:T(8,128)(2,1)S(1)} collective-permute-done((bf16[48,3200]{1,0:T(8,128)(2,1)S(1)}, bf16[48,3200]{1,0:T(8,128)(2,1)S(1)}, u32[]{:S(2)}, u32[]{:S(2)}) %collective-permute-start.43) | collective-permute-done | bytes 307232 | tf_op jit(solution)/shard_map/ppermute | solution.py:573
  302.0 12.2 %collective-permute-done.44 = bf16[48,3200]{1,0:T(8,128)(2,1)S(1)} collective-permute-done((bf16[48,3200]{1,0:T(8,128)(2,1)S(1)}, bf16[48,3200]{1,0:T(8,128)(2,1)S(1)}, u32[]{:S(2)}, u32[]{:S(2)}) %collective-permute-start.44) | collective-permute-done | bytes 307232 | tf_op jit(solution)/shard_map/ppermute | solution.py:573
  (211 shorter events, 89.5 us)
Async XLA Ops:
  9.4 14.7 %collective-permute-start.2 = (bf16[48,1664]{1,0:T(8,128)(2,1)S(1)}, bf16[48,1664]{1,0:T(8,128)(2,1)S(1)}, u32[]{:S(2)}, u32[]{:S(2)}) collective-permute-start(bf16[48,1664]{1,0:T(8,128)(2,1)S(1)} %pad_maximum_fusion.20), channel_id=1, source_target_pairs={{0,16},{1,17},{2,18},{3,19},{4,20},{5,21},{6,22},{7,23},{8,24},{9,... | collective-permute-start | bytes 479240 | tf_op jit(solution)/shard_map/ppermute | solution.py:573
  12.0 12.2 %collective-permute-start.3 = (bf16[48,1664]{1,0:T(8,128)(2,1)S(1)}, bf16[48,1664]{1,0:T(8,128)(2,1)S(1)}, u32[]{:S(2)}, u32[]{:S(2)}) collective-permute-start(bf16[48,1664]{1,0:T(8,128)(2,1)S(1)} %pad_maximum_fusion.20), channel_id=1, source_target_pairs={{0,24},{1,25},{2,26},{3,27},{4,28},{5,29},{6,30},{7,31},{8,16},{9,... | collective-permute-start | bytes 479240 | tf_op jit(solution)/shard_map/ppermute | solution.py:573
  29.6 14.0 %collective-permute-start.7 = (bf16[48,1536]{1,0:T(8,128)(2,1)S(1)}, bf16[48,1536]{1,0:T(8,128)(2,1)S(1)}, u32[]{:S(2)}, u32[]{:S(2)}) collective-permute-start(bf16[48,1536]{1,0:T(8,128)(2,1)S(1)} %get-tuple-element.88), channel_id=1, source_target_pairs={{0,16},{1,17},{2,18},{3,19},{4,20},{5,21},{6,22},{7,23},{8,24},{9,... | collective-permute-start | bytes 442376 | tf_op jit(solution)/shard_map/ppermute | solution.py:573
  30.7 12.9 %collective-permute-start.8 = (bf16[48,1536]{1,0:T(8,128)(2,1)S(1)}, bf16[48,1536]{1,0:T(8,128)(2,1)S(1)}, u32[]{:S(2)}, u32[]{:S(2)}) collective-permute-start(bf16[48,1536]{1,0:T(8,128)(2,1)S(1)} %get-tuple-element.88), channel_id=1, source_target_pairs={{0,24},{1,25},{2,26},{3,27},{4,28},{5,29},{6,30},{7,31},{8,16},{9,... | collective-permute-start | bytes 442376 | tf_op jit(solution)/shard_map/ppermute | solution.py:573
  44.0 16.0 %collective-permute-start.14 = (bf16[192,768]{1,0:T(8,128)(2,1)S(1)}, bf16[192,768]{1,0:T(8,128)(2,1)S(1)}, u32[]{:S(2)}, u32[]{:S(2)}) collective-permute-start(bf16[192,768]{1,0:T(8,128)(2,1)S(1)} %pad_maximum_fusion.18), channel_id=1, source_target_pairs={{0,16},{1,17},{2,18},{3,19},{4,20},{5,21},{6,22},{7,23},{8,24},{9,... | collective-permute-start | bytes 884744 | tf_op jit(solution)/shard_map/ppermute | solution.py:573
  47.6 12.5 %collective-permute-start.12 = (bf16[4,48,768]{2,1,0:T(8,128)(2,1)S(1)}, bf16[4,48,768]{2,1,0:T(8,128)(2,1)S(1)}, u32[]{:S(2)}, u32[]{:S(2)}) collective-permute-start(bf16[4,48,768]{2,1,0:T(8,128)(2,1)S(1)} %get-tuple-element.214), channel_id=1, source_target_pairs={{0,4},{1,5},{2,6},{3,7},{4,0},{5,1},{6,2},{7,3},{8,12},{9,13},{10,... | collective-permute-start | bytes 884744 | tf_op jit(solution)/shard_map/ppermute | solution.py:573
  50.7 19.4 %collective-permute-start.16 = (bf16[4,2,48,896]{3,2,1,0:T(8,128)(2,1)S(1)}, bf16[4,2,48,896]{3,2,1,0:T(8,128)(2,1)S(1)}, u32[]{:S(2)}, u32[]{:S(2)}) collective-permute-start(bf16[4,2,48,896]{3,2,1,0:T(8,128)(2,1)S(1)} %pad_maximum_fusion.6), channel_id=1, source_target_pairs={{0,4},{1,5},{2,6},{3,7},{4,0},{5,1},{6,2},{7,3},{8,12},{9,13},{10,... | collective-permute-start | bytes 2064392 | tf_op jit(solution)/shard_map/ppermute | solution.py:573
  51.2 17.9 %collective-permute-start.15 = (bf16[4,2,48,768]{3,2,0,1:T(8,128)(2,1)S(1)}, bf16[4,2,48,768]{3,2,0,1:T(8,128)(2,1)S(1)}, u32[]{:S(2)}, u32[]{:S(2)}) collective-permute-start(bf16[4,2,48,768]{3,2,0,1:T(8,128)(2,1)S(1)} %pad_maximum_fusion.9), channel_id=1, source_target_pairs={{0,2},{1,3},{2,0},{3,1},{4,6},{5,7},{6,4},{7,5},{8,10},{9,11},{10,... | collective-permute-start | bytes 1769480 | tf_op jit(solution)/shard_map/ppermute | solution.py:573
  70.3 13.2 %collective-permute-start.18 = (bf16[4,2,48,768]{3,2,0,1:T(8,128)(2,1)S(1)}, bf16[4,2,48,768]{3,2,0,1:T(8,128)(2,1)}, u32[]{:S(2)}, u32[]{:S(2)}) collective-permute-start(bf16[4,2,48,768]{3,2,0,1:T(8,128)(2,1)S(1)} %get-tuple-element.95), channel_id=1, source_target_pairs={{0,4},{1,5},{2,6},{3,7},{4,0},{5,1},{6,2},{7,3},{8,12},{9,13},{10,... | collective-permute-start | bytes 1769480 | tf_op jit(solution)/shard_map/ppermute | solution.py:573
  71.9 29.2 %collective-permute-start.22 = (bf16[128,768]{1,0:T(8,128)(2,1)}, bf16[128,768]{1,0:T(8,128)(2,1)}, u32[]{:S(2)}, u32[]{:S(2)}) collective-permute-start(bf16[128,768]{1,0:T(8,128)(2,1)} %cotangent.3), channel_id=1, source_target_pairs={{0,2},{1,3},{2,0},{3,1},{4,6},{5,7},{6,4},{7,5},{8,10},{9,11},{10,... | collective-permute-start | bytes 589832 | tf_op jit(solution)/shard_map/ppermute | solution.py:573
  74.5 21.4 %collective-permute-start.21 = (bf16[768,768]{1,0:T(8,128)(2,1)}, bf16[768,768]{1,0:T(8,128)(2,1)}, u32[]{:S(2)}, u32[]{:S(2)}) collective-permute-start(bf16[768,768]{1,0:T(8,128)(2,1)} %slice.104), channel_id=1, source_target_pairs={{0,1},{1,0},{2,3},{3,2},{4,5},{5,4},{6,7},{7,6},{8,9},{9,8},{10,11... | collective-permute-start | bytes 3538952 | tf_op jit(solution)/shard_map/ppermute | solution.py:573
  74.5 21.4 %collective-permute-start.20 = (bf16[768,768]{1,0:T(8,128)(2,1)S(1)}, bf16[768,768]{1,0:T(8,128)(2,1)}, u32[]{:S(2)}, u32[]{:S(2)}) collective-permute-start(bf16[768,768]{1,0:T(8,128)(2,1)S(1)} %bitcast.568), channel_id=1, source_target_pairs={{0,1},{1,0},{2,3},{3,2},{4,5},{5,4},{6,7},{7,6},{8,9},{9,8},{10,11... | collective-permute-start | bytes 3538952 | tf_op jit(solution)/shard_map/ppermute | solution.py:573
  75.0 15.5 %collective-permute-start.17 = (bf16[4,2,48,768]{3,2,0,1:T(8,128)(2,1)S(1)}, bf16[4,2,48,768]{3,2,0,1:T(8,128)(2,1)}, u32[]{:S(2)}, u32[]{:S(2)}) collective-permute-start(bf16[4,2,48,768]{3,2,0,1:T(8,128)(2,1)S(1)} %get-tuple-element.94), channel_id=1, source_target_pairs={{0,2},{1,3},{2,0},{3,1},{4,6},{5,7},{6,4},{7,5},{8,10},{9,11},{10,... | collective-permute-start | bytes 1769480 | tf_op jit(solution)/shard_map/ppermute | solution.py:573
  101.6 29.5 %collective-permute-start.25 = (bf16[2,2,192,768]{3,2,0,1:T(8,128)(2,1)S(1)}, bf16[2,2,192,768]{3,2,0,1:T(8,128)(2,1)S(1)}, u32[]{:S(2)}, u32[]{:S(2)}) collective-permute-start(bf16[2,2,192,768]{3,2,0,1:T(8,128)(2,1)S(1)} %pad_maximum_fusion.5), channel_id=1, source_target_pairs={{0,4},{1,5},{2,6},{3,7},{4,0},{5,1},{6,2},{7,3},{8,12},{9,13},{10,... | collective-permute-start | bytes 3538952 | tf_op jit(solution)/shard_map/ppermute | solution.py:573
  163.2 37.1 %collective-permute-start.31 = (bf16[2,2,192,768]{3,2,1,0:T(8,128)(2,1)}, bf16[2,2,192,768]{3,2,1,0:T(8,128)(2,1)S(1)}, u32[]{:S(2)}, u32[]{:S(2)}) collective-permute-start(bf16[2,2,192,768]{3,2,1,0:T(8,128)(2,1)} %fusion), channel_id=1, source_target_pairs={{0,4},{1,5},{2,6},{3,7},{4,0},{5,1},{6,2},{7,3},{8,12},{9,13},{10,... | collective-permute-start | bytes 3538952 | tf_op jit(solution)/shard_map/ppermute | solution.py:573
  173.2 42.5 %collective-permute-start.33 = (bf16[768,768]{1,0:T(8,128)(2,1)}, bf16[768,768]{1,0:T(8,128)(2,1)}, u32[]{:S(2)}, u32[]{:S(2)}) collective-permute-start(bf16[768,768]{1,0:T(8,128)(2,1)} %get-tuple-element.134), channel_id=1, source_target_pairs={{0,1},{1,0},{2,3},{3,2},{4,5},{5,4},{6,7},{7,6},{8,9},{9,8},{10,11... | collective-permute-start | bytes 3538952 | tf_op jit(solution)/shard_map/ppermute | solution.py:573
  200.3 19.9 %collective-permute-start.34 = (bf16[768,768]{1,0:T(8,128)(2,1)}, bf16[768,768]{1,0:T(8,128)(2,1)}, u32[]{:S(2)}, u32[]{:S(2)}) collective-permute-start(bf16[768,768]{1,0:T(8,128)(2,1)} %get-tuple-element.135), channel_id=1, source_target_pairs={{0,1},{1,0},{2,3},{3,2},{4,5},{5,4},{6,7},{7,6},{8,9},{9,8},{10,11... | collective-permute-start | bytes 3538952 | tf_op jit(solution)/shard_map/ppermute | solution.py:573
  204.3 15.9 %collective-permute-start.32 = (bf16[2,192,768]{2,1,0:T(8,128)(2,1)}, bf16[2,192,768]{2,1,0:T(8,128)(2,1)}, u32[]{:S(2)}, u32[]{:S(2)}) collective-permute-start(bf16[2,192,768]{2,1,0:T(8,128)(2,1)} %fusion.1), channel_id=1, source_target_pairs={{0,8},{1,9},{2,10},{3,11},{4,12},{5,13},{6,14},{7,15},{8,0},{9,1},... | collective-permute-start | bytes 1769480 | tf_op jit(solution)/shard_map/ppermute | solution.py:573
  220.2 17.9 %collective-permute-start.28 = (bf16[128,768]{1,0:T(8,128)(2,1)S(1)}, bf16[128,768]{1,0:T(8,128)(2,1)S(1)}, u32[]{:S(2)}, u32[]{:S(2)}) collective-permute-start(bf16[128,768]{1,0:T(8,128)(2,1)S(1)} %copy-done.14), channel_id=1, source_target_pairs={{0,2},{1,3},{2,0},{3,1},{4,6},{5,7},{6,4},{7,5},{8,10},{9,11},{10,... | collective-permute-start | bytes 589832 | tf_op jit(solution)/shard_map/ppermute | solution.py:573
  224.6 34.8 %collective-permute-start.36 = (bf16[2,2,2,48,768]{4,3,2,1,0:T(8,128)(2,1)}, bf16[2,2,2,48,768]{4,3,2,1,0:T(8,128)(2,1)}, u32[]{:S(2)}, u32[]{:S(2)}) collective-permute-start(bf16[2,2,2,48,768]{4,3,2,1,0:T(8,128)(2,1)} %pad_maximum_fusion.15), channel_id=1, source_target_pairs={{0,2},{1,3},{2,0},{3,1},{4,6},{5,7},{6,4},{7,5},{8,10},{9,11},{10,... | collective-permute-start | bytes 1769480 | tf_op jit(solution)/shard_map/ppermute | solution.py:573
  228.6 30.8 %collective-permute-start.35 = (bf16[2,2,2,48,768]{4,3,2,1,0:T(8,128)(2,1)}, bf16[2,2,2,48,768]{4,3,2,1,0:T(8,128)(2,1)}, u32[]{:S(2)}, u32[]{:S(2)}) collective-permute-start(bf16[2,2,2,48,768]{4,3,2,1,0:T(8,128)(2,1)} %pad_maximum_fusion.14), channel_id=1, source_target_pairs={{0,4},{1,5},{2,6},{3,7},{4,0},{5,1},{6,2},{7,3},{8,12},{9,13},{10,... | collective-permute-start | bytes 1769480 | tf_op jit(solution)/shard_map/ppermute | solution.py:573
  231.3 28.1 %collective-permute-start.39 = (bf16[2,2,2,48,896]{4,3,2,1,0:T(8,128)(2,1)}, bf16[2,2,2,48,896]{4,3,2,1,0:T(8,128)(2,1)}, u32[]{:S(2)}, u32[]{:S(2)}) collective-permute-start(bf16[2,2,2,48,896]{4,3,2,1,0:T(8,128)(2,1)} %fusion.2), channel_id=1, source_target_pairs={{0,2},{1,3},{2,0},{3,1},{4,6},{5,7},{6,4},{7,5},{8,10},{9,11},{10,... | collective-permute-start | bytes 2064392 | tf_op jit(solution)/shard_map/ppermute | solution.py:573
  234.5 24.9 %collective-permute-start.38 = (bf16[2,2,2,48,768]{4,3,2,1,0:T(8,128)(2,1)}, bf16[2,2,2,48,768]{4,3,2,1,0:T(8,128)(2,1)}, u32[]{:S(2)}, u32[]{:S(2)}) collective-permute-start(bf16[2,2,2,48,768]{4,3,2,1,0:T(8,128)(2,1)} %fusion.4), channel_id=1, source_target_pairs={{0,4},{1,5},{2,6},{3,7},{4,0},{5,1},{6,2},{7,3},{8,12},{9,13},{10,... | collective-permute-start | bytes 1769480 | tf_op jit(solution)/shard_map/ppermute | solution.py:573
  238.1 21.3 %collective-permute-start.40 = (bf16[192,768]{1,0:T(8,128)(2,1)}, bf16[192,768]{1,0:T(8,128)(2,1)S(1)}, u32[]{:S(2)}, u32[]{:S(2)}) collective-permute-start(bf16[192,768]{1,0:T(8,128)(2,1)} %fusion.7), channel_id=1, source_target_pairs={{0,16},{1,17},{2,18},{3,19},{4,20},{5,21},{6,22},{7,23},{8,24},{9,... | collective-permute-start | bytes 884744 | tf_op jit(solution)/shard_map/ppermute | solution.py:573
  264.4 15.9 %collective-permute-start.41 = (bf16[2,2,48,1536]{3,2,1,0:T(8,128)(2,1)S(1)}, bf16[2,2,48,1536]{3,2,1,0:T(8,128)(2,1)S(1)}, u32[]{:S(2)}, u32[]{:S(2)}) collective-permute-start(bf16[2,2,48,1536]{3,2,1,0:T(8,128)(2,1)S(1)} %pad_maximum_fusion.16), channel_id=1, source_target_pairs={{0,2},{1,3},{2,0},{3,1},{4,6},{5,7},{6,4},{7,5},{8,10},{9,11},{10,... | collective-permute-start | bytes 1769480 | tf_op jit(solution)/shard_map/ppermute | solution.py:573
  266.1 48.3 %collective-permute-start.47 = (f32[24,768]{1,0:T(8,128)S(1)}, f32[24,768]{1,0:T(8,128)S(1)}, u32[]{:S(2)}, u32[]{:S(2)}) collective-permute-start(f32[24,768]{1,0:T(8,128)S(1)} %get-tuple-element.243), channel_id=1, source_target_pairs={{0,1},{1,0},{2,3},{3,2},{4,5},{5,4},{6,7},{7,6},{8,9},{9,8},{10,11... | collective-permute-start | bytes 221192 | tf_op jit(solution)/shard_map/ppermute | solution.py:573
  266.2 48.2 %collective-permute-start.48 = (f32[24,768]{1,0:T(8,128)S(1)}, f32[24,768]{1,0:T(8,128)S(1)}, u32[]{:S(2)}, u32[]{:S(2)}) collective-permute-start(f32[24,768]{1,0:T(8,128)S(1)} %get-tuple-element.245), channel_id=1, source_target_pairs={{0,2},{1,3},{2,0},{3,1},{4,6},{5,7},{6,4},{7,5},{8,10},{9,11},{10,... | collective-permute-start | bytes 221192 | tf_op jit(solution)/shard_map/ppermute | solution.py:573
  268.0 18.1 %collective-permute-start.42 = (bf16[2,2,48,1664]{3,2,1,0:T(8,128)(2,1)S(1)}, bf16[2,2,48,1664]{3,2,1,0:T(8,128)(2,1)S(1)}, u32[]{:S(2)}, u32[]{:S(2)}) collective-permute-start(bf16[2,2,48,1664]{3,2,1,0:T(8,128)(2,1)S(1)} %pad_maximum_fusion.8), channel_id=1, source_target_pairs={{0,4},{1,5},{2,6},{3,7},{4,0},{5,1},{6,2},{7,3},{8,12},{9,13},{10,... | collective-permute-start | bytes 1916936 | tf_op jit(solution)/shard_map/ppermute | solution.py:573
  289.4 12.6 %collective-permute-start.43 = (bf16[48,3200]{1,0:T(8,128)(2,1)S(1)}, bf16[48,3200]{1,0:T(8,128)(2,1)S(1)}, u32[]{:S(2)}, u32[]{:S(2)}) collective-permute-start(bf16[48,3200]{1,0:T(8,128)(2,1)S(1)} %get-tuple-element.157), channel_id=1, source_target_pairs={{0,8},{1,9},{2,10},{3,11},{4,12},{5,13},{6,14},{7,15},{8,0},{9,1},... | collective-permute-start | bytes 921608 | tf_op jit(solution)/shard_map/ppermute | solution.py:573
  289.9 24.3 %collective-permute-start.44 = (bf16[48,3200]{1,0:T(8,128)(2,1)S(1)}, bf16[48,3200]{1,0:T(8,128)(2,1)S(1)}, u32[]{:S(2)}, u32[]{:S(2)}) collective-permute-start(bf16[48,3200]{1,0:T(8,128)(2,1)S(1)} %get-tuple-element.159), channel_id=1, source_target_pairs={{0,16},{1,17},{2,18},{3,19},{4,20},{5,21},{6,22},{7,23},{8,24},{9,... | collective-permute-start | bytes 921608 | tf_op jit(solution)/shard_map/ppermute | solution.py:573
  291.6 22.6 %collective-permute-start.45 = (bf16[48,3200]{1,0:T(8,128)(2,1)S(1)}, bf16[48,3200]{1,0:T(8,128)(2,1)S(1)}, u32[]{:S(2)}, u32[]{:S(2)}) collective-permute-start(bf16[48,3200]{1,0:T(8,128)(2,1)S(1)} %get-tuple-element.158), channel_id=1, source_target_pairs={{0,24},{1,25},{2,26},{3,27},{4,28},{5,29},{6,30},{7,31},{8,16},{9,... | collective-permute-start | bytes 921608 | tf_op jit(solution)/shard_map/ppermute | solution.py:573
  302.0 12.5 %collective-permute-start.49 = (f32[24,768]{1,0:T(8,128)S(1)}, f32[24,768]{1,0:T(8,128)S(1)}, u32[]{:S(2)}, u32[]{:S(2)}) collective-permute-start(f32[24,768]{1,0:T(8,128)S(1)} %get-tuple-element.244), channel_id=1, source_target_pairs={{0,3},{1,2},{2,1},{3,0},{4,7},{5,6},{6,5},{7,4},{8,11},{9,10},{10,... | collective-permute-start | bytes 221192 | tf_op jit(solution)/shard_map/ppermute | solution.py:573
  (35 other events, 288.7 us)
